TPU v7x, 256 devices: a whole 4x4x8 slice. The times are simulated.
256 devices in a mesh: rep: 32 (over y, z_hi, x), fsdp: 8 (over z_lo, core).
Axes of the slice: x: 4, y: 4, z: 8 (z_hi: 2, z_lo: 4; z = z_hi * 4 + z_lo), core: 2. Of those that a mesh axis runs over, the one named last changes fastest.
Arguments:
- inputs: bfloat16 [2, 32, 2048, 4096], P(None, 'rep', 'fsdp'), may hold values from -6 to 6
- targets: bfloat16 [2, 32, 2048, 512], P(None, 'rep', 'fsdp'), may hold values from -6 to 6
- weights: bfloat16 [32, 4096, 512], P('rep', 'fsdp'), may hold values from -6 to 6
- first_moment: float32 [32, 4096, 512], P('rep', 'fsdp'), may hold values from -0.0078125 to 0.0078125
- second_moment: float32 [32, 4096, 512], P('rep', 'fsdp'), may hold values from 2.5e-08 to 1e-06
- global_weights: float32 [4096, 512], P('fsdp'), may hold values from -6 to 6
- outer_moment: float32 [4096, 512], P('fsdp'), may hold values from -4 to 4
- drift: float32 [32, 4096, 512], P('rep', 'fsdp'), may hold values from -6 to 6
Outputs:
- weights_out: bfloat16 [32, 4096, 512], P('rep', 'fsdp')
- global_out: float32 [4096, 512], P('fsdp')
All inputs are finite; a program needn't handle non-finite values.
Results may differ from a plain program's by a relative error of at most 0.0065.
Values may be sent and summed in bfloat16 or wider, within the bound.
No kernel may reach another device: no remote copies, remote signals or barrier semaphores. Data moves between devices by JAX's collectives and lax.ppermute only.
A program may use at most 128 MiB of HBM per device.

v0:
```python
import jax
import jax.numpy as jnp
from jax import lax
from jax.sharding import PartitionSpec as P

STEPS = 2


inner_rate = 0.2
beta_first = 0.9
beta_second = 0.95
adam_eps = 1e-08
decay_rate = 0.1
mix_share = 0.5
outer_rate = 0.7
outer_beta = 0.9


def contract_rows(left, right):
    return lax.dot_general(
        left, right, (((0,), (0,)), ((), ())), preferred_element_type=jnp.float32
    )


def outer_update(global_weights, outer_moment, drift):
    replicas = lax.axis_size("rep")
    mean_drift = lax.psum(drift[0].astype(jnp.bfloat16), "rep").astype(jnp.float32) / replicas
    new_moment = outer_beta * outer_moment + mean_drift
    return global_weights - outer_rate * (mean_drift + outer_beta * new_moment)


def per_device(
    inputs, targets, weights, first_moment, second_moment, global_weights, outer_moment, drift
):
    feats_all = inputs[:, 0]
    tok_rows = feats_all.shape[1]
    width = feats_all.shape[2]
    tokens_total = tok_rows * lax.axis_size("fsdp")
    scale = width ** (-0.5)
    current = weights[0]
    moment_one = first_moment[0]
    moment_two = second_moment[0]
    global_out = outer_update(global_weights, outer_moment, drift)
    for step in range(STEPS):
        target_rows = targets[step, 0].astype(jnp.float32)
        feats = feats_all[step]
        keys = (
            jnp.dot(
                feats,
                lax.all_gather(current, "fsdp", axis=0, tiled=True),
                preferred_element_type=jnp.float32,
            )
            * scale
        )
        residual = (keys - target_rows).astype(jnp.bfloat16)
        grad = lax.psum_scatter(
            contract_rows(feats, residual), "fsdp", scatter_dimension=0, tiled=True
        ) * (scale / tokens_total)
        moment_one = beta_first * moment_one + (1.0 - beta_first) * grad
        moment_two = beta_second * moment_two + (1.0 - beta_second) * grad * grad
        wide = current.astype(jnp.float32)
        updated = wide - inner_rate * (
            moment_one / (jnp.sqrt(moment_two) + adam_eps) + decay_rate * wide
        )
        if step == 0:
            updated = mix_share * updated + (1.0 - mix_share) * global_out
        current = updated.astype(jnp.bfloat16)
    return (current[None], global_out)


def solution(mesh):
    in_specs = (
        P(None, "rep", "fsdp", None),
        P(None, "rep", "fsdp", None),
        P("rep", "fsdp", None),
        P("rep", "fsdp", None),
        P("rep", "fsdp", None),
        P("fsdp", None),
        P("fsdp", None),
        P("rep", "fsdp", None),
    )
    out_specs = (P("rep", "fsdp", None), P("fsdp", None))
    return jax.shard_map(
        per_device, mesh=mesh, in_specs=in_specs, out_specs=out_specs, check_vma=False
    )
```

profile of v0, /device:TPU:34, one launch (start us, length us, event | category | flops | bytes accessed | tf_op | source)
XLA Modules:
  0.0 672.5 jit_solution(4993911200659760415)
XLA Ops:
  8.0 0.0 all-gather.6.cloned.1.call-start
  8.0 0.7 all-gather.6.cloned.1.call-update
  8.7 0.0 all-reduce.2.cloned.1.call-start
  8.8 2.2 copy.13
  11.0 0.0 all-reduce.2.cloned.1.call-update
  11.0 0.0 reduce-scatter.3.cloned.1.call-start
  11.1 53.1 %all-gather.6.cloned.1.call-done = bf16[1,4096,512]{2,1,0:T(8,128)(2,1)} async-done(((bf16[1,512,512]{2,1,0:T(8,128)(2,1)}), bf16[1,4096,512]{2,1,0:T(8,128)(2,1)}) %all-gather.6.cloned.1.call-update) | async-done | bytes 4194320 | tf_op jit(solution)/shard_map/all_gather | solution.py:50
  64.2 9.3 %convolution_bitcast_fusion.1 = f32[4096,512]{0,1:T(8,128)} fusion(bf16[2,1,256,4096]{3,2,1,0:T(8,128)(2,1)} %param.8, bf16[1,4096,512]{2,1,0:T(8,128)(2,1)} %all-gather.6.cloned.1.call-done, bf16[2,1,256,512]{3,2,1,0:T(8,128)(2,1)} %param.9), kind=kOutput, calls=%fused_computation.1 | convolution fusion | flops 2148007936 | bytes 17039360 | tf_op jit(solution)/shard_map/dot_general | solution.py:20
  73.5 0.0 copy-start.1
  73.5 0.0 copy-start.2
  73.5 0.0 copy-start.3
  73.5 0.0 reduce-scatter.3.cloned.1.call-update
  73.5 0.0 all-gather.4.cloned.1.call-start
  73.5 1.0 copy-done.1
  74.5 1.0 copy.10
  75.5 0.0 copy-done.2
  75.5 0.3 copy.11
  75.9 0.0 copy-done.3
  75.9 0.3 copy.12
  76.2 1.6 copy.14
  77.8 2.5 copy.15
  80.3 421.4 %all-reduce.2.cloned.1.call-done = bf16[512,512]{0,1:T(8,128)(2,1)} async-done(((bf16[512,512]{0,1:T(8,128)(2,1)}), bf16[512,512]{0,1:T(8,128)(2,1)}) %all-reduce.2.cloned.1.call-update) | async-done | bytes 524304 | tf_op jit(solution)/shard_map/psum | solution.py:27
  501.7 0.0 reduce-scatter.3.cloned.1.call-done
  501.7 4.1 fusion.51
  505.8 0.0 all-gather.4.cloned.1.call-update
  505.8 0.0 reduce-scatter.5.cloned.1.call-start
  505.9 52.3 %all-gather.4.cloned.1.call-done = bf16[4096,512]{0,1:T(8,128)(2,1)} async-done(((bf16[512,512]{0,1:T(8,128)(2,1)}), bf16[4096,512]{0,1:T(8,128)(2,1)}) %all-gather.4.cloned.1.call-update) | async-done | bytes 4194320 | tf_op jit(solution)/shard_map/all_gather | solution.py:50
  558.1 9.3 %convolution_bitcast_fusion = f32[4096,512]{0,1:T(8,128)} fusion(bf16[2,1,256,4096]{3,2,1,0:T(8,128)(2,1)} %param.8, bf16[4096,512]{0,1:T(8,128)(2,1)} %all-gather.4.cloned.1.call-done, bf16[2,1,256,512]{3,2,1,0:T(8,128)(2,1)} %param.9), kind=kOutput, calls=%fused_computation | convolution fusion | flops 2148007936 | bytes 17039360 | tf_op jit(solution)/shard_map/dot_general | solution.py:20
  567.4 0.0 copy-start
  567.4 0.0 reduce-scatter.5.cloned.1.call-update
  567.5 2.6 copy.17
  570.0 91.7 %reduce-scatter.5.cloned.1.call-done = f32[512,512]{0,1:T(8,128)} async-done(((f32[4096,512]{0,1:T(8,128)}), f32[512,512]{0,1:T(8,128)}) %reduce-scatter.5.cloned.1.call-update) | async-done | bytes 1048592 | tf_op jit(solution)/shard_map/reduce_scatter | solution.py:56
  661.8 0.0 copy-done
  661.8 2.6 fusion.54
  664.4 1.0 copy.16
Async XLA Ops:
  8.0 56.2 %all-gather.6.cloned.1.call-start = ((), (), s32[]{:S(2)}) async-start(), calls=%async_computation.6 | async-start | bytes 4718592 | tf_op jit(solution)/shard_map/all_gather | solution.py:50
  8.7 492.9 %all-reduce.2.cloned.1.call-start = ((), (), s32[]{:S(2)}) async-start(), calls=%async_computation.3 | async-start | bytes 1048576 | tf_op jit(solution)/shard_map/psum | solution.py:27
  11.0 490.6 %reduce-scatter.3.cloned.1.call-start = ((), (), s32[]{:S(2)}) async-start(), calls=%async_computation.2 | async-start | bytes 9437184 | tf_op jit(solution)/shard_map/reduce_scatter | solution.py:56
  73.5 1.0 copy-start.1
  73.5 2.0 copy-start.2
  73.5 2.4 copy-start.3
  73.5 484.6 %all-gather.4.cloned.1.call-start = ((), (), s32[]{:S(2)}) async-start(), calls=%async_computation.4 | async-start | bytes 4718592 | tf_op jit(solution)/shard_map/all_gather | solution.py:50
  505.8 156.0 %reduce-scatter.5.cloned.1.call-start = ((), (), s32[]{:S(2)}) async-start(), calls=%async_computation.5 | async-start | bytes 9437184 | tf_op jit(solution)/shard_map/reduce_scatter | solution.py:56
  567.4 94.3 %copy-start = (bf16[512,512]{0,1:T(8,128)(2,1)S(1)}, bf16[512,512]{0,1:T(8,128)(2,1)}, u32[]{:S(2)}) copy-start(bf16[512,512]{0,1:T(8,128)(2,1)} %get-tuple-element.4) | copy-start | bytes 1572868
Sparse Core Ops, SparseCore 0:
  10.6 53.5 all-gather.5
  73.6 96.0 reduce-scatter.2
  505.9 52.1 all-gather.3
  567.6 94.1 reduce-scatter.4
Sparse Core Ops, SparseCore 1:
  11.8 489.8 all-reduce.1
where the time goes:
time: 676 us; the launch traced here: 673 us
  waiting for transfers between devices  619 us (92%)
  matrix products  18.6 us (3%)
  between operations  15.2 us (2%)
  local copies, waits for them, and re-layouts  12.6 us (2%)
    psum x1, waiting for transfers between devices, outer_update(): lax.psum(drift[0].astype(jnp.bfloat16), 'rep').astype(jnp.float32)  421 us
    all_gather x2, waiting for transfers between devices, per_device(): lax.all_gather(current, 'fsdp', axis=0, tiled=True)  105 us
    reduce_scatter x2, waiting for transfers between devices, per_device(): lax.psum_scatter(contract_rows(feats, residual), 'fsdp', scatter_dimensio...  91.7 us
    dot_general x2, matrix products, contract_rows(): lax.dot_general(left, right, (((0,), (0,)), ((), ())), preferred_element_...  18.6 us
  transfers between devices with their start and end apart: 5, of which 4 were waited for; matrix products, arithmetic and copies ran while one was open for 3% of the time, Pallas kernels for 0%

commit v1 on v0

v1 whole, which is shorter than its diff:
```python
import jax
import jax.numpy as jnp
from jax import lax
from jax.sharding import PartitionSpec as P

STEPS = 2
CHUNKS = 2

inner_rate = 0.2
beta_first = 0.9
beta_second = 0.95
adam_eps = 1e-08
decay_rate = 0.1
mix_share = 0.5
outer_rate = 0.7
outer_beta = 0.9

BF = jnp.bfloat16
F32 = jnp.float32


def xor_perm(size, stride, extent, k):
    pairs = []
    for i in range(size):
        at = (i // stride) % extent
        pairs.append((i, i + ((at ^ k) - at) * stride))
    return pairs


def swap(value, axis, stride, extent, k):
    return lax.ppermute(value, axis, xor_perm(lax.axis_size(axis), stride, extent, k))


def core_swap(value):
    return swap(value, "fsdp", 1, 2, 1)


def z_swap(value, k):
    return swap(value, "fsdp", 2, 4, k)


def scatter_sum(value, me, stride, extent):
    rows = value.shape[0] // extent
    total = lax.dynamic_slice_in_dim(value, me * rows, rows).astype(F32)
    for k in range(1, extent):
        piece = lax.dynamic_slice_in_dim(value, (me ^ k) * rows, rows)
        total = total + swap(piece, "rep", stride, extent, k).astype(F32)
    return total


def gather(value, me, stride, extent):
    rows = value.shape[0]
    whole = jnp.zeros((rows * extent,) + value.shape[1:], value.dtype)
    whole = lax.dynamic_update_slice_in_dim(whole, value, me * rows, 0)
    for k in range(1, extent):
        piece = swap(value, "rep", stride, extent, k)
        whole = lax.dynamic_update_slice_in_dim(whole, piece, (me ^ k) * rows, 0)
    return whole


def mean_of_drift(drift):
    at = lax.axis_index("rep")
    replicas = lax.axis_size("rep")
    x, z_hi, y = at % 4, (at // 4) % 2, at // 8
    part = drift.astype(BF)
    part = scatter_sum(part, x, 1, 4).astype(BF)
    part = scatter_sum(part, y, 8, 4).astype(BF)
    part = scatter_sum(part, z_hi, 4, 2)
    part = (part / replicas).astype(BF)
    part = gather(part, z_hi, 4, 2)
    part = gather(part, y, 8, 4)
    return gather(part, x, 1, 4).astype(F32)


def outer_update(global_weights, outer_moment, drift):
    mean_drift = mean_of_drift(drift)
    new_moment = outer_beta * outer_moment + mean_drift
    return global_weights - outer_rate * (mean_drift + outer_beta * new_moment)


def per_device(
    inputs, targets, weights, first_moment, second_moment, global_weights, outer_moment, drift
):
    at = lax.axis_index("fsdp")
    core, z = at % 2, at // 2
    tok_rows, width = inputs.shape[2], inputs.shape[3]
    tokens_total = tok_rows * lax.axis_size("fsdp")
    scale = width ** (-0.5)
    rows, columns = weights.shape[1], weights.shape[2]
    cols = columns // CHUNKS

    def half(feats, parity):
        return jnp.concatenate(
            [
                lax.dynamic_slice_in_dim(feats, (2 * (z ^ j) + parity) * rows, rows, 1)
                for j in range(4)
            ],
            axis=1,
        )

    feats, aims = [], []
    for step in range(STEPS):
        mine = half(inputs[step, 0], core)
        theirs = core_swap(half(inputs[step, 0], 1 - core))
        feats.append(jnp.concatenate([mine, theirs], axis=0))
        aim = targets[step, 0]
        aims.append(jnp.concatenate([aim, core_swap(aim)], axis=0))

    global_out = outer_update(global_weights, outer_moment, drift[0])

    current = [weights[0][:, k * cols : (k + 1) * cols] for k in range(CHUNKS)]
    ones = [first_moment[0][:, k * cols : (k + 1) * cols] for k in range(CHUNKS)]
    twos = [second_moment[0][:, k * cols : (k + 1) * cols] for k in range(CHUNKS)]
    for step in range(STEPS):
        for k in range(CHUNKS):
            own = current[k]
            near = z_swap(own, 1)
            far = z_swap(own, 3)
            rest = z_swap(far, 1)
            whole = jnp.concatenate([own, near, rest, far], axis=0)
            part = jnp.dot(feats[step], whole, preferred_element_type=F32)
            other = core_swap(part)
            other = jnp.concatenate([other[tok_rows:], other[:tok_rows]], axis=0)
            aim = aims[step][:, k * cols : (k + 1) * cols].astype(F32)
            residual = ((part + other) * scale - aim).astype(BF)
            grads = lax.dot_general(
                feats[step], residual, (((0,), (0,)), ((), ())), preferred_element_type=F32
            ).reshape(4, rows, cols)
            passed = z_swap(grads[2].astype(BF), 1)
            from_near = z_swap(grads[1].astype(BF), 1)
            from_far = z_swap((grads[3] + passed.astype(F32)).astype(BF), 3)
            grad = (grads[0] + from_near.astype(F32) + from_far.astype(F32)) * (
                scale / tokens_total
            )
            ones[k] = beta_first * ones[k] + (1.0 - beta_first) * grad
            twos[k] = beta_second * twos[k] + (1.0 - beta_second) * grad * grad
            wide = own.astype(F32)
            updated = wide - inner_rate * (
                ones[k] / (jnp.sqrt(twos[k]) + adam_eps) + decay_rate * wide
            )
            if step == 0:
                outer = global_out[:, k * cols : (k + 1) * cols]
                updated = mix_share * updated + (1.0 - mix_share) * outer
            current[k] = updated.astype(BF)
    return (jnp.concatenate(current, axis=1)[None], global_out)


def solution(mesh):
    in_specs = (
        P(None, "rep", "fsdp", None),
        P(None, "rep", "fsdp", None),
        P("rep", "fsdp", None),
        P("rep", "fsdp", None),
        P("rep", "fsdp", None),
        P("fsdp", None),
        P("fsdp", None),
        P("rep", "fsdp", None),
    )
    out_specs = (P("rep", "fsdp", None), P("fsdp", None))
    return jax.shard_map(
        per_device, mesh=mesh, in_specs=in_specs, out_specs=out_specs, check_vma=False
    )
```

time: 676 us -> 204 us (0.30)
  the two profiles are of different devices: /device:TPU:34 before, /device:TPU:1 now
where the time goes in v1:
time: 204 us
  waiting for transfers between devices  91.3 us (45%)
  starting transfers between devices  80.1 us (39%)
  local copies, waits for them, and re-layouts  11.4 us (6%)
  matrix products  11.3 us (6%)
  other arithmetic  8.35 us (4%)
    ppermute x46, waiting for transfers between devices, swap(): lax.ppermute(value, axis, xor_perm(lax.axis_size(axis), stride, extent, k))  91.3 us
    ppermute x46, starting transfers between devices, swap(): lax.ppermute(value, axis, xor_perm(lax.axis_size(axis), stride, extent, k))  80.1 us
    dot_general x4, matrix products, per_device(): lax.dot_general(feats[step], residual, (((0,), (0,)), ((), ())), preferre...  5.7 us
    dot_general x4, matrix products, per_device(): part = jnp.dot(feats[step], whole, preferred_element_type=F32)  5.58 us
  transfers between devices with their start and end apart: 46, of which 22 were waited for; matrix products, arithmetic and copies ran while one was open for 13% of the time, Pallas kernels for 0%

profile of v1, /device:TPU:1, one launch (start us, length us, event | category | flops | bytes accessed | tf_op | source)
XLA Modules:
  0.0 203.6 jit_solution(11239657767137637781)
XLA Ops:
  0.6 1.8 fusion.117
  2.5 5.2 %collective-permute-start.33 = (bf16[512,256]{1,0:T(8,128)(2,1)}, bf16[512,256]{1,0:T(8,128)(2,1)}, u32[]{:S(2)}, u32[]{:S(2)}) collective-permute-start(bf16[512,256]{1,0:T(8,128)(2,1)} %get-tuple-element.39), channel_id=1, source_target_pairs={{0,6},{1,7},{2,4},{3,5},{4,2},{5,3},{6,0},{7,1},{8,14},{9,15},{10,... | collective-permute-start | bytes 786440 | tf_op jit(solution)/shard_map/ppermute | solution.py:31
  7.6 1.3 convert_element_type.160
  9.0 2.8 %collective-permute-start.10 = (bf16[128,512]{1,0:T(8,128)(2,1)S(1)}, bf16[128,512]{1,0:T(8,128)(2,1)S(1)}, u32[]{:S(2)}, u32[]{:S(2)}) collective-permute-start(bf16[128,512]{1,0:T(8,128)(2,1)S(1)} %get-tuple-element.48), channel_id=1, source_target_pairs={{0,16},{8,24},{16,0},{24,8},{32,48},{40,56},{48,32},{56,40},{64,80... | collective-permute-start | bytes 393224 | tf_op jit(solution)/shard_map/ppermute | solution.py:31
  11.8 0.9 collective-permute-start.11
  12.7 3.9 %fusion.110 = (bf16[1,1,256,4096]{3,2,1,0:T(8,128)(2,1)S(1)}, bf16[1,1,256,4096]{3,2,1,0:T(8,128)(2,1)}) fusion(bf16[2,1,256,4096]{3,2,1,0:T(8,128)(2,1)} %param.8), kind=kLoop, calls=%fused_computation.181 | loop fusion | bytes 8388608 | tf_op jit(solution)/shard_map/slice | solution.py:103
  16.6 2.6 %dynamic-slice_bitcast_fusion.15 = (bf16[256,512]{1,0:T(8,128)(2,1)}, bf16[256,512]{1,0:T(8,128)(2,1)S(1)}, bf16[256,512]{1,0:T(8,128)(2,1)S(1)}, bf16[256,512]{...) fusion(bf16[1,1,256,4096]{3,2,1,0:T(8,128)(2,1)} %get-tuple-ele, ...), kind=kLoop, calls=%fused_computation.145 | loop fusion | bytes 4194336 | tf_op jit(solution)/shard_map/dynamic_slice | solution.py:95
  19.2 1.1 pad_maximum_fusion.2
  21.0 1.3 collective-permute-start.12
  22.3 2.6 %collective-permute-start.13 = (bf16[32,512]{1,0:T(8,128)(2,1)}, bf16[32,512]{1,0:T(8,128)(2,1)}, u32[]{:S(2)}, u32[]{:S(2)}) collective-permute-start(bf16[32,512]{1,0:T(8,128)(2,1)} %get-tuple-element.51), channel_id=1, source_target_pairs={{0,128},{8,136},{16,144},{24,152},{32,160},{40,168},{48,176},{56,1... | collective-permute-start | bytes 98312 | tf_op jit(solution)/shard_map/ppermute | solution.py:31
  24.9 1.3 dynamic-slice_bitcast_fusion.7
  26.8 2.3 %collective-permute-start = (bf16[256,2048]{1,0:T(8,128)(2,1)S(1)}, bf16[256,2048]{1,0:T(8,128)(2,1)}, u32[]{:S(2)}, u32[]{:S(2)}) collective-permute-start(bf16[256,2048]{1,0:T(8,128)(2,1)S(1)} %copy-done.6), channel_id=1, source_target_pairs={{0,1},{1,0},{2,3},{3,2},{4,5},{5,4},{6,7},{7,6},{8,9},{9,8},{10,11... | collective-permute-start | bytes 3145736 | tf_op jit(solution)/shard_map/ppermute | solution.py:31
  30.3 5.6 %collective-permute-start.15 = (bf16[16,512]{1,0:T(8,128)(2,1)S(1)}, bf16[16,512]{1,0:T(8,128)(2,1)S(1)}, u32[]{:S(2)}, u32[]{:S(2)}) collective-permute-start(bf16[16,512]{1,0:T(8,128)(2,1)S(1)} %constant_dynamic-slice_fusion), channel_id=1, source_target_pairs={{0,32},{8,40},{16,48},{24,56},{32,0},{40,8},{48,16},{56,24},{64,96... | collective-permute-start | bytes 49160 | tf_op jit(solution)/shard_map/ppermute | solution.py:31
  36.0 1.3 pad_maximum_fusion.3
  37.3 3.8 %collective-permute-done.15 = bf16[16,512]{1,0:T(8,128)(2,1)S(1)} collective-permute-done((bf16[16,512]{1,0:T(8,128)(2,1)S(1)}, bf16[16,512]{1,0:T(8,128)(2,1)S(1)}, u32[]{:S(2)}, u32[]{:S(2)}) %collective-permute-start.15) | collective-permute-done | bytes 16416 | tf_op jit(solution)/shard_map/ppermute | solution.py:31
  41.1 1.6 collective-permute-start.16
  42.8 5.1 %collective-permute-done.16 = bf16[16,512]{1,0:T(8,128)(2,1)S(1)} collective-permute-done((bf16[16,512]{1,0:T(8,128)(2,1)S(1)}, bf16[16,512]{1,0:T(8,128)(2,1)S(1)}, u32[]{:S(2)}, u32[]{:S(2)}) %collective-permute-start.16) | collective-permute-done | bytes 16416 | tf_op jit(solution)/shard_map/ppermute | solution.py:31
  48.0 2.6 %collective-permute-done.17 = bf16[32,512]{1,0:T(8,128)(2,1)S(1)} collective-permute-done((bf16[32,512]{1,0:T(8,128)(2,1)S(1)}, bf16[32,512]{1,0:T(8,128)(2,1)S(1)}, u32[]{:S(2)}, u32[]{:S(2)}) %collective-permute-start.17) | collective-permute-done | bytes 32800 | tf_op jit(solution)/shard_map/ppermute | solution.py:31
  50.6 3.5 %collective-permute-start.18 = (bf16[32,512]{1,0:T(8,128)(2,1)S(1)}, bf16[32,512]{1,0:T(8,128)(2,1)S(1)}, u32[]{:S(2)}, u32[]{:S(2)}) collective-permute-start(bf16[32,512]{1,0:T(8,128)(2,1)S(1)} %constant_dynamic-update-slice_fusion.8), channel_id=1, source_target_pairs={{0,128},{8,136},{16,144},{24,152},{32,160},{40,168},{48,176},{56,1... | collective-permute-start | bytes 98312 | tf_op jit(solution)/shard_map/ppermute | solution.py:31
  54.1 1.3 collective-permute-done.18
  55.4 3.2 %collective-permute-start.19 = (bf16[32,512]{1,0:T(8,128)(2,1)S(1)}, bf16[32,512]{1,0:T(8,128)(2,1)S(1)}, u32[]{:S(2)}, u32[]{:S(2)}) collective-permute-start(bf16[32,512]{1,0:T(8,128)(2,1)S(1)} %constant_dynamic-update-slice_fusion.8), channel_id=1, source_target_pairs={{0,192},{8,200},{16,208},{24,216},{32,224},{40,232},{48,240},{56,2... | collective-permute-start | bytes 98312 | tf_op jit(solution)/shard_map/ppermute | solution.py:31
  58.7 2.2 %collective-permute-start.34 = (bf16[512,256]{1,0:T(8,128)(2,1)}, bf16[512,256]{1,0:T(8,128)(2,1)S(1)}, u32[]{:S(2)}, u32[]{:S(2)}) collective-permute-start(bf16[512,256]{1,0:T(8,128)(2,1)} %collective-permute-done.33), channel_id=1, source_target_pairs={{0,2},{1,3},{2,0},{3,1},{4,6},{5,7},{6,4},{7,5},{8,10},{9,11},{10,... | collective-permute-start | bytes 786440 | tf_op jit(solution)/shard_map/ppermute | solution.py:31
  60.9 1.3 collective-permute-start.1
  62.2 5.5 %collective-permute-start.23 = (bf16[256,2048]{1,0:T(8,128)(2,1)S(1)}, bf16[256,2048]{1,0:T(8,128)(2,1)S(1)}, u32[]{:S(2)}, u32[]{:S(2)}) collective-permute-start(bf16[256,2048]{1,0:T(8,128)(2,1)S(1)} %pad_maximum_fusion.3), channel_id=1, source_target_pairs={{0,1},{1,0},{2,3},{3,2},{4,5},{5,4},{6,7},{7,6},{8,9},{9,8},{10,11... | collective-permute-start | bytes 3145736 | tf_op jit(solution)/shard_map/ppermute | solution.py:31
  67.8 1.7 collective-permute-start.20
  69.5 1.6 collective-permute-start.21
  71.2 2.2 %fusion.19 = f32[512,256]{1,0:T(8,128)S(1)} fusion(bf16[512,256]{1,0:T(8,128)(2,1)} %collective-permute-done.33, bf16[512,256]{1,0:T(8,128)(2,1)S(1)} %collective-permute-done.34, bf16[512,256]{1,0:T(8,128)(2,1)} %collective-permute-done.32, bf16[512,256]{1,0:T(8,128)(2,1)} %get-tuple-element.39, bf16[256,2048]{1,0:T(8,128)(2,1)} %collective-permute-done, ...), kind=kOutput, calls=%fused_computation.25 | convolution fusion | flops 551550976 | bytes 3670016 | tf_op jit(solution)/shard_map/dot_general | solution.py:121
  73.4 5.4 %collective-permute-start.35 = (f32[512,256]{1,0:T(8,128)S(1)}, f32[512,256]{1,0:T(8,128)S(1)}, u32[]{:S(2)}, u32[]{:S(2)}) collective-permute-start(f32[512,256]{1,0:T(8,128)S(1)} %fusion.19), channel_id=1, source_target_pairs={{0,1},{1,0},{2,3},{3,2},{4,5},{5,4},{6,7},{7,6},{8,9},{9,8},{10,11... | collective-permute-start | bytes 1572872 | tf_op jit(solution)/shard_map/ppermute | solution.py:31
  79.0 0.9 collective-permute-start.22
  79.9 2.0 fusion.3
  81.9 1.5 collective-permute-start.4
  83.4 2.0 fusion.121
  85.5 1.6 collective-permute-start.37
  87.1 2.0 %fusion.120 = (bf16[2048,256]{1,0:T(8,128)(2,1)S(1)}, f32[2048,256]{1,0:T(8,128)S(1)}) fusion(f32[512,256]{1,0:T(8,128)S(1)} %fusion.3, f32[256,256]{1,0:T(8,128)S(1)} %get-tuple-element.37, f32[256,256]{1,0:T(8,128)S(1)} %get-tuple-element.36, bf16[256,512]{1,0:T(8,128)(2,1)S(1)} %get-tuple-element.41, bf16[256,512]{1,0:T(8,128)(2,1)S(1)} %collective-permute-done.5, ...), kind=kOutput, calls=%fused_computation.191 | convolution fusion | flops 549060608 | bytes 6815744 | tf_op jit(solution)/shard_map/dot_general | solution.py:126
  89.4 1.5 collective-permute-start.36
  91.0 2.6 %collective-permute-done.37 = bf16[512,256]{1,0:T(8,128)(2,1)S(1)} collective-permute-done((bf16[512,256]{1,0:T(8,128)(2,1)S(1)}, bf16[512,256]{1,0:T(8,128)(2,1)S(1)}, u32[]{:S(2)}, u32[]{:S(2)}) %collective-permute-start.37) | collective-permute-done | bytes 262176 | tf_op jit(solution)/shard_map/ppermute | solution.py:31
  93.6 1.3 collective-permute-start.38
  94.9 4.3 %collective-permute-done.7 = bf16[512,256]{1,0:T(8,128)(2,1)S(1)} collective-permute-done((bf16[512,256]{1,0:T(8,128)(2,1)S(1)}, bf16[512,256]{1,0:T(8,128)(2,1)S(1)}, u32[]{:S(2)}, u32[]{:S(2)}) %collective-permute-start.7) | collective-permute-done | bytes 262176 | tf_op jit(solution)/shard_map/ppermute | solution.py:31
  99.3 1.3 collective-permute-start.8
  100.9 3.9 %collective-permute-done.36 = bf16[512,256]{1,0:T(8,128)(2,1)S(1)} collective-permute-done((bf16[512,256]{1,0:T(8,128)(2,1)S(1)}, bf16[512,256]{1,0:T(8,128)(2,1)S(1)}, u32[]{:S(2)}, u32[]{:S(2)}) %collective-permute-start.36) | collective-permute-done | bytes 262176 | tf_op jit(solution)/shard_map/ppermute | solution.py:31
  104.8 5.6 %collective-permute-done.6 = bf16[512,256]{1,0:T(8,128)(2,1)S(1)} collective-permute-done((bf16[512,256]{1,0:T(8,128)(2,1)S(1)}, bf16[512,256]{1,0:T(8,128)(2,1)S(1)}, u32[]{:S(2)}, u32[]{:S(2)}) %collective-permute-start.6) | collective-permute-done | bytes 262176 | tf_op jit(solution)/shard_map/ppermute | solution.py:31
  110.4 6.8 %collective-permute-done.38 = bf16[512,256]{1,0:T(8,128)(2,1)S(1)} collective-permute-done((bf16[512,256]{1,0:T(8,128)(2,1)S(1)}, bf16[512,256]{1,0:T(8,128)(2,1)S(1)}, u32[]{:S(2)}, u32[]{:S(2)}) %collective-permute-start.38) | collective-permute-done | bytes 262176 | tf_op jit(solution)/shard_map/ppermute | solution.py:31
  117.2 5.6 %collective-permute-done.8 = bf16[512,256]{1,0:T(8,128)(2,1)S(1)} collective-permute-done((bf16[512,256]{1,0:T(8,128)(2,1)S(1)}, bf16[512,256]{1,0:T(8,128)(2,1)S(1)}, u32[]{:S(2)}, u32[]{:S(2)}) %collective-permute-start.8) | collective-permute-done | bytes 262176 | tf_op jit(solution)/shard_map/ppermute | solution.py:31
  122.9 1.0 fusion.39
  124.0 2.1 %collective-permute-start.40 = (bf16[512,256]{1,0:T(8,128)(2,1)S(1)}, bf16[512,256]{1,0:T(8,128)(2,1)S(1)}, u32[]{:S(2)}, u32[]{:S(2)}) collective-permute-start(bf16[512,256]{1,0:T(8,128)(2,1)S(1)} %get-tuple-element.7), channel_id=1, source_target_pairs={{0,6},{1,7},{2,4},{3,5},{4,2},{5,3},{6,0},{7,1},{8,14},{9,15},{10,... | collective-permute-start | bytes 786440 | tf_op jit(solution)/shard_map/ppermute | solution.py:31
  126.1 1.2 collective-permute-start.25
  127.3 5.6 %collective-permute-done.40 = bf16[512,256]{1,0:T(8,128)(2,1)S(1)} collective-permute-done((bf16[512,256]{1,0:T(8,128)(2,1)S(1)}, bf16[512,256]{1,0:T(8,128)(2,1)S(1)}, u32[]{:S(2)}, u32[]{:S(2)}) %collective-permute-start.40) | collective-permute-done | bytes 262176 | tf_op jit(solution)/shard_map/ppermute | solution.py:31
  132.9 6.1 %collective-permute-start.41 = (bf16[512,256]{1,0:T(8,128)(2,1)S(1)}, bf16[512,256]{1,0:T(8,128)(2,1)S(1)}, u32[]{:S(2)}, u32[]{:S(2)}) collective-permute-start(bf16[512,256]{1,0:T(8,128)(2,1)S(1)} %collective-permute-done.40), channel_id=1, source_target_pairs={{0,2},{1,3},{2,0},{3,1},{4,6},{5,7},{6,4},{7,5},{8,10},{9,11},{10,... | collective-permute-start | bytes 786440 | tf_op jit(solution)/shard_map/ppermute | solution.py:31
  139.1 6.8 %collective-permute-start.26 = (bf16[512,256]{1,0:T(8,128)(2,1)S(1)}, bf16[512,256]{1,0:T(8,128)(2,1)S(1)}, u32[]{:S(2)}, u32[]{:S(2)}) collective-permute-start(bf16[512,256]{1,0:T(8,128)(2,1)S(1)} %collective-permute-done.25), channel_id=1, source_target_pairs={{0,2},{1,3},{2,0},{3,1},{4,6},{5,7},{6,4},{7,5},{8,10},{9,11},{10,... | collective-permute-start | bytes 786440 | tf_op jit(solution)/shard_map/ppermute | solution.py:31
  145.9 5.1 %collective-permute-done.41 = bf16[512,256]{1,0:T(8,128)(2,1)S(1)} collective-permute-done((bf16[512,256]{1,0:T(8,128)(2,1)S(1)}, bf16[512,256]{1,0:T(8,128)(2,1)S(1)}, u32[]{:S(2)}, u32[]{:S(2)}) %collective-permute-start.41) | collective-permute-done | bytes 262176 | tf_op jit(solution)/shard_map/ppermute | solution.py:31
  152.5 4.1 %collective-permute-done.24 = bf16[512,256]{1,0:T(8,128)(2,1)S(1)} collective-permute-done((bf16[512,256]{1,0:T(8,128)(2,1)S(1)}, bf16[512,256]{1,0:T(8,128)(2,1)S(1)}, u32[]{:S(2)}, u32[]{:S(2)}) %collective-permute-start.24) | collective-permute-done | bytes 262176 | tf_op jit(solution)/shard_map/ppermute | solution.py:31
  156.7 5.6 %collective-permute-done.26 = bf16[512,256]{1,0:T(8,128)(2,1)S(1)} collective-permute-done((bf16[512,256]{1,0:T(8,128)(2,1)S(1)}, bf16[512,256]{1,0:T(8,128)(2,1)S(1)}, u32[]{:S(2)}, u32[]{:S(2)}) %collective-permute-start.26) | collective-permute-done | bytes 262176 | tf_op jit(solution)/shard_map/ppermute | solution.py:31
  166.0 1.0 collective-permute-start.30
  167.6 0.9 collective-permute-start.29
  168.5 4.0 %collective-permute-done.44 = bf16[512,256]{1,0:T(8,128)(2,1)S(1)} collective-permute-done((bf16[512,256]{1,0:T(8,128)(2,1)S(1)}, bf16[512,256]{1,0:T(8,128)(2,1)S(1)}, u32[]{:S(2)}, u32[]{:S(2)}) %collective-permute-start.44) | collective-permute-done | bytes 262176 | tf_op jit(solution)/shard_map/ppermute | solution.py:31
  172.5 2.1 %collective-permute-start.45 = (bf16[512,256]{1,0:T(8,128)(2,1)S(1)}, bf16[512,256]{1,0:T(8,128)(2,1)S(1)}, u32[]{:S(2)}, u32[]{:S(2)}) collective-permute-start(bf16[512,256]{1,0:T(8,128)(2,1)S(1)} %fusion.51), channel_id=1, source_target_pairs={{0,6},{1,7},{2,4},{3,5},{4,2},{5,3},{6,0},{7,1},{8,14},{9,15},{10,... | collective-permute-start | bytes 786440 | tf_op jit(solution)/shard_map/ppermute | solution.py:31
  174.7 3.4 %collective-permute-done.30 = bf16[512,256]{1,0:T(8,128)(2,1)S(1)} collective-permute-done((bf16[512,256]{1,0:T(8,128)(2,1)S(1)}, bf16[512,256]{1,0:T(8,128)(2,1)S(1)}, u32[]{:S(2)}, u32[]{:S(2)}) %collective-permute-start.30) | collective-permute-done | bytes 262176 | tf_op jit(solution)/shard_map/ppermute | solution.py:31
  178.2 2.1 %collective-permute-start.31 = (bf16[512,256]{1,0:T(8,128)(2,1)S(1)}, bf16[512,256]{1,0:T(8,128)(2,1)S(1)}, u32[]{:S(2)}, u32[]{:S(2)}) collective-permute-start(bf16[512,256]{1,0:T(8,128)(2,1)S(1)} %fusion.57), channel_id=1, source_target_pairs={{0,6},{1,7},{2,4},{3,5},{4,2},{5,3},{6,0},{7,1},{8,14},{9,15},{10,... | collective-permute-start | bytes 786440 | tf_op jit(solution)/shard_map/ppermute | solution.py:31
  180.3 3.4 %collective-permute-done.43 = bf16[512,256]{1,0:T(8,128)(2,1)S(1)} collective-permute-done((bf16[512,256]{1,0:T(8,128)(2,1)S(1)}, bf16[512,256]{1,0:T(8,128)(2,1)S(1)}, u32[]{:S(2)}, u32[]{:S(2)}) %collective-permute-start.43) | collective-permute-done | bytes 262176 | tf_op jit(solution)/shard_map/ppermute | solution.py:31
  183.7 5.6 %collective-permute-done.29 = bf16[512,256]{1,0:T(8,128)(2,1)S(1)} collective-permute-done((bf16[512,256]{1,0:T(8,128)(2,1)S(1)}, bf16[512,256]{1,0:T(8,128)(2,1)S(1)}, u32[]{:S(2)}, u32[]{:S(2)}) %collective-permute-start.29) | collective-permute-done | bytes 262176 | tf_op jit(solution)/shard_map/ppermute | solution.py:31
  189.3 6.4 %collective-permute-done.45 = bf16[512,256]{1,0:T(8,128)(2,1)S(1)} collective-permute-done((bf16[512,256]{1,0:T(8,128)(2,1)S(1)}, bf16[512,256]{1,0:T(8,128)(2,1)S(1)}, u32[]{:S(2)}, u32[]{:S(2)}) %collective-permute-start.45) | collective-permute-done | bytes 262176 | tf_op jit(solution)/shard_map/ppermute | solution.py:31
  195.7 5.6 %collective-permute-done.31 = bf16[512,256]{1,0:T(8,128)(2,1)S(1)} collective-permute-done((bf16[512,256]{1,0:T(8,128)(2,1)S(1)}, bf16[512,256]{1,0:T(8,128)(2,1)S(1)}, u32[]{:S(2)}, u32[]{:S(2)}) %collective-permute-start.31) | collective-permute-done | bytes 262176 | tf_op jit(solution)/shard_map/ppermute | solution.py:31
  201.3 1.4 fusion.42
  202.7 0.8 maximum_bitcast_fusion
  (116 shorter events, 9.8 us)
Async XLA Ops:
  2.5 56.2 %collective-permute-start.33 = (bf16[512,256]{1,0:T(8,128)(2,1)}, bf16[512,256]{1,0:T(8,128)(2,1)}, u32[]{:S(2)}, u32[]{:S(2)}) collective-permute-start(bf16[512,256]{1,0:T(8,128)(2,1)} %get-tuple-element.39), channel_id=1, source_target_pairs={{0,6},{1,7},{2,4},{3,5},{4,2},{5,3},{6,0},{7,1},{8,14},{9,15},{10,... | collective-permute-start | bytes 786440 | tf_op jit(solution)/shard_map/ppermute | solution.py:31
  7.6 54.6 %collective-permute-start.32 = (bf16[512,256]{1,0:T(8,128)(2,1)}, bf16[512,256]{1,0:T(8,128)(2,1)}, u32[]{:S(2)}, u32[]{:S(2)}) collective-permute-start(bf16[512,256]{1,0:T(8,128)(2,1)} %get-tuple-element.39), channel_id=1, source_target_pairs={{0,2},{1,3},{2,0},{3,1},{4,6},{5,7},{6,4},{7,5},{8,10},{9,11},{10,... | collective-permute-start | bytes 786440 | tf_op jit(solution)/shard_map/ppermute | solution.py:31
  9.0 11.3 %collective-permute-start.10 = (bf16[128,512]{1,0:T(8,128)(2,1)S(1)}, bf16[128,512]{1,0:T(8,128)(2,1)S(1)}, u32[]{:S(2)}, u32[]{:S(2)}) collective-permute-start(bf16[128,512]{1,0:T(8,128)(2,1)S(1)} %get-tuple-element.48), channel_id=1, source_target_pairs={{0,16},{8,24},{16,0},{24,8},{32,48},{40,56},{48,32},{56,40},{64,80... | collective-permute-start | bytes 393224 | tf_op jit(solution)/shard_map/ppermute | solution.py:31
  11.8 8.4 %collective-permute-start.11 = (bf16[128,512]{1,0:T(8,128)(2,1)S(1)}, bf16[128,512]{1,0:T(8,128)(2,1)S(1)}, u32[]{:S(2)}, u32[]{:S(2)}) collective-permute-start(bf16[128,512]{1,0:T(8,128)(2,1)S(1)} %get-tuple-element.47), channel_id=1, source_target_pairs={{0,24},{8,16},{16,8},{24,0},{32,56},{40,48},{48,40},{56,32},{64,88... | collective-permute-start | bytes 393224 | tf_op jit(solution)/shard_map/ppermute | solution.py:31
  12.7 7.6 %collective-permute-start.9 = (bf16[128,512]{1,0:T(8,128)(2,1)S(1)}, bf16[128,512]{1,0:T(8,128)(2,1)S(1)}, u32[]{:S(2)}, u32[]{:S(2)}) collective-permute-start(bf16[128,512]{1,0:T(8,128)(2,1)S(1)} %get-tuple-element.46), channel_id=1, source_target_pairs={{0,8},{8,0},{16,24},{24,16},{32,40},{40,32},{48,56},{56,48},{64,72... | collective-permute-start | bytes 393224 | tf_op jit(solution)/shard_map/ppermute | solution.py:31
  21.0 5.2 %collective-permute-start.12 = (bf16[32,512]{1,0:T(8,128)(2,1)}, bf16[32,512]{1,0:T(8,128)(2,1)}, u32[]{:S(2)}, u32[]{:S(2)}) collective-permute-start(bf16[32,512]{1,0:T(8,128)(2,1)} %get-tuple-element.49), channel_id=1, source_target_pairs={{0,64},{8,72},{16,80},{24,88},{32,96},{40,104},{48,112},{56,120},{... | collective-permute-start | bytes 98312 | tf_op jit(solution)/shard_map/ppermute | solution.py:31
  22.3 6.8 %collective-permute-start.13 = (bf16[32,512]{1,0:T(8,128)(2,1)}, bf16[32,512]{1,0:T(8,128)(2,1)}, u32[]{:S(2)}, u32[]{:S(2)}) collective-permute-start(bf16[32,512]{1,0:T(8,128)(2,1)} %get-tuple-element.51), channel_id=1, source_target_pairs={{0,128},{8,136},{16,144},{24,152},{32,160},{40,168},{48,176},{56,1... | collective-permute-start | bytes 98312 | tf_op jit(solution)/shard_map/ppermute | solution.py:31
  24.9 4.6 %collective-permute-start.14 = (bf16[32,512]{1,0:T(8,128)(2,1)}, bf16[32,512]{1,0:T(8,128)(2,1)}, u32[]{:S(2)}, u32[]{:S(2)}) collective-permute-start(bf16[32,512]{1,0:T(8,128)(2,1)} %get-tuple-element.50), channel_id=1, source_target_pairs={{0,192},{8,200},{16,208},{24,216},{32,224},{40,232},{48,240},{56,2... | collective-permute-start | bytes 98312 | tf_op jit(solution)/shard_map/ppermute | solution.py:31
  26.2 16.5 %copy-start.7 = (bf16[2,1,256,512]{3,2,1,0:T(8,128)(2,1)S(1)}, bf16[2,1,256,512]{3,2,1,0:T(8,128)(2,1)}, u32[]{:S(2)}) copy-start(bf16[2,1,256,512]{3,2,1,0:T(8,128)(2,1)} %param.9) | copy-start | bytes 1572868
  26.8 44.3 %collective-permute-start = (bf16[256,2048]{1,0:T(8,128)(2,1)S(1)}, bf16[256,2048]{1,0:T(8,128)(2,1)}, u32[]{:S(2)}, u32[]{:S(2)}) collective-permute-start(bf16[256,2048]{1,0:T(8,128)(2,1)S(1)} %copy-done.6), channel_id=1, source_target_pairs={{0,1},{1,0},{2,3},{3,2},{4,5},{5,4},{6,7},{7,6},{8,9},{9,8},{10,11... | collective-permute-start | bytes 3145736 | tf_op jit(solution)/shard_map/ppermute | solution.py:31
  29.1 38.6 %collective-permute-start.2 = (bf16[512,256]{1,0:T(8,128)(2,1)}, bf16[512,256]{1,0:T(8,128)(2,1)}, u32[]{:S(2)}, u32[]{:S(2)}) collective-permute-start(bf16[512,256]{1,0:T(8,128)(2,1)} %get-tuple-element.38), channel_id=1, source_target_pairs={{0,6},{1,7},{2,4},{3,5},{4,2},{5,3},{6,0},{7,1},{8,14},{9,15},{10,... | collective-permute-start | bytes 786440 | tf_op jit(solution)/shard_map/ppermute | solution.py:31
  30.3 5.7 %copy-start.17 = (bf16[32,512]{1,0:T(8,128)(2,1)}, bf16[32,512]{1,0:T(8,128)(2,1)S(1)}, u32[]{:S(2)}) copy-start(bf16[32,512]{1,0:T(8,128)(2,1)S(1)} %add_convert_fusion) | copy-start | bytes 98308
  30.3 10.8 %collective-permute-start.15 = (bf16[16,512]{1,0:T(8,128)(2,1)S(1)}, bf16[16,512]{1,0:T(8,128)(2,1)S(1)}, u32[]{:S(2)}, u32[]{:S(2)}) collective-permute-start(bf16[16,512]{1,0:T(8,128)(2,1)S(1)} %constant_dynamic-slice_fusion), channel_id=1, source_target_pairs={{0,32},{8,40},{16,48},{24,56},{32,0},{40,8},{48,16},{56,24},{64,96... | collective-permute-start | bytes 49160 | tf_op jit(solution)/shard_map/ppermute | solution.py:31
  36.0 5.1 %copy-start.18 = (bf16[32,512]{1,0:T(8,128)(2,1)S(1)}, bf16[32,512]{1,0:T(8,128)(2,1)}, u32[]{:S(2)}) copy-start(bf16[32,512]{1,0:T(8,128)(2,1)} %copy-done.17) | copy-start | bytes 98308
  36.0 35.1 %copy-start.12 = (bf16[256,512]{1,0:T(8,128)(2,1)S(1)}, bf16[256,512]{1,0:T(8,128)(2,1)}, u32[]{:S(2)}) copy-start(bf16[256,512]{1,0:T(8,128)(2,1)} %get-tuple-element.18) | copy-start | bytes 786436
  36.0 35.1 %copy-start.13 = (bf16[256,512]{1,0:T(8,128)(2,1)S(1)}, bf16[256,512]{1,0:T(8,128)(2,1)}, u32[]{:S(2)}) copy-start(bf16[256,512]{1,0:T(8,128)(2,1)} %get-tuple-element.23) | copy-start | bytes 786436
  37.3 33.9 %copy-start.14 = (bf16[256,512]{1,0:T(8,128)(2,1)S(1)}, bf16[256,512]{1,0:T(8,128)(2,1)}, u32[]{:S(2)}) copy-start(bf16[256,512]{1,0:T(8,128)(2,1)} %get-tuple-element.24) | copy-start | bytes 786436
  37.3 33.8 %copy-start.15 = (bf16[256,512]{1,0:T(8,128)(2,1)S(1)}, bf16[256,512]{1,0:T(8,128)(2,1)}, u32[]{:S(2)}) copy-start(bf16[256,512]{1,0:T(8,128)(2,1)} %get-tuple-element.25) | copy-start | bytes 786436
  41.1 6.7 %collective-permute-start.16 = (bf16[16,512]{1,0:T(8,128)(2,1)S(1)}, bf16[16,512]{1,0:T(8,128)(2,1)S(1)}, u32[]{:S(2)}, u32[]{:S(2)}) collective-permute-start(bf16[16,512]{1,0:T(8,128)(2,1)S(1)} %get-tuple-element.3), channel_id=1, source_target_pairs={{0,32},{8,40},{16,48},{24,56},{32,0},{40,8},{48,16},{56,24},{64,96... | collective-permute-start | bytes 49160 | tf_op jit(solution)/shard_map/ppermute | solution.py:31
  47.8 2.8 %collective-permute-start.17 = (bf16[32,512]{1,0:T(8,128)(2,1)S(1)}, bf16[32,512]{1,0:T(8,128)(2,1)S(1)}, u32[]{:S(2)}, u32[]{:S(2)}) collective-permute-start(bf16[32,512]{1,0:T(8,128)(2,1)S(1)} %constant_dynamic-update-slice_fusion.8), channel_id=1, source_target_pairs={{0,64},{8,72},{16,80},{24,88},{32,96},{40,104},{48,112},{56,120},{... | collective-permute-start | bytes 98312 | tf_op jit(solution)/shard_map/ppermute | solution.py:31
  50.6 4.8 %collective-permute-start.18 = (bf16[32,512]{1,0:T(8,128)(2,1)S(1)}, bf16[32,512]{1,0:T(8,128)(2,1)S(1)}, u32[]{:S(2)}, u32[]{:S(2)}) collective-permute-start(bf16[32,512]{1,0:T(8,128)(2,1)S(1)} %constant_dynamic-update-slice_fusion.8), channel_id=1, source_target_pairs={{0,128},{8,136},{16,144},{24,152},{32,160},{40,168},{48,176},{56,1... | collective-permute-start | bytes 98312 | tf_op jit(solution)/shard_map/ppermute | solution.py:31
  55.4 5.4 %collective-permute-start.19 = (bf16[32,512]{1,0:T(8,128)(2,1)S(1)}, bf16[32,512]{1,0:T(8,128)(2,1)S(1)}, u32[]{:S(2)}, u32[]{:S(2)}) collective-permute-start(bf16[32,512]{1,0:T(8,128)(2,1)S(1)} %constant_dynamic-update-slice_fusion.8), channel_id=1, source_target_pairs={{0,192},{8,200},{16,208},{24,216},{32,224},{40,232},{48,240},{56,2... | collective-permute-start | bytes 98312 | tf_op jit(solution)/shard_map/ppermute | solution.py:31
  58.7 10.8 %collective-permute-start.34 = (bf16[512,256]{1,0:T(8,128)(2,1)}, bf16[512,256]{1,0:T(8,128)(2,1)S(1)}, u32[]{:S(2)}, u32[]{:S(2)}) collective-permute-start(bf16[512,256]{1,0:T(8,128)(2,1)} %collective-permute-done.33), channel_id=1, source_target_pairs={{0,2},{1,3},{2,0},{3,1},{4,6},{5,7},{6,4},{7,5},{8,10},{9,11},{10,... | collective-permute-start | bytes 786440 | tf_op jit(solution)/shard_map/ppermute | solution.py:31
  60.9 18.1 %collective-permute-start.1 = (bf16[512,256]{1,0:T(8,128)(2,1)}, bf16[512,256]{1,0:T(8,128)(2,1)S(1)}, u32[]{:S(2)}, u32[]{:S(2)}) collective-permute-start(bf16[512,256]{1,0:T(8,128)(2,1)} %get-tuple-element.38), channel_id=1, source_target_pairs={{0,2},{1,3},{2,0},{3,1},{4,6},{5,7},{6,4},{7,5},{8,10},{9,11},{10,... | collective-permute-start | bytes 786440 | tf_op jit(solution)/shard_map/ppermute | solution.py:31
  62.2 83.7 %collective-permute-start.23 = (bf16[256,2048]{1,0:T(8,128)(2,1)S(1)}, bf16[256,2048]{1,0:T(8,128)(2,1)S(1)}, u32[]{:S(2)}, u32[]{:S(2)}) collective-permute-start(bf16[256,2048]{1,0:T(8,128)(2,1)S(1)} %pad_maximum_fusion.3), channel_id=1, source_target_pairs={{0,1},{1,0},{2,3},{3,2},{4,5},{5,4},{6,7},{7,6},{8,9},{9,8},{10,11... | collective-permute-start | bytes 3145736 | tf_op jit(solution)/shard_map/ppermute | solution.py:31
  67.8 5.6 %collective-permute-start.20 = (bf16[128,512]{1,0:T(8,128)(2,1)S(1)}, bf16[128,512]{1,0:T(8,128)(2,1)S(1)}, u32[]{:S(2)}, u32[]{:S(2)}) collective-permute-start(bf16[128,512]{1,0:T(8,128)(2,1)S(1)} %constant_dynamic-update-slice_fusion.4), channel_id=1, source_target_pairs={{0,8},{8,0},{16,24},{24,16},{32,40},{40,32},{48,56},{56,48},{64,72... | collective-permute-start | bytes 393224 | tf_op jit(solution)/shard_map/ppermute | solution.py:31
  69.5 9.3 %collective-permute-start.21 = (bf16[128,512]{1,0:T(8,128)(2,1)S(1)}, bf16[128,512]{1,0:T(8,128)(2,1)S(1)}, u32[]{:S(2)}, u32[]{:S(2)}) collective-permute-start(bf16[128,512]{1,0:T(8,128)(2,1)S(1)} %constant_dynamic-update-slice_fusion.4), channel_id=1, source_target_pairs={{0,16},{8,24},{16,0},{24,8},{32,48},{40,56},{48,32},{56,40},{64,80... | collective-permute-start | bytes 393224 | tf_op jit(solution)/shard_map/ppermute | solution.py:31
  71.1 8.8 %collective-permute-start.3 = (bf16[512,256]{1,0:T(8,128)(2,1)}, bf16[512,256]{1,0:T(8,128)(2,1)S(1)}, u32[]{:S(2)}, u32[]{:S(2)}) collective-permute-start(bf16[512,256]{1,0:T(8,128)(2,1)} %collective-permute-done.2), channel_id=1, source_target_pairs={{0,2},{1,3},{2,0},{3,1},{4,6},{5,7},{6,4},{7,5},{8,10},{9,11},{10,... | collective-permute-start | bytes 786440 | tf_op jit(solution)/shard_map/ppermute | solution.py:31
  71.2 8.7 %copy-start.16 = (bf16[512,256]{1,0:T(8,128)(2,1)S(1)}, bf16[512,256]{1,0:T(8,128)(2,1)}, u32[]{:S(2)}) copy-start(bf16[512,256]{1,0:T(8,128)(2,1)} %get-tuple-element.38) | copy-start | bytes 786436
  73.4 10.0 %collective-permute-start.35 = (f32[512,256]{1,0:T(8,128)S(1)}, f32[512,256]{1,0:T(8,128)S(1)}, u32[]{:S(2)}, u32[]{:S(2)}) collective-permute-start(f32[512,256]{1,0:T(8,128)S(1)} %fusion.19), channel_id=1, source_target_pairs={{0,1},{1,0},{2,3},{3,2},{4,5},{5,4},{6,7},{7,6},{8,9},{9,8},{10,11... | collective-permute-start | bytes 1572872 | tf_op jit(solution)/shard_map/ppermute | solution.py:31
  78.8 4.6 %collective-permute-start.5 = (bf16[256,512]{1,0:T(8,128)(2,1)S(1)}, bf16[256,512]{1,0:T(8,128)(2,1)S(1)}, u32[]{:S(2)}, u32[]{:S(2)}) collective-permute-start(bf16[256,512]{1,0:T(8,128)(2,1)S(1)} %get-tuple-element.41), channel_id=1, source_target_pairs={{0,1},{1,0},{2,3},{3,2},{4,5},{5,4},{6,7},{7,6},{8,9},{9,8},{10,11... | collective-permute-start | bytes 786440 | tf_op jit(solution)/shard_map/ppermute | solution.py:31
  79.0 10.4 %collective-permute-start.22 = (bf16[128,512]{1,0:T(8,128)(2,1)S(1)}, bf16[128,512]{1,0:T(8,128)(2,1)S(1)}, u32[]{:S(2)}, u32[]{:S(2)}) collective-permute-start(bf16[128,512]{1,0:T(8,128)(2,1)S(1)} %constant_dynamic-update-slice_fusion.4), channel_id=1, source_target_pairs={{0,24},{8,16},{16,8},{24,0},{32,56},{40,48},{48,40},{56,32},{64,88... | collective-permute-start | bytes 393224 | tf_op jit(solution)/shard_map/ppermute | solution.py:31
  81.9 5.2 %collective-permute-start.4 = (f32[512,256]{1,0:T(8,128)S(1)}, f32[512,256]{1,0:T(8,128)S(1)}, u32[]{:S(2)}, u32[]{:S(2)}) collective-permute-start(f32[512,256]{1,0:T(8,128)S(1)} %fusion.3), channel_id=1, source_target_pairs={{0,1},{1,0},{2,3},{3,2},{4,5},{5,4},{6,7},{7,6},{8,9},{9,8},{10,11... | collective-permute-start | bytes 1572872 | tf_op jit(solution)/shard_map/ppermute | solution.py:31
  85.5 8.1 %collective-permute-start.37 = (bf16[512,256]{1,0:T(8,128)(2,1)S(1)}, bf16[512,256]{1,0:T(8,128)(2,1)S(1)}, u32[]{:S(2)}, u32[]{:S(2)}) collective-permute-start(bf16[512,256]{1,0:T(8,128)(2,1)S(1)} %get-tuple-element.33), channel_id=1, source_target_pairs={{0,2},{1,3},{2,0},{3,1},{4,6},{5,7},{6,4},{7,5},{8,10},{9,11},{10,... | collective-permute-start | bytes 786440 | tf_op jit(solution)/shard_map/ppermute | solution.py:31
  89.2 11.4 %copy-start.4 = (f32[512,512]{1,0:T(8,128)S(1)}, f32[512,512]{1,0:T(8,128)}, u32[]{:S(2)}) copy-start(f32[512,512]{1,0:T(8,128)} %param.13) | copy-start | bytes 3145732
  89.2 11.4 %copy-start.5 = (f32[512,512]{1,0:T(8,128)S(1)}, f32[512,512]{1,0:T(8,128)}, u32[]{:S(2)}) copy-start(f32[512,512]{1,0:T(8,128)} %param.14) | copy-start | bytes 3145732
  89.2 9.9 %collective-permute-start.7 = (bf16[512,256]{1,0:T(8,128)(2,1)S(1)}, bf16[512,256]{1,0:T(8,128)(2,1)S(1)}, u32[]{:S(2)}, u32[]{:S(2)}) collective-permute-start(bf16[512,256]{1,0:T(8,128)(2,1)S(1)} %get-tuple-element.29), channel_id=1, source_target_pairs={{0,2},{1,3},{2,0},{3,1},{4,6},{5,7},{6,4},{7,5},{8,10},{9,11},{10,... | collective-permute-start | bytes 786440 | tf_op jit(solution)/shard_map/ppermute | solution.py:31
  89.4 15.4 %collective-permute-start.36 = (bf16[512,256]{1,0:T(8,128)(2,1)S(1)}, bf16[512,256]{1,0:T(8,128)(2,1)S(1)}, u32[]{:S(2)}, u32[]{:S(2)}) collective-permute-start(bf16[512,256]{1,0:T(8,128)(2,1)S(1)} %get-tuple-element.32), channel_id=1, source_target_pairs={{0,2},{1,3},{2,0},{3,1},{4,6},{5,7},{6,4},{7,5},{8,10},{9,11},{10,... | collective-permute-start | bytes 786440 | tf_op jit(solution)/shard_map/ppermute | solution.py:31
  90.9 19.5 %collective-permute-start.6 = (bf16[512,256]{1,0:T(8,128)(2,1)S(1)}, bf16[512,256]{1,0:T(8,128)(2,1)S(1)}, u32[]{:S(2)}, u32[]{:S(2)}) collective-permute-start(bf16[512,256]{1,0:T(8,128)(2,1)S(1)} %get-tuple-element.28), channel_id=1, source_target_pairs={{0,2},{1,3},{2,0},{3,1},{4,6},{5,7},{6,4},{7,5},{8,10},{9,11},{10,... | collective-permute-start | bytes 786440 | tf_op jit(solution)/shard_map/ppermute | solution.py:31
  93.6 23.6 %collective-permute-start.38 = (bf16[512,256]{1,0:T(8,128)(2,1)S(1)}, bf16[512,256]{1,0:T(8,128)(2,1)S(1)}, u32[]{:S(2)}, u32[]{:S(2)}) collective-permute-start(bf16[512,256]{1,0:T(8,128)(2,1)S(1)} %fusion.54), channel_id=1, source_target_pairs={{0,6},{1,7},{2,4},{3,5},{4,2},{5,3},{6,0},{7,1},{8,14},{9,15},{10,... | collective-permute-start | bytes 786440 | tf_op jit(solution)/shard_map/ppermute | solution.py:31
  99.2 23.6 %copy-start = (f32[1,512,512]{2,1,0:T(8,128)S(1)}, f32[1,512,512]{2,1,0:T(8,128)}, u32[]{:S(2)}) copy-start(f32[1,512,512]{2,1,0:T(8,128)} %param.11) | copy-start | bytes 3145732
  99.2 23.6 %copy-start.1 = (f32[1,512,512]{2,1,0:T(8,128)S(1)}, f32[1,512,512]{2,1,0:T(8,128)}, u32[]{:S(2)}) copy-start(f32[1,512,512]{2,1,0:T(8,128)} %param.12) | copy-start | bytes 3145732
  99.2 23.6 %copy-start.3 = (bf16[1,512,512]{2,1,0:T(8,128)(2,1)S(1)}, bf16[1,512,512]{2,1,0:T(8,128)(2,1)}, u32[]{:S(2)}) copy-start(bf16[1,512,512]{2,1,0:T(8,128)(2,1)} %param.10) | copy-start | bytes 1572868
  99.3 23.6 %collective-permute-start.8 = (bf16[512,256]{1,0:T(8,128)(2,1)S(1)}, bf16[512,256]{1,0:T(8,128)(2,1)S(1)}, u32[]{:S(2)}, u32[]{:S(2)}) collective-permute-start(bf16[512,256]{1,0:T(8,128)(2,1)S(1)} %fusion.60), channel_id=1, source_target_pairs={{0,6},{1,7},{2,4},{3,5},{4,2},{5,3},{6,0},{7,1},{8,14},{9,15},{10,... | collective-permute-start | bytes 786440 | tf_op jit(solution)/shard_map/ppermute | solution.py:31
  100.9 23.1 %copy-start.2 = (f32[512,512]{1,0:T(8,128)}, f32[512,512]{1,0:T(8,128)S(1)}, u32[]{:S(2)}) copy-start(f32[512,512]{1,0:T(8,128)S(1)} %fusion.2) | copy-start | bytes 3145732
  122.9 28.2 %copy-start.8 = (bf16[256,512]{1,0:T(8,128)(2,1)S(1)}, bf16[256,512]{1,0:T(8,128)(2,1)}, u32[]{:S(2)}) copy-start(bf16[256,512]{1,0:T(8,128)(2,1)} %get-tuple-element.10) | copy-start | bytes 786436
  122.9 28.1 %copy-start.9 = (bf16[256,512]{1,0:T(8,128)(2,1)S(1)}, bf16[256,512]{1,0:T(8,128)(2,1)}, u32[]{:S(2)}) copy-start(bf16[256,512]{1,0:T(8,128)(2,1)} %get-tuple-element.15) | copy-start | bytes 786436
  122.9 28.1 %copy-start.10 = (bf16[256,512]{1,0:T(8,128)(2,1)S(1)}, bf16[256,512]{1,0:T(8,128)(2,1)}, u32[]{:S(2)}) copy-start(bf16[256,512]{1,0:T(8,128)(2,1)} %get-tuple-element.16) | copy-start | bytes 786436
  122.9 28.1 %copy-start.11 = (bf16[256,512]{1,0:T(8,128)(2,1)S(1)}, bf16[256,512]{1,0:T(8,128)(2,1)}, u32[]{:S(2)}) copy-start(bf16[256,512]{1,0:T(8,128)(2,1)} %get-tuple-element.17) | copy-start | bytes 786436
  124.0 9.0 %collective-permute-start.40 = (bf16[512,256]{1,0:T(8,128)(2,1)S(1)}, bf16[512,256]{1,0:T(8,128)(2,1)S(1)}, u32[]{:S(2)}, u32[]{:S(2)}) collective-permute-start(bf16[512,256]{1,0:T(8,128)(2,1)S(1)} %get-tuple-element.7), channel_id=1, source_target_pairs={{0,6},{1,7},{2,4},{3,5},{4,2},{5,3},{6,0},{7,1},{8,14},{9,15},{10,... | collective-permute-start | bytes 786440 | tf_op jit(solution)/shard_map/ppermute | solution.py:31
  126.1 13.0 %collective-permute-start.25 = (bf16[512,256]{1,0:T(8,128)(2,1)S(1)}, bf16[512,256]{1,0:T(8,128)(2,1)S(1)}, u32[]{:S(2)}, u32[]{:S(2)}) collective-permute-start(bf16[512,256]{1,0:T(8,128)(2,1)S(1)} %get-tuple-element.6), channel_id=1, source_target_pairs={{0,6},{1,7},{2,4},{3,5},{4,2},{5,3},{6,0},{7,1},{8,14},{9,15},{10,... | collective-permute-start | bytes 786440 | tf_op jit(solution)/shard_map/ppermute | solution.py:31
  127.3 18.6 %collective-permute-start.39 = (bf16[512,256]{1,0:T(8,128)(2,1)S(1)}, bf16[512,256]{1,0:T(8,128)(2,1)S(1)}, u32[]{:S(2)}, u32[]{:S(2)}) collective-permute-start(bf16[512,256]{1,0:T(8,128)(2,1)S(1)} %get-tuple-element.7), channel_id=1, source_target_pairs={{0,2},{1,3},{2,0},{3,1},{4,6},{5,7},{6,4},{7,5},{8,10},{9,11},{10,... | collective-permute-start | bytes 786440 | tf_op jit(solution)/shard_map/ppermute | solution.py:31
  132.9 18.1 %collective-permute-start.41 = (bf16[512,256]{1,0:T(8,128)(2,1)S(1)}, bf16[512,256]{1,0:T(8,128)(2,1)S(1)}, u32[]{:S(2)}, u32[]{:S(2)}) collective-permute-start(bf16[512,256]{1,0:T(8,128)(2,1)S(1)} %collective-permute-done.40), channel_id=1, source_target_pairs={{0,2},{1,3},{2,0},{3,1},{4,6},{5,7},{6,4},{7,5},{8,10},{9,11},{10,... | collective-permute-start | bytes 786440 | tf_op jit(solution)/shard_map/ppermute | solution.py:31
  139.1 17.6 %collective-permute-start.24 = (bf16[512,256]{1,0:T(8,128)(2,1)S(1)}, bf16[512,256]{1,0:T(8,128)(2,1)S(1)}, u32[]{:S(2)}, u32[]{:S(2)}) collective-permute-start(bf16[512,256]{1,0:T(8,128)(2,1)S(1)} %get-tuple-element.6), channel_id=1, source_target_pairs={{0,2},{1,3},{2,0},{3,1},{4,6},{5,7},{6,4},{7,5},{8,10},{9,11},{10,... | collective-permute-start | bytes 786440 | tf_op jit(solution)/shard_map/ppermute | solution.py:31
  139.1 23.2 %collective-permute-start.26 = (bf16[512,256]{1,0:T(8,128)(2,1)S(1)}, bf16[512,256]{1,0:T(8,128)(2,1)S(1)}, u32[]{:S(2)}, u32[]{:S(2)}) collective-permute-start(bf16[512,256]{1,0:T(8,128)(2,1)S(1)} %collective-permute-done.25), channel_id=1, source_target_pairs={{0,2},{1,3},{2,0},{3,1},{4,6},{5,7},{6,4},{7,5},{8,10},{9,11},{10,... | collective-permute-start | bytes 786440 | tf_op jit(solution)/shard_map/ppermute | solution.py:31
  151.8 11.8 %collective-permute-start.42 = (f32[512,256]{1,0:T(8,128)S(1)}, f32[512,256]{1,0:T(8,128)S(1)}, u32[]{:S(2)}, u32[]{:S(2)}) collective-permute-start(f32[512,256]{1,0:T(8,128)S(1)} %fusion.27), channel_id=1, source_target_pairs={{0,1},{1,0},{2,3},{3,2},{4,5},{5,4},{6,7},{7,6},{8,9},{9,8},{10,11... | collective-permute-start | bytes 1572872 | tf_op jit(solution)/shard_map/ppermute | solution.py:31
  152.4 11.2 %collective-permute-start.28 = (bf16[256,512]{1,0:T(8,128)(2,1)S(1)}, bf16[256,512]{1,0:T(8,128)(2,1)S(1)}, u32[]{:S(2)}, u32[]{:S(2)}) collective-permute-start(bf16[256,512]{1,0:T(8,128)(2,1)S(1)} %get-tuple-element.40), channel_id=1, source_target_pairs={{0,1},{1,0},{2,3},{3,2},{4,5},{5,4},{6,7},{7,6},{8,9},{9,8},{10,11... | collective-permute-start | bytes 786440 | tf_op jit(solution)/shard_map/ppermute | solution.py:31
  163.0 2.1 %collective-permute-start.27 = (f32[512,256]{1,0:T(8,128)S(1)}, f32[512,256]{1,0:T(8,128)S(1)}, u32[]{:S(2)}, u32[]{:S(2)}) collective-permute-start(f32[512,256]{1,0:T(8,128)S(1)} %fusion.11), channel_id=1, source_target_pairs={{0,1},{1,0},{2,3},{3,2},{4,5},{5,4},{6,7},{7,6},{8,9},{9,8},{10,11... | collective-permute-start | bytes 1572872 | tf_op jit(solution)/shard_map/ppermute | solution.py:31
  164.5 8.0 %collective-permute-start.44 = (bf16[512,256]{1,0:T(8,128)(2,1)S(1)}, bf16[512,256]{1,0:T(8,128)(2,1)S(1)}, u32[]{:S(2)}, u32[]{:S(2)}) collective-permute-start(bf16[512,256]{1,0:T(8,128)(2,1)S(1)} %get-tuple-element.31), channel_id=1, source_target_pairs={{0,2},{1,3},{2,0},{3,1},{4,6},{5,7},{6,4},{7,5},{8,10},{9,11},{10,... | collective-permute-start | bytes 786440 | tf_op jit(solution)/shard_map/ppermute | solution.py:31
  166.0 12.1 %collective-permute-start.30 = (bf16[512,256]{1,0:T(8,128)(2,1)S(1)}, bf16[512,256]{1,0:T(8,128)(2,1)S(1)}, u32[]{:S(2)}, u32[]{:S(2)}) collective-permute-start(bf16[512,256]{1,0:T(8,128)(2,1)S(1)} %get-tuple-element.27), channel_id=1, source_target_pairs={{0,2},{1,3},{2,0},{3,1},{4,6},{5,7},{6,4},{7,5},{8,10},{9,11},{10,... | collective-permute-start | bytes 786440 | tf_op jit(solution)/shard_map/ppermute | solution.py:31
  167.0 16.7 %collective-permute-start.43 = (bf16[512,256]{1,0:T(8,128)(2,1)S(1)}, bf16[512,256]{1,0:T(8,128)(2,1)S(1)}, u32[]{:S(2)}, u32[]{:S(2)}) collective-permute-start(bf16[512,256]{1,0:T(8,128)(2,1)S(1)} %get-tuple-element.30), channel_id=1, source_target_pairs={{0,2},{1,3},{2,0},{3,1},{4,6},{5,7},{6,4},{7,5},{8,10},{9,11},{10,... | collective-permute-start | bytes 786440 | tf_op jit(solution)/shard_map/ppermute | solution.py:31
  167.6 21.8 %collective-permute-start.29 = (bf16[512,256]{1,0:T(8,128)(2,1)S(1)}, bf16[512,256]{1,0:T(8,128)(2,1)S(1)}, u32[]{:S(2)}, u32[]{:S(2)}) collective-permute-start(bf16[512,256]{1,0:T(8,128)(2,1)S(1)} %get-tuple-element.26), channel_id=1, source_target_pairs={{0,2},{1,3},{2,0},{3,1},{4,6},{5,7},{6,4},{7,5},{8,10},{9,11},{10,... | collective-permute-start | bytes 786440 | tf_op jit(solution)/shard_map/ppermute | solution.py:31
  172.5 23.2 %collective-permute-start.45 = (bf16[512,256]{1,0:T(8,128)(2,1)S(1)}, bf16[512,256]{1,0:T(8,128)(2,1)S(1)}, u32[]{:S(2)}, u32[]{:S(2)}) collective-permute-start(bf16[512,256]{1,0:T(8,128)(2,1)S(1)} %fusion.51), channel_id=1, source_target_pairs={{0,6},{1,7},{2,4},{3,5},{4,2},{5,3},{6,0},{7,1},{8,14},{9,15},{10,... | collective-permute-start | bytes 786440 | tf_op jit(solution)/shard_map/ppermute | solution.py:31
  178.2 23.2 %collective-permute-start.31 = (bf16[512,256]{1,0:T(8,128)(2,1)S(1)}, bf16[512,256]{1,0:T(8,128)(2,1)S(1)}, u32[]{:S(2)}, u32[]{:S(2)}) collective-permute-start(bf16[512,256]{1,0:T(8,128)(2,1)S(1)} %fusion.57), channel_id=1, source_target_pairs={{0,6},{1,7},{2,4},{3,5},{4,2},{5,3},{6,0},{7,1},{8,14},{9,15},{10,... | collective-permute-start | bytes 786440 | tf_op jit(solution)/shard_map/ppermute | solution.py:31
  (1 other events, 1.9 us)

commit v2 on v0

v2 whole, which is shorter than its diff:
```python
import functools

import jax
import jax.numpy as jnp
from jax import lax
from jax.experimental import pallas as pl
from jax.experimental.pallas import tpu as pltpu
from jax.sharding import PartitionSpec as P

CHUNKS = 2

inner_rate = 0.2
beta_first = 0.9
beta_second = 0.95
adam_eps = 1e-08
decay_rate = 0.1
mix_share = 0.5
outer_rate = 0.7
outer_beta = 0.9

BF = jnp.bfloat16
F32 = jnp.float32
VMEM_LIMIT = 16 << 20
PREPARE_LIMIT = 56 << 20
FLOPS = 10**11

ANY = pl.BlockSpec(memory_space=pl.ANY)
FULL = pl.BlockSpec(memory_space=pltpu.VMEM)
SCALAR = pl.BlockSpec(memory_space=pltpu.SMEM)


def swap(value, axis, change):
    pairs = [(i, change(i)) for i in range(lax.axis_size(axis))]
    return lax.ppermute(value, axis, pairs)


def pair_swap(value, g):
    return swap(value, "fsdp", lambda i: i ^ g)


def far_swap(value):
    return swap(value, "fsdp", lambda i: i ^ 6)


def shaped(shape, dtype):
    return jax.ShapeDtypeStruct(shape, dtype)


def call(body, outs, operands, gates=(), specs=None, limit=VMEM_LIMIT, scratch=()):
    n = len(gates)
    size = sum(v.size * v.dtype.itemsize for v in operands)

    def kernel(*refs):
        body(*refs[n:])

    return pl.pallas_call(
        kernel,
        name=getattr(body, "func", body).__name__.removesuffix("_kernel"),
        grid=(1,),
        out_shape=outs,
        in_specs=[ANY] * n + (specs or [FULL] * len(operands)),
        out_specs=jax.tree.map(lambda _: FULL, outs),
        scratch_shapes=scratch,
        compiler_params=pltpu.CompilerParams(vmem_limit_bytes=limit),
        cost_estimate=pl.CostEstimate(flops=FLOPS, bytes_accessed=size, transcendentals=0),
    )(*gates, *operands)


def prepare_kernel(step, groups, depth, place, feats, *refs):
    outs, done = refs[:-1], refs[-1]
    copies = []
    for g, out in zip(groups, outs):
        at = place[0] ^ g
        for j, shard in enumerate((at, at ^ 6)):
            columns = pl.ds(pl.multiple_of(shard * depth, depth), depth)
            copies.append(
                pltpu.make_async_copy(
                    feats.at[step, 0, :, columns],
                    out.at[:, j * depth : (j + 1) * depth],
                    done.at[len(copies)],
                )
            )
    for copy in copies:
        copy.start()
    for copy in copies:
        copy.wait()


def keys_kernel(scale, place, *refs):
    feats, chunks, (kept, sent, whole) = refs[:4], refs[4:-3], refs[-3:]
    rows = feats[0].shape[0]
    core = place[0] % 2
    for k in range(len(chunks) // 3):
        aims, own, far = chunks[3 * k : 3 * k + 3]
        depth, cols = own.shape[0], own.shape[1] // 2
        for g in range(4):
            part = jnp.dot(feats[g][:, :depth], own[...], preferred_element_type=F32)
            part += jnp.dot(feats[g][:, depth:], far[...], preferred_element_type=F32)
            part *= scale
            if g == 0:
                part -= aims[...].astype(F32)
            whole[...] = part
            for half, out in ((1 - core, sent), (core, kept)):
                columns = pl.ds(pl.multiple_of(half * cols, cols), cols)
                out[g * rows : (g + 1) * rows, k * cols : (k + 1) * cols] = whole[:, columns]


def core_sum_kernel(*refs):
    pairs, out = refs[:-1], refs[-1]
    rows = out.shape[0] // 4
    cols = pairs[0].shape[1]
    for k in range(len(pairs) // 2):
        kept, other = pairs[2 * k : 2 * k + 2]
        for g in range(4):
            here, there = g * rows, (g ^ 1) * rows
            total = kept[here : here + rows] + other[there : there + rows]
            out[here : here + rows, k * cols : (k + 1) * cols] = total.astype(BF)


def residual_kernel(part, other, out):
    rows = out.shape[0] // 4
    for g in range(4):
        here, there = g * rows, (g ^ 2) * rows
        total = part[here : here + rows].astype(F32) + other[there : there + rows].astype(F32)
        out[here : here + rows] = total.astype(BF)


def grads_kernel(shard, place, *refs):
    feats, (mine, other), outs, whole = refs[:4], refs[4:6], refs[6:-1], refs[-1]
    rows, depth = feats[0].shape[0], outs[0].shape[0]
    core = place[0] % 2
    cols = mine.shape[1] // CHUNKS
    for k in range(CHUNKS):
        part = slice(k * cols, (k + 1) * cols)
        for half, residual, flip in ((core, mine, 0), (1 - core, other, 1)):
            columns = pl.ds(pl.multiple_of((2 * k + half) * cols, cols), cols)
            for g in range(4):
                there = (g ^ flip) * rows
                whole[g * rows : (g + 1) * rows, columns] = residual[there : there + rows, part]
    at = slice(shard * depth, (shard + 1) * depth)
    dims = (((0,), (0,)), ((), ()))
    total = None
    for g in range(4):
        term = lax.dot_general(
            feats[g][:, at],
            whole[g * rows : (g + 1) * rows],
            dims,
            preferred_element_type=F32,
        )
        total = term if total is None else total + term
    cols = outs[0].shape[1]
    for k, out in enumerate(outs):
        out[...] = total[:, k * cols : (k + 1) * cols].astype(out.dtype)


def cast_kernel(drift, out):
    share, rows = out.shape[0], out.shape[1]
    for i in range(share):
        out[i] = drift[0, i * rows : (i + 1) * rows].astype(BF)


def sum_kernel(pieces, out):
    out[...] = jnp.sum(pieces[...].astype(F32), axis=0).astype(BF)


def mean_kernel(replicas, part, other, out):
    mean = ((part[...].astype(F32) + other[...].astype(F32)) / replicas).astype(BF)
    out[...] = jnp.broadcast_to(mean[None], out.shape)


def planes(size):
    return [[i for i in range(size) if (i // 4) % 2 == hi] for hi in range(2)]


def adam(factor, kept, far, own, one, two):
    grad = (kept + far.astype(F32)) * factor
    one = beta_first * one + (1.0 - beta_first) * grad
    two = beta_second * two + (1.0 - beta_second) * grad * grad
    wide = own.astype(F32)
    updated = wide - inner_rate * (one / (jnp.sqrt(two) + adam_eps) + decay_rate * wide)
    return one, two, updated


def first_update_kernel(factor, kept, far, own, one, two, outer, new, new_one, new_two):
    first, second, updated = adam(factor, kept[...], far[...], own[...], one[...], two[...])
    new_one[...] = first
    new_two[...] = second
    new[...] = (mix_share * updated + (1.0 - mix_share) * outer[...]).astype(BF)


def update_kernel(factor, kept, far, own, one, two, *rest):
    done, out = rest[:-1], rest[-1]
    _, _, updated = adam(factor, kept[...], far[...], own[...], one[...], two[...])
    cols = updated.shape[1]
    if done:
        for k, block in enumerate(done):
            out[0, :, k * cols : (k + 1) * cols] = block[...]
        out[0, :, len(done) * cols :] = updated.astype(BF)
    else:
        out[...] = updated.astype(BF)


def outer_kernel(pieces, global_weights, outer_moment, out):
    share, rows = pieces.shape[0], pieces.shape[1]
    for i in range(share):
        at = slice(i * rows, (i + 1) * rows)
        mean_drift = pieces[i].astype(F32)
        new_moment = outer_beta * outer_moment[at] + mean_drift
        out[at] = global_weights[at] - outer_rate * (mean_drift + outer_beta * new_moment)


def per_device(
    inputs, targets, weights, first_moment, second_moment, global_weights, outer_moment, drift
):
    place = lax.axis_index("fsdp").astype(jnp.int32).reshape(1)
    tok_rows, width = inputs.shape[2], inputs.shape[3]
    tokens_total = tok_rows * lax.axis_size("fsdp")
    scale = width ** (-0.5)
    rows, columns = weights.shape[1], weights.shape[2]
    wide = columns // CHUNKS
    cols = wide // 2
    factor = scale / tokens_total
    replicas = lax.axis_size("rep")
    groups = planes(replicas)
    share = len(groups[0])

    def prepare(step, wanted, gates):
        return call(
            functools.partial(prepare_kernel, step, wanted, rows),
            [shaped((tok_rows, 2 * rows), BF)] * len(wanted),
            [place, inputs],
            gates,
            [SCALAR, ANY],
            limit=PREPARE_LIMIT,
            scratch=[pltpu.SemaphoreType.DMA((2 * len(wanted),))],
        )

    def chunk(lead, k):
        at = lead + (0, k)
        height = tok_rows if len(lead) > 1 else rows
        return pl.BlockSpec((None,) * len(lead) + (height, wide), lambda i: at)

    def keys(step, feats, chunks, own, far, gates):
        views, specs = [], []
        for k in chunks:
            views += [targets, own, far]
            specs += [chunk((step, 0), k)] + ([chunk((0,), k)] if step == 0 else [FULL]) * 2
        return call(
            functools.partial(keys_kernel, scale),
            [shaped((4 * tok_rows, len(chunks) * cols), F32)] * 2,
            [place, *feats, *views],
            gates,
            [SCALAR] + [FULL] * 4 + specs,
            scratch=[pltpu.VMEM((tok_rows, wide), F32)],
        )

    def core_sum(pairs, gates):
        blocks = []
        for kept, sent in pairs:
            blocks += [kept, pair_swap(sent, 1)]
        out = shaped((4 * tok_rows, columns // 2), BF)
        return call(core_sum_kernel, out, blocks, gates)

    def residuals(part, gates):
        return call(residual_kernel, shaped(part.shape, BF), [part, pair_swap(part, 2)], gates)

    def grads(shard, dtype, parts, feats, mine, other, gates):
        return call(
            functools.partial(grads_kernel, shard),
            [shaped((rows, columns // parts), dtype)] * parts,
            [place, *feats, mine, other],
            gates,
            [SCALAR] + [FULL] * 6,
            scratch=[pltpu.VMEM((4 * tok_rows, columns), BF)],
        )

    def first_update(k, kept, far, gates):
        state = chunk((0,), k)
        block = shaped((rows, wide), F32)
        return call(
            functools.partial(first_update_kernel, factor),
            [shaped((rows, wide), BF), block, block],
            [kept, far, weights, first_moment, second_moment, global_out],
            gates,
            [chunk((), k), FULL, state, state, state, chunk((), k)],
        )

    def update(k, kept, far, own, one, two, done, gates):
        return call(
            functools.partial(update_kernel, factor),
            shaped((1, rows, columns) if done else (rows, wide), BF),
            [kept, far, own, one, two, *done],
            gates,
            [chunk((), k)] + [FULL] * (4 + len(done)),
        )

    far = far_swap(weights)
    packs = prepare(0, (0, 1, 2, 3), [])
    feats = [packs[0]] + [pair_swap(packs[g], g) for g in (1, 2, 3)]
    rows_of = rows // share
    casted = call(cast_kernel, shaped((share, rows_of, columns), BF), [drift], [feats[1]])
    pieces = lax.all_to_all(casted, "rep", 0, 0, axis_index_groups=groups)
    packs = prepare(1, (0, 1, 2, 3), [casted])
    summed = call(sum_kernel, shaped((rows_of, columns), BF), [pieces], [packs[0]])
    summed_other = swap(summed, "rep", lambda i: i ^ 4)

    both = keys(0, feats, (0, 1), weights, far, [summed])
    part = core_sum([both], [])
    copies = call(
        functools.partial(mean_kernel, replicas),
        shaped((share, rows_of, columns), BF),
        [summed, summed_other],
        [part],
    )
    means = lax.all_to_all(copies, "rep", 0, 0, axis_index_groups=groups)
    mine = residuals(part, [means])
    other = pair_swap(mine, 1)
    across_a, across_b = grads(1, BF, CHUNKS, feats, mine, other, [])
    far_a, far_b = far_swap(across_a), far_swap(across_b)
    later = [packs[0]] + [pair_swap(packs[g], g) for g in (1, 2, 3)]
    (kept,) = grads(0, F32, 1, feats, mine, other, [across_b])
    global_out = call(
        outer_kernel,
        shaped((rows, columns), F32),
        [means, global_weights, outer_moment],
        [kept],
    )
    own_a, one_a, two_a = first_update(0, kept, far_a, [])
    gather_a = far_swap(own_a)
    own_b, one_b, two_b = first_update(1, kept, far_b, [own_a, *later[1:3]])
    gather_b = far_swap(own_b)

    keys_a = keys(1, later, (0,), own_a, gather_a, [own_b])
    keys_b = keys(1, later, (1,), own_b, gather_b, [keys_a[0]])
    part = core_sum([keys_a, keys_b], [])
    mine = residuals(part, [])
    other = pair_swap(mine, 1)
    across_a, across_b = grads(1, BF, CHUNKS, later, mine, other, [])
    far_a, far_b = far_swap(across_a), far_swap(across_b)
    (kept,) = grads(0, F32, 1, later, mine, other, [across_b])
    done_a = update(0, kept, far_a, own_a, one_a, two_a, [], [])
    weights_out = update(1, kept, far_b, own_b, one_b, two_b, [done_a], [])
    return (weights_out, global_out)


def solution(mesh):
    in_specs = (
        P(None, "rep", "fsdp", None),
        P(None, "rep", "fsdp", None),
        P("rep", "fsdp", None),
        P("rep", "fsdp", None),
        P("rep", "fsdp", None),
        P("fsdp", None),
        P("fsdp", None),
        P("rep", "fsdp", None),
    )
    out_specs = (P("rep", "fsdp", None), P("fsdp", None))
    return jax.shard_map(
        per_device, mesh=mesh, in_specs=in_specs, out_specs=out_specs, check_vma=False
    )
```

time: 676 us -> 178 us (0.26)
  waiting for transfers between devices: 619 us -> 97.5 us
  Pallas kernels: 0 us -> 32.4 us
  starting transfers between devices: 0.21 us -> 26 us
  matrix products: 18.6 us -> 0 us
  blocking collectives: 0 us -> 16.1 us
  between operations: 15.2 us -> 0.87 us
  local copies, waits for them, and re-layouts: 12.6 us -> 3.82 us
    psum x1 -> x0, waiting for transfers between devices: 421 us -> none  [outer_update(): lax.psum(drift[0].astype(jnp.bfloat16), 'rep').astype(jnp.float32)]
    all_gather x2 -> x0, waiting for transfers between devices: 105 us -> none  [per_device(): lax.all_gather(current, 'fsdp', axis=0, tiled=True)]
    reduce_scatter x2 -> x0, waiting for transfers between devices: 91.7 us -> none  [per_device(): lax.psum_scatter(contract_rows(feats, residual), 'fsdp', scatter_dimensio...]
    ppermute x0 -> x21, waiting for transfers between devices: none -> 89.9 us  [swap(): return lax.ppermute(value, axis, pairs)]
    pallas_call x0 -> x21, Pallas kernels: none -> 32.4 us  [call(): pl.pallas_call(kernel, name=getattr(body, 'func', body).__name__.removesu...]
    dot_general x2 -> x0, matrix products: 18.6 us -> none  [contract_rows(): lax.dot_general(left, right, (((0,), (0,)), ((), ())), preferred_element_...]
    ppermute x0 -> x21, starting transfers between devices: none -> 18.5 us  [swap(): return lax.ppermute(value, axis, pairs)]
    all_to_all x0 -> x1, blocking collectives: none -> 16.1 us  [per_device(): means = lax.all_to_all(copies, 'rep', 0, 0, axis_index_groups=groups)]
  transfers between devices with their start and end apart: 5 -> 22, of which waited for: 4 -> 16; matrix products, arithmetic and copies ran while one was open for 3% -> 0% of each run, Pallas kernels for 0% -> 12%
where the time goes in v2:
time: 178 us; the launch traced here: 177 us
  waiting for transfers between devices  97.5 us (55%)
  Pallas kernels  32.4 us (18%)
  starting transfers between devices  26 us (15%)
  blocking collectives  16.1 us (9%)
  local copies, waits for them, and re-layouts  3.82 us (2%)
    ppermute x21, waiting for transfers between devices, swap(): return lax.ppermute(value, axis, pairs)  89.9 us
    pallas_call x21, Pallas kernels, call(): pl.pallas_call(kernel, name=getattr(body, 'func', body).__name__.removesu...  32.4 us
    ppermute x21, starting transfers between devices, swap(): return lax.ppermute(value, axis, pairs)  18.5 us
    all_to_all x1, blocking collectives, per_device(): means = lax.all_to_all(copies, 'rep', 0, 0, axis_index_groups=groups)  16.1 us
    all_to_all x1, waiting for transfers between devices, per_device(): pieces = lax.all_to_all(casted, 'rep', 0, 0, axis_index_groups=groups)  7.56 us
    all_to_all x1, starting transfers between devices, per_device(): pieces = lax.all_to_all(casted, 'rep', 0, 0, axis_index_groups=groups)  7.48 us
    unnamed x38, local copies, waits for them, and re-layouts  3.82 us
  transfers between devices with their start and end apart: 22, of which 16 were waited for; matrix products, arithmetic and copies ran while one was open for 0% of the time, Pallas kernels for 12%

profile of v2, /device:TPU:34, one launch (start us, length us, event | category | flops | bytes accessed | tf_op | source)
XLA Modules:
  0.0 176.7 jit_solution(11503579261495620576)
XLA Ops:
  0.6 3.0 %prepare.2 = (bf16[256,1024]{1,0:T(8,128)(2,1)}, bf16[256,1024]{1,0:T(8,128)(2,1)}, bf16[256,1024]{1,0:T(8,128)(2,1)}, bf16[256,1024]{1,0:T(8,128)(2,1)}) custom-call(s32[1]{0:T(128)} %bitcast.refs_0_.refs_1_, bf16[2,1,256,4096]{3,2,1,0:T(8,128)(2,1)} %refs_2_.3), custom_call_target="tpu_custom_call" | custom-call | flops 99999997952 | bytes 4194308 | tf_op jit(solution)/shard_map/prepare/pallas_call | solution.py:56
  3.6 0.1 collective-permute-start
  3.7 2.0 %collective-permute-start.6 = (bf16[1,512,512]{2,1,0:T(8,128)(2,1)}, bf16[1,512,512]{2,1,0:T(8,128)(2,1)}, u32[]{:S(2)}, u32[]{:S(2)}) collective-permute-start(bf16[1,512,512]{2,1,0:T(8,128)(2,1)} %refs_5_.1), channel_id=1, source_target_pairs={{0,6},{1,7},{2,4},{3,5},{4,2},{5,3},{6,0},{7,1},{8,14},{9,15},{10,... | collective-permute-start | bytes 1572872 | tf_op jit(solution)/shard_map/ppermute | solution.py:34
  5.8 2.8 %collective-permute-start.4 = (bf16[256,1024]{1,0:T(8,128)(2,1)}, bf16[256,1024]{1,0:T(8,128)(2,1)}, u32[]{:S(2)}, u32[]{:S(2)}) collective-permute-start(bf16[256,1024]{1,0:T(8,128)(2,1)} %get-tuple-element.32), channel_id=1, source_target_pairs={{0,2},{1,3},{2,0},{3,1},{4,6},{5,7},{6,4},{7,5},{8,10},{9,11},{10,... | collective-permute-start | bytes 1572872 | tf_op jit(solution)/shard_map/ppermute | solution.py:34
  8.6 0.8 cast.1.refs_0_
  9.4 0.8 copy-done.9
  10.3 7.5 %all-to-all-start = ((bf16[16,32,512]{2,1,0:T(8,128)(2,1)}), bf16[16,32,512]{2,1,0:T(8,128)(2,1)S(1)}, u32[]{:S(2)}, u32[]{:S(2)}) async-start(bf16[16,32,512]{2,1,0:T(8,128)(2,1)} %cast.1.refs_0_), calls=%async_computation | async-start | bytes 1048576 | tf_op jit(solution)/shard_map/all_to_all | solution.py:302
  17.7 2.9 %prepare.3 = (bf16[256,1024]{1,0:T(8,128)(2,1)}, bf16[256,1024]{1,0:T(8,128)(2,1)}, bf16[256,1024]{1,0:T(8,128)(2,1)}, bf16[256,1024]{1,0:T(8,128)(2,1)}) custom-call(bf16[16,32,512]{2,1,0:T(8,128)(2,1)} %cast.1.refs_0_, s32[1]{0:T(128)} %bitcast.refs_0_.refs_1_, bf16[2,1,256,4096]{3,2,1,0:T(8,128)(2,1)} %refs_2_.3), custom_call_target="tpu_custom_call" | custom-call | flops 99999997952 | bytes 4194308 | tf_op jit(solution)/shard_map/prepare/pallas_call | solution.py:56
  20.7 7.6 %all-to-all-done.refs_1_ = bf16[16,32,512]{2,1,0:T(8,128)(2,1)S(1)} async-done(((bf16[16,32,512]{2,1,0:T(8,128)(2,1)}), bf16[16,32,512]{2,1,0:T(8,128)(2,1)S(1)}, u32[]{:S(2)}, u32[]{:S(2)}) %all-to-all-start) | async-done | bytes 524320 | tf_op jit(solution)/shard_map/all_to_all | solution.py:302
  28.2 1.0 copy-done.17
  29.3 0.1 sum.1.refs_0_.refs_1_
  29.3 0.5 collective-permute-done.6.refs_8_.refs_11_
  29.8 3.1 %collective-permute-done.4.refs_4_.refs_3_ = bf16[256,1024]{1,0:T(8,128)(2,1)} collective-permute-done((bf16[256,1024]{1,0:T(8,128)(2,1)}, bf16[256,1024]{1,0:T(8,128)(2,1)}, u32[]{:S(2)}, u32[]{:S(2)}) %collective-permute-start.4) | collective-permute-done | bytes 524320 | tf_op jit(solution)/shard_map/ppermute | solution.py:34
  32.9 10.3 %collective-permute-done.5.refs_5_.refs_4_ = bf16[256,1024]{1,0:T(8,128)(2,1)} collective-permute-done((bf16[256,1024]{1,0:T(8,128)(2,1)}, bf16[256,1024]{1,0:T(8,128)(2,1)}, u32[]{:S(2)}, u32[]{:S(2)}) %collective-permute-start.5) | collective-permute-done | bytes 524320 | tf_op jit(solution)/shard_map/ppermute | solution.py:34
  43.2 3.2 %keys.3 = (f32[1024,256]{1,0:T(8,128)S(1)}, f32[1024,256]{1,0:T(8,128)S(1)}) custom-call(bf16[32,512]{1,0:T(8,128)(2,1)S(1)} %sum.1.refs_0_.refs_1_, s32[1]{0:T(128)} %bitcast.refs_0_.refs_1_, bf16[256,1024]{1,0:T(8,128)(2,1)S(1)} %copy-done.15, bf16[256,1024]{1,0:T(8,128)(2,1)S(1)} %copy-done.10, bf16[256,1024]{1,0:T(8,128)(2,1)} %collective-permute-done.4.refs_4_.refs_3_, ...), custom_call_target="tpu_custom_call" | custom-call | flops 99999997952 | bytes 5242884 | tf_op jit(solution)/shard_map/keys/pallas_call | solution.py:56
  46.4 0.4 collective-permute-start.7
  46.8 4.5 %collective-permute-start.8 = (bf16[32,512]{1,0:T(8,128)(2,1)S(1)}, bf16[32,512]{1,0:T(8,128)(2,1)S(1)}, u32[]{:S(2)}, u32[]{:S(2)}) collective-permute-start(bf16[32,512]{1,0:T(8,128)(2,1)S(1)} %sum.1.refs_0_.refs_1_), channel_id=1, source_target_pairs={{0,32},{8,40},{16,48},{24,56},{32,0},{40,8},{48,16},{56,24},{64,96... | collective-permute-start | bytes 98312 | tf_op jit(solution)/shard_map/ppermute | solution.py:34
  51.3 0.1 core_sum.2.refs_0_.refs_1_
  51.4 1.8 %collective-permute-start.9 = (bf16[1024,256]{1,0:T(8,128)(2,1)S(1)}, bf16[1024,256]{1,0:T(8,128)(2,1)S(1)}, u32[]{:S(2)}, u32[]{:S(2)}) collective-permute-start(bf16[1024,256]{1,0:T(8,128)(2,1)S(1)} %core_sum.2.refs_0_.refs_1_), channel_id=1, source_target_pairs={{0,2},{1,3},{2,0},{3,1},{4,6},{5,7},{6,4},{7,5},{8,10},{9,11},{10,... | collective-permute-start | bytes 1572872 | tf_op jit(solution)/shard_map/ppermute | solution.py:34
  53.2 2.0 %collective-permute-done.8.refs_2_ = bf16[32,512]{1,0:T(8,128)(2,1)S(1)} collective-permute-done((bf16[32,512]{1,0:T(8,128)(2,1)S(1)}, bf16[32,512]{1,0:T(8,128)(2,1)S(1)}, u32[]{:S(2)}, u32[]{:S(2)}) %collective-permute-start.8) | collective-permute-done | bytes 32800 | tf_op jit(solution)/shard_map/ppermute | solution.py:34
  55.3 16.1 %all_to_all.10.refs_0_.refs_1_ = bf16[16,32,512]{2,1,0:T(8,128)(2,1)S(1)} all-to-all(bf16[16,32,512]{2,1,0:T(8,128)(2,1)S(1)} %mean.1), channel_id=1, replica_groups={{0,8,16,24,64,72,80,88,128,136,144,152,192,200,208,216},{32,40,48,56,96..., dimensions={0} | all-to-all | bytes 1048576 | tf_op jit(solution)/shard_map/all_to_all | solution.py:315
  71.4 0.1 residual.2.refs_5_.refs_6_
  71.5 0.7 copy-done
  72.2 0.5 collective-permute-start.1
  72.7 0.7 collective-permute-start.2
  73.4 0.6 collective-permute-start.3
  74.1 0.8 collective-permute-done.10.refs_6_.refs_7_
  74.8 2.9 %grads.4 = (bf16[512,256]{1,0:T(8,128)(2,1)}, bf16[512,256]{1,0:T(8,128)(2,1)}) custom-call(s32[1]{0:T(128)} %bitcast.refs_0_.refs_1_, bf16[256,1024]{1,0:T(8,128)(2,1)S(1)} %copy-done.16, bf16[256,1024]{1,0:T(8,128)(2,1)S(1)} %copy-done.10, bf16[256,1024]{1,0:T(8,128)(2,1)} %collective-permute-done.4.refs_4_.refs_3_, ...), custom_call_target="tpu_custom_call" | custom-call | flops 99999997952 | bytes 3145732 | tf_op jit(solution)/shard_map/grads/pallas_call | solution.py:56
  77.7 0.2 collective-permute-start.11
  78.0 1.8 %collective-permute-start.12 = (bf16[512,256]{1,0:T(8,128)(2,1)}, bf16[512,256]{1,0:T(8,128)(2,1)}, u32[]{:S(2)}, u32[]{:S(2)}) collective-permute-start(bf16[512,256]{1,0:T(8,128)(2,1)} %get-tuple-element.36.refs_0_), channel_id=1, source_target_pairs={{0,6},{1,7},{2,4},{3,5},{4,2},{5,3},{6,0},{7,1},{8,14},{9,15},{10,... | collective-permute-start | bytes 786440 | tf_op jit(solution)/shard_map/ppermute | solution.py:34
  79.7 2.1 %grads.5.refs_0_.refs_3_ = f32[512,512]{1,0:T(8,128)S(1)} custom-call(bf16[512,256]{1,0:T(8,128)(2,1)} %get-tuple-element.36.refs_0_, s32[1]{0:T(128)} %bitcast.refs_0_.refs_1_, bf16[256,1024]{1,0:T(8,128)(2,1)S(1)} %copy-done.16, bf16[256,1024]{1,0:T(8,128)(2,1)S(1)} %copy-done.11, bf16[256,1024]{1,0:T(8,128)(2,1)} %collective-permute-done.4.refs_4_.refs_3_, ...), custom_call_target="tpu_custom_call" | custom-call | flops 99999997952 | bytes 3145732 | tf_op jit(solution)/shard_map/grads/pallas_call | solution.py:56
  81.9 0.0 copy-start.5
  81.9 0.0 copy-start.6
  81.9 1.2 outer.1.refs_5_.refs_8_
  83.1 4.1 %collective-permute-done.11.refs_1_ = bf16[512,256]{1,0:T(8,128)(2,1)} collective-permute-done((bf16[512,256]{1,0:T(8,128)(2,1)}, bf16[512,256]{1,0:T(8,128)(2,1)}, u32[]{:S(2)}, u32[]{:S(2)}) %collective-permute-start.11) | collective-permute-done | bytes 262176 | tf_op jit(solution)/shard_map/ppermute | solution.py:34
  87.2 1.2 copy-done.14
  88.4 1.6 first_update.2
  90.0 0.0 copy-start.8
  90.0 0.3 collective-permute-start.13
  90.4 2.3 %collective-permute-done.12.refs_4_ = bf16[512,256]{1,0:T(8,128)(2,1)} collective-permute-done((bf16[512,256]{1,0:T(8,128)(2,1)}, bf16[512,256]{1,0:T(8,128)(2,1)}, u32[]{:S(2)}, u32[]{:S(2)}) %collective-permute-start.12) | collective-permute-done | bytes 262176 | tf_op jit(solution)/shard_map/ppermute | solution.py:34
  92.6 1.6 first_update.3
  94.2 0.3 collective-permute-start.15
  94.5 2.6 %collective-permute-done.3.refs_5_.refs_4_ = bf16[256,1024]{1,0:T(8,128)(2,1)} collective-permute-done((bf16[256,1024]{1,0:T(8,128)(2,1)}, bf16[256,1024]{1,0:T(8,128)(2,1)}, u32[]{:S(2)}, u32[]{:S(2)}) %collective-permute-start.3) | collective-permute-done | bytes 524320 | tf_op jit(solution)/shard_map/ppermute | solution.py:34
  97.1 24.7 %collective-permute-done.13.refs_8_ = bf16[512,256]{1,0:T(8,128)(2,1)S(1)} collective-permute-done((bf16[512,256]{1,0:T(8,128)(2,1)S(1)}, bf16[512,256]{1,0:T(8,128)(2,1)S(1)}, u32[]{:S(2)}, u32[]{:S(2)}) %collective-permute-start.13) | collective-permute-done | bytes 262176 | tf_op jit(solution)/shard_map/ppermute | solution.py:34
  121.8 2.3 %keys.4 = (f32[1024,128]{1,0:T(8,128)S(1)}, f32[1024,128]{1,0:T(8,128)S(1)}) custom-call(bf16[512,256]{1,0:T(8,128)(2,1)S(1)} %get-tuple-element.39.refs_0_.refs_7_.refs_2_, s32[1]{0:T(128)} %bitcast.refs_0_.refs_1_, bf16[256,1024]{1,0:T(8,128)(2,1)S(1)} %copy-done.18, bf16[256,1024]{1,0:T(8,128)(2,1)} %collective-permute-done.1.refs_1_.refs_3_.refs_2_, ...), custom_call_target="tpu_custom_call" | custom-call | flops 99999997952 | bytes 3145732 | tf_op jit(solution)/shard_map/keys/pallas_call | solution.py:56
  124.1 0.1 collective-permute-start.14
  124.2 1.4 collective-permute-done.15.refs_8_
  125.6 2.3 %keys.5 = (f32[1024,128]{1,0:T(8,128)S(1)}, f32[1024,128]{1,0:T(8,128)S(1)}) custom-call(f32[1024,128]{1,0:T(8,128)S(1)} %get-tuple-element.40.refs_0_, s32[1]{0:T(128)} %bitcast.refs_0_.refs_1_, bf16[256,1024]{1,0:T(8,128)(2,1)S(1)} %copy-done.18, bf16[256,1024]{1,0:T(8,128)(2,1)} %collective-permute-done.1.refs_1_.refs_3_.refs_2_, ...), custom_call_target="tpu_custom_call" | custom-call | flops 99999997952 | bytes 3145732 | tf_op jit(solution)/shard_map/keys/pallas_call | solution.py:56
  127.9 0.1 collective-permute-start.16
  128.0 1.9 %collective-permute-done.16.refs_3_ = f32[1024,128]{1,0:T(8,128)S(1)} collective-permute-done((f32[1024,128]{1,0:T(8,128)S(1)}, f32[1024,128]{1,0:T(8,128)S(1)}, u32[]{:S(2)}, u32[]{:S(2)}) %collective-permute-start.16) | collective-permute-done | bytes 524320 | tf_op jit(solution)/shard_map/ppermute | solution.py:34
  129.9 0.1 core_sum.3.refs_0_
  130.0 0.1 collective-permute-start.17
  130.1 14.0 %collective-permute-done.17.refs_1_ = bf16[1024,256]{1,0:T(8,128)(2,1)S(1)} collective-permute-done((bf16[1024,256]{1,0:T(8,128)(2,1)S(1)}, bf16[1024,256]{1,0:T(8,128)(2,1)S(1)}, u32[]{:S(2)}, u32[]{:S(2)}) %collective-permute-start.17) | collective-permute-done | bytes 524320 | tf_op jit(solution)/shard_map/ppermute | solution.py:34
  144.1 0.1 residual.3.refs_5_.refs_6_
  144.2 0.1 collective-permute-start.18
  144.3 1.9 %collective-permute-done.18.refs_6_.refs_7_ = bf16[1024,256]{1,0:T(8,128)(2,1)S(1)} collective-permute-done((bf16[1024,256]{1,0:T(8,128)(2,1)S(1)}, bf16[1024,256]{1,0:T(8,128)(2,1)S(1)}, u32[]{:S(2)}, u32[]{:S(2)}) %collective-permute-start.18) | collective-permute-done | bytes 524320 | tf_op jit(solution)/shard_map/ppermute | solution.py:34
  146.2 3.0 %grads.6 = (bf16[512,256]{1,0:T(8,128)(2,1)S(1)}, bf16[512,256]{1,0:T(8,128)(2,1)}) custom-call(s32[1]{0:T(128)} %bitcast.refs_0_.refs_1_, bf16[256,1024]{1,0:T(8,128)(2,1)S(1)} %copy-done.18, bf16[256,1024]{1,0:T(8,128)(2,1)} %collective-permute-done.1.refs_1_.refs_3_.refs_2_, bf16[256,1024]{1,0:T(8,128)(2,1)} %collective-permute-done.2.refs_2_.refs_4_.refs_3_, ...), custom_call_target="tpu_custom_call" | custom-call | flops 99999997952 | bytes 3145732 | tf_op jit(solution)/shard_map/grads/pallas_call | solution.py:56
  149.1 0.3 collective-permute-start.20
  149.4 1.8 collective-permute-start.19
  151.2 2.2 %grads.7.refs_0_ = f32[512,512]{1,0:T(8,128)S(1)} custom-call(bf16[512,256]{1,0:T(8,128)(2,1)} %get-tuple-element.44.refs_0_, s32[1]{0:T(128)} %bitcast.refs_0_.refs_1_, bf16[256,1024]{1,0:T(8,128)(2,1)S(1)} %copy-done.18, bf16[256,1024]{1,0:T(8,128)(2,1)} %collective-permute-done.1.refs_1_.refs_3_.refs_2_, ...), custom_call_target="tpu_custom_call" | custom-call | flops 99999997952 | bytes 3145732 | tf_op jit(solution)/shard_map/grads/pallas_call | solution.py:56
  153.4 16.0 %collective-permute-done.20.refs_1_ = bf16[512,256]{1,0:T(8,128)(2,1)S(1)} collective-permute-done((bf16[512,256]{1,0:T(8,128)(2,1)S(1)}, bf16[512,256]{1,0:T(8,128)(2,1)S(1)}, u32[]{:S(2)}, u32[]{:S(2)}) %collective-permute-start.20) | collective-permute-done | bytes 262176 | tf_op jit(solution)/shard_map/ppermute | solution.py:34
  169.4 0.4 update.2.refs_5_
  169.9 4.6 %collective-permute-done.19.refs_1_ = bf16[512,256]{1,0:T(8,128)(2,1)} collective-permute-done((bf16[512,256]{1,0:T(8,128)(2,1)}, bf16[512,256]{1,0:T(8,128)(2,1)}, u32[]{:S(2)}, u32[]{:S(2)}) %collective-permute-start.19) | collective-permute-done | bytes 262176 | tf_op jit(solution)/shard_map/ppermute | solution.py:34
  174.5 2.2 %update.3 = bf16[1,512,512]{2,1,0:T(8,128)(2,1)} custom-call(f32[512,512]{1,0:T(8,128)S(1)} %grads.7.refs_0_, bf16[512,256]{1,0:T(8,128)(2,1)} %collective-permute-done.19.refs_1_, bf16[512,256]{1,0:T(8,128)(2,1)S(1)} %get-tuple-element.39.refs_0_.refs_7_.refs_2_, f32[512,256]{1,0:T(8,128)S(1)} %get-tuple-element.45.refs_3_, ...), custom_call_target="tpu_custom_call" | custom-call | flops 99999997952 | bytes 2883584 | tf_op jit(solution)/shard_map/update/pallas_call | solution.py:56
  (40 shorter events, 0.1 us)
Async XLA Ops:
  0.6 7.9 %copy-start.2 = (f32[1,512,512]{2,1,0:T(8,128)S(1)}, f32[1,512,512]{2,1,0:T(8,128)}, u32[]{:S(2)}) copy-start(f32[1,512,512]{2,1,0:T(8,128)} %refs_1_.3) | copy-start | bytes 3145732
  3.6 4.9 %collective-permute-start = (bf16[256,1024]{1,0:T(8,128)(2,1)}, bf16[256,1024]{1,0:T(8,128)(2,1)S(1)}, u32[]{:S(2)}, u32[]{:S(2)}) collective-permute-start(bf16[256,1024]{1,0:T(8,128)(2,1)} %get-tuple-element.26), channel_id=1, source_target_pairs={{0,1},{1,0},{2,3},{3,2},{4,5},{5,4},{6,7},{7,6},{8,9},{9,8},{10,11... | collective-permute-start | bytes 1572872 | tf_op jit(solution)/shard_map/ppermute | solution.py:34
  3.7 26.1 %collective-permute-start.6 = (bf16[1,512,512]{2,1,0:T(8,128)(2,1)}, bf16[1,512,512]{2,1,0:T(8,128)(2,1)}, u32[]{:S(2)}, u32[]{:S(2)}) collective-permute-start(bf16[1,512,512]{2,1,0:T(8,128)(2,1)} %refs_5_.1), channel_id=1, source_target_pairs={{0,6},{1,7},{2,4},{3,5},{4,2},{5,3},{6,0},{7,1},{8,14},{9,15},{10,... | collective-permute-start | bytes 1572872 | tf_op jit(solution)/shard_map/ppermute | solution.py:34
  5.8 27.1 %collective-permute-start.4 = (bf16[256,1024]{1,0:T(8,128)(2,1)}, bf16[256,1024]{1,0:T(8,128)(2,1)}, u32[]{:S(2)}, u32[]{:S(2)}) collective-permute-start(bf16[256,1024]{1,0:T(8,128)(2,1)} %get-tuple-element.32), channel_id=1, source_target_pairs={{0,2},{1,3},{2,0},{3,1},{4,6},{5,7},{6,4},{7,5},{8,10},{9,11},{10,... | collective-permute-start | bytes 1572872 | tf_op jit(solution)/shard_map/ppermute | solution.py:34
  8.6 34.6 %collective-permute-start.5 = (bf16[256,1024]{1,0:T(8,128)(2,1)}, bf16[256,1024]{1,0:T(8,128)(2,1)}, u32[]{:S(2)}, u32[]{:S(2)}) collective-permute-start(bf16[256,1024]{1,0:T(8,128)(2,1)} %get-tuple-element.33), channel_id=1, source_target_pairs={{0,3},{1,2},{2,1},{3,0},{4,7},{5,6},{6,5},{7,4},{8,11},{9,10},{10,... | collective-permute-start | bytes 1572872 | tf_op jit(solution)/shard_map/ppermute | solution.py:34
  9.4 0.8 copy-start.9
  10.3 18.0 %all-to-all-start = ((bf16[16,32,512]{2,1,0:T(8,128)(2,1)}), bf16[16,32,512]{2,1,0:T(8,128)(2,1)S(1)}, u32[]{:S(2)}, u32[]{:S(2)}) async-start(bf16[16,32,512]{2,1,0:T(8,128)(2,1)} %cast.1.refs_0_), calls=%async_computation | async-start | bytes 1048576 | tf_op jit(solution)/shard_map/all_to_all | solution.py:302
  28.2 1.0 copy-start.17
  29.3 13.9 %copy-start.7 = (bf16[2,1,256,512]{3,2,1,0:T(8,128)(2,1)S(1)}, bf16[2,1,256,512]{3,2,1,0:T(8,128)(2,1)}, u32[]{:S(2)}) copy-start(bf16[2,1,256,512]{3,2,1,0:T(8,128)(2,1)} %refs_6_.7) | copy-start | bytes 1572868
  29.3 13.9 %copy-start.10 = (bf16[256,1024]{1,0:T(8,128)(2,1)S(1)}, bf16[256,1024]{1,0:T(8,128)(2,1)}, u32[]{:S(2)}) copy-start(bf16[256,1024]{1,0:T(8,128)(2,1)} %copy-done.9) | copy-start | bytes 1572868
  29.3 13.9 %copy-start.15 = (bf16[256,1024]{1,0:T(8,128)(2,1)S(1)}, bf16[256,1024]{1,0:T(8,128)(2,1)}, u32[]{:S(2)}) copy-start(bf16[256,1024]{1,0:T(8,128)(2,1)} %get-tuple-element.31.refs_2_.refs_1_) | copy-start | bytes 1572868
  46.4 4.9 %collective-permute-start.7 = (f32[1024,256]{1,0:T(8,128)S(1)}, f32[1024,256]{1,0:T(8,128)S(1)}, u32[]{:S(2)}, u32[]{:S(2)}) collective-permute-start(f32[1024,256]{1,0:T(8,128)S(1)} %get-tuple-element.35), channel_id=1, source_target_pairs={{0,1},{1,0},{2,3},{3,2},{4,5},{5,4},{6,7},{7,6},{8,9},{9,8},{10,11... | collective-permute-start | bytes 3145736 | tf_op jit(solution)/shard_map/ppermute | solution.py:34
  46.8 8.4 %collective-permute-start.8 = (bf16[32,512]{1,0:T(8,128)(2,1)S(1)}, bf16[32,512]{1,0:T(8,128)(2,1)S(1)}, u32[]{:S(2)}, u32[]{:S(2)}) collective-permute-start(bf16[32,512]{1,0:T(8,128)(2,1)S(1)} %sum.1.refs_0_.refs_1_), channel_id=1, source_target_pairs={{0,32},{8,40},{16,48},{24,56},{32,0},{40,8},{48,16},{56,24},{64,96... | collective-permute-start | bytes 98312 | tf_op jit(solution)/shard_map/ppermute | solution.py:34
  51.4 20.0 %collective-permute-start.9 = (bf16[1024,256]{1,0:T(8,128)(2,1)S(1)}, bf16[1024,256]{1,0:T(8,128)(2,1)S(1)}, u32[]{:S(2)}, u32[]{:S(2)}) collective-permute-start(bf16[1024,256]{1,0:T(8,128)(2,1)S(1)} %core_sum.2.refs_0_.refs_1_), channel_id=1, source_target_pairs={{0,2},{1,3},{2,0},{3,1},{4,6},{5,7},{6,4},{7,5},{8,10},{9,11},{10,... | collective-permute-start | bytes 1572872 | tf_op jit(solution)/shard_map/ppermute | solution.py:34
  71.4 0.8 copy-start
  71.4 3.4 %copy-start.16 = (bf16[256,1024]{1,0:T(8,128)(2,1)S(1)}, bf16[256,1024]{1,0:T(8,128)(2,1)}, u32[]{:S(2)}) copy-start(bf16[256,1024]{1,0:T(8,128)(2,1)} %get-tuple-element.31.refs_2_.refs_1_) | copy-start | bytes 1572868
  72.2 2.6 %collective-permute-start.10 = (bf16[1024,256]{1,0:T(8,128)(2,1)S(1)}, bf16[1024,256]{1,0:T(8,128)(2,1)S(1)}, u32[]{:S(2)}, u32[]{:S(2)}) collective-permute-start(bf16[1024,256]{1,0:T(8,128)(2,1)S(1)} %residual.2.refs_5_.refs_6_), channel_id=1, source_target_pairs={{0,1},{1,0},{2,3},{3,2},{4,5},{5,4},{6,7},{7,6},{8,9},{9,8},{10,11... | collective-permute-start | bytes 1572872 | tf_op jit(solution)/shard_map/ppermute | solution.py:34
  72.2 18.2 %collective-permute-start.1 = (bf16[256,1024]{1,0:T(8,128)(2,1)}, bf16[256,1024]{1,0:T(8,128)(2,1)}, u32[]{:S(2)}, u32[]{:S(2)}) collective-permute-start(bf16[256,1024]{1,0:T(8,128)(2,1)} %get-tuple-element.28), channel_id=1, source_target_pairs={{0,1},{1,0},{2,3},{3,2},{4,5},{5,4},{6,7},{7,6},{8,9},{9,8},{10,11... | collective-permute-start | bytes 1572872 | tf_op jit(solution)/shard_map/ppermute | solution.py:34
  72.7 17.6 %collective-permute-start.2 = (bf16[256,1024]{1,0:T(8,128)(2,1)}, bf16[256,1024]{1,0:T(8,128)(2,1)}, u32[]{:S(2)}, u32[]{:S(2)}) collective-permute-start(bf16[256,1024]{1,0:T(8,128)(2,1)} %get-tuple-element.29), channel_id=1, source_target_pairs={{0,2},{1,3},{2,0},{3,1},{4,6},{5,7},{6,4},{7,5},{8,10},{9,11},{10,... | collective-permute-start | bytes 1572872 | tf_op jit(solution)/shard_map/ppermute | solution.py:34
  73.4 6.3 %copy-start.11 = (bf16[256,1024]{1,0:T(8,128)(2,1)S(1)}, bf16[256,1024]{1,0:T(8,128)(2,1)}, u32[]{:S(2)}) copy-start(bf16[256,1024]{1,0:T(8,128)(2,1)} %copy-done.9) | copy-start | bytes 1572868
  73.4 23.7 %collective-permute-start.3 = (bf16[256,1024]{1,0:T(8,128)(2,1)}, bf16[256,1024]{1,0:T(8,128)(2,1)}, u32[]{:S(2)}, u32[]{:S(2)}) collective-permute-start(bf16[256,1024]{1,0:T(8,128)(2,1)} %get-tuple-element.30), channel_id=1, source_target_pairs={{0,3},{1,2},{2,1},{3,0},{4,7},{5,6},{6,5},{7,4},{8,11},{9,10},{10,... | collective-permute-start | bytes 1572872 | tf_op jit(solution)/shard_map/ppermute | solution.py:34
  77.7 9.5 %collective-permute-start.11 = (bf16[512,256]{1,0:T(8,128)(2,1)}, bf16[512,256]{1,0:T(8,128)(2,1)}, u32[]{:S(2)}, u32[]{:S(2)}) collective-permute-start(bf16[512,256]{1,0:T(8,128)(2,1)} %get-tuple-element.37), channel_id=1, source_target_pairs={{0,6},{1,7},{2,4},{3,5},{4,2},{5,3},{6,0},{7,1},{8,14},{9,15},{10,... | collective-permute-start | bytes 786440 | tf_op jit(solution)/shard_map/ppermute | solution.py:34
  78.0 3.9 %copy-start.1 = (bf16[16,32,512]{2,1,0:T(8,128)(2,1)S(1)}, bf16[16,32,512]{2,1,0:T(8,128)(2,1)}, u32[]{:S(2)}) copy-start(bf16[16,32,512]{2,1,0:T(8,128)(2,1)} %copy-done) | copy-start | bytes 1572868
  78.0 3.9 %copy-start.3 = (f32[512,512]{1,0:T(8,128)S(1)}, f32[512,512]{1,0:T(8,128)}, u32[]{:S(2)}) copy-start(f32[512,512]{1,0:T(8,128)} %refs_2_.4) | copy-start | bytes 3145732
  78.0 3.9 %copy-start.4 = (f32[512,512]{1,0:T(8,128)S(1)}, f32[512,512]{1,0:T(8,128)}, u32[]{:S(2)}) copy-start(f32[512,512]{1,0:T(8,128)} %refs_3_.2) | copy-start | bytes 3145732
  78.0 14.6 %collective-permute-start.12 = (bf16[512,256]{1,0:T(8,128)(2,1)}, bf16[512,256]{1,0:T(8,128)(2,1)}, u32[]{:S(2)}, u32[]{:S(2)}) collective-permute-start(bf16[512,256]{1,0:T(8,128)(2,1)} %get-tuple-element.36.refs_0_), channel_id=1, source_target_pairs={{0,6},{1,7},{2,4},{3,5},{4,2},{5,3},{6,0},{7,1},{8,14},{9,15},{10,... | collective-permute-start | bytes 786440 | tf_op jit(solution)/shard_map/ppermute | solution.py:34
  81.9 5.3 %copy-start.5 = (f32[1,512,512]{2,1,0:T(8,128)S(1)}, f32[1,512,512]{2,1,0:T(8,128)}, u32[]{:S(2)}) copy-start(f32[1,512,512]{2,1,0:T(8,128)} %refs_6_.5) | copy-start | bytes 3145732
  81.9 5.3 %copy-start.6 = (f32[1,512,512]{2,1,0:T(8,128)S(1)}, f32[1,512,512]{2,1,0:T(8,128)}, u32[]{:S(2)}) copy-start(f32[1,512,512]{2,1,0:T(8,128)} %refs_7_.3) | copy-start | bytes 3145732
  87.2 1.2 copy-start.14
  90.0 31.8 %copy-start.12 = (bf16[512,256]{1,0:T(8,128)(2,1)}, bf16[512,256]{1,0:T(8,128)(2,1)S(1)}, u32[]{:S(2)}) copy-start(bf16[512,256]{1,0:T(8,128)(2,1)S(1)} %get-tuple-element.38.refs_0_.refs_7_.refs_2_) | copy-start | bytes 786436
  90.0 31.8 %copy-start.8 = (bf16[2,1,256,512]{3,2,1,0:T(8,128)(2,1)S(1)}, bf16[2,1,256,512]{3,2,1,0:T(8,128)(2,1)}, u32[]{:S(2)}) copy-start(bf16[2,1,256,512]{3,2,1,0:T(8,128)(2,1)} %refs_6_.7) | copy-start | bytes 1572868
  90.0 31.8 %copy-start.18 = (bf16[256,1024]{1,0:T(8,128)(2,1)S(1)}, bf16[256,1024]{1,0:T(8,128)(2,1)}, u32[]{:S(2)}) copy-start(bf16[256,1024]{1,0:T(8,128)(2,1)} %get-tuple-element.27.refs_0_.refs_2_.refs_1_) | copy-start | bytes 1572868
  90.0 31.8 %collective-permute-start.13 = (bf16[512,256]{1,0:T(8,128)(2,1)S(1)}, bf16[512,256]{1,0:T(8,128)(2,1)S(1)}, u32[]{:S(2)}, u32[]{:S(2)}) collective-permute-start(bf16[512,256]{1,0:T(8,128)(2,1)S(1)} %get-tuple-element.38.refs_0_.refs_7_.refs_2_), channel_id=1, source_target_pairs={{0,6},{1,7},{2,4},{3,5},{4,2},{5,3},{6,0},{7,1},{8,14},{9,15},{10,... | collective-permute-start | bytes 786440 | tf_op jit(solution)/shard_map/ppermute | solution.py:34
  94.2 31.4 %collective-permute-start.15 = (bf16[512,256]{1,0:T(8,128)(2,1)S(1)}, bf16[512,256]{1,0:T(8,128)(2,1)S(1)}, u32[]{:S(2)}, u32[]{:S(2)}) collective-permute-start(bf16[512,256]{1,0:T(8,128)(2,1)S(1)} %get-tuple-element.39.refs_0_.refs_7_.refs_2_), channel_id=1, source_target_pairs={{0,6},{1,7},{2,4},{3,5},{4,2},{5,3},{6,0},{7,1},{8,14},{9,15},{10,... | collective-permute-start | bytes 786440 | tf_op jit(solution)/shard_map/ppermute | solution.py:34
  124.1 3.9 %collective-permute-start.14 = (f32[1024,128]{1,0:T(8,128)S(1)}, f32[1024,128]{1,0:T(8,128)S(1)}, u32[]{:S(2)}, u32[]{:S(2)}) collective-permute-start(f32[1024,128]{1,0:T(8,128)S(1)} %get-tuple-element.41), channel_id=1, source_target_pairs={{0,1},{1,0},{2,3},{3,2},{4,5},{5,4},{6,7},{7,6},{8,9},{9,8},{10,11... | collective-permute-start | bytes 1572872 | tf_op jit(solution)/shard_map/ppermute | solution.py:34
  127.9 2.0 %collective-permute-start.16 = (f32[1024,128]{1,0:T(8,128)S(1)}, f32[1024,128]{1,0:T(8,128)S(1)}, u32[]{:S(2)}, u32[]{:S(2)}) collective-permute-start(f32[1024,128]{1,0:T(8,128)S(1)} %get-tuple-element.43), channel_id=1, source_target_pairs={{0,1},{1,0},{2,3},{3,2},{4,5},{5,4},{6,7},{7,6},{8,9},{9,8},{10,11... | collective-permute-start | bytes 1572872 | tf_op jit(solution)/shard_map/ppermute | solution.py:34
  130.0 14.1 %collective-permute-start.17 = (bf16[1024,256]{1,0:T(8,128)(2,1)S(1)}, bf16[1024,256]{1,0:T(8,128)(2,1)S(1)}, u32[]{:S(2)}, u32[]{:S(2)}) collective-permute-start(bf16[1024,256]{1,0:T(8,128)(2,1)S(1)} %core_sum.3.refs_0_), channel_id=1, source_target_pairs={{0,2},{1,3},{2,0},{3,1},{4,6},{5,7},{6,4},{7,5},{8,10},{9,11},{10,... | collective-permute-start | bytes 1572872 | tf_op jit(solution)/shard_map/ppermute | solution.py:34
  144.2 2.0 %collective-permute-start.18 = (bf16[1024,256]{1,0:T(8,128)(2,1)S(1)}, bf16[1024,256]{1,0:T(8,128)(2,1)S(1)}, u32[]{:S(2)}, u32[]{:S(2)}) collective-permute-start(bf16[1024,256]{1,0:T(8,128)(2,1)S(1)} %residual.3.refs_5_.refs_6_), channel_id=1, source_target_pairs={{0,1},{1,0},{2,3},{3,2},{4,5},{5,4},{6,7},{7,6},{8,9},{9,8},{10,11... | collective-permute-start | bytes 1572872 | tf_op jit(solution)/shard_map/ppermute | solution.py:34
  149.1 20.3 %collective-permute-start.20 = (bf16[512,256]{1,0:T(8,128)(2,1)S(1)}, bf16[512,256]{1,0:T(8,128)(2,1)S(1)}, u32[]{:S(2)}, u32[]{:S(2)}) collective-permute-start(bf16[512,256]{1,0:T(8,128)(2,1)S(1)} %get-tuple-element.47), channel_id=1, source_target_pairs={{0,6},{1,7},{2,4},{3,5},{4,2},{5,3},{6,0},{7,1},{8,14},{9,15},{10,... | collective-permute-start | bytes 786440 | tf_op jit(solution)/shard_map/ppermute | solution.py:34
  149.4 20.0 %copy-start.13 = (bf16[512,256]{1,0:T(8,128)(2,1)S(1)}, bf16[512,256]{1,0:T(8,128)(2,1)}, u32[]{:S(2)}) copy-start(bf16[512,256]{1,0:T(8,128)(2,1)} %copy-done.12) | copy-start | bytes 786436
  149.4 25.0 %collective-permute-start.19 = (bf16[512,256]{1,0:T(8,128)(2,1)}, bf16[512,256]{1,0:T(8,128)(2,1)}, u32[]{:S(2)}, u32[]{:S(2)}) collective-permute-start(bf16[512,256]{1,0:T(8,128)(2,1)} %get-tuple-element.44.refs_0_), channel_id=1, source_target_pairs={{0,6},{1,7},{2,4},{3,5},{4,2},{5,3},{6,0},{7,1},{8,14},{9,15},{10,... | collective-permute-start | bytes 786440 | tf_op jit(solution)/shard_map/ppermute | solution.py:34

commit v3 on v2

--- a/solution.py
+++ b/solution.py
@@ -86,18 +86,18 @@
         copy.wait()
 
 
-def keys_kernel(scale, place, *refs):
-    feats, chunks, (kept, sent, whole) = refs[:4], refs[4:-3], refs[-3:]
+def keys_kernel(scale, count, own_first, place, *refs):
+    feats, chunks, (kept, sent, whole) = refs[:count], refs[count:-3], refs[-3:]
     rows = feats[0].shape[0]
     core = place[0] % 2
     for k in range(len(chunks) // 3):
         aims, own, far = chunks[3 * k : 3 * k + 3]
         depth, cols = own.shape[0], own.shape[1] // 2
-        for g in range(4):
+        for g in range(count):
             part = jnp.dot(feats[g][:, :depth], own[...], preferred_element_type=F32)
             part += jnp.dot(feats[g][:, depth:], far[...], preferred_element_type=F32)
             part *= scale
-            if g == 0:
+            if g == 0 and own_first:
                 part -= aims[...].astype(F32)
             whole[...] = part
             for half, out in ((1 - core, sent), (core, kept)):
@@ -105,29 +105,39 @@
                 out[g * rows : (g + 1) * rows, k * cols : (k + 1) * cols] = whole[:, columns]
 
 
-def core_sum_kernel(*refs):
+def core_sum_kernel(rows, *refs):
     pairs, out = refs[:-1], refs[-1]
-    rows = out.shape[0] // 4
     cols = pairs[0].shape[1]
     for k in range(len(pairs) // 2):
         kept, other = pairs[2 * k : 2 * k + 2]
-        for g in range(4):
+        for g in range(out.shape[0] // rows):
             here, there = g * rows, (g ^ 1) * rows
             total = kept[here : here + rows] + other[there : there + rows]
             out[here : here + rows, k * cols : (k + 1) * cols] = total.astype(BF)
 
 
-def residual_kernel(part, other, out):
-    rows = out.shape[0] // 4
-    for g in range(4):
-        here, there = g * rows, (g ^ 2) * rows
-        total = part[here : here + rows].astype(F32) + other[there : there + rows].astype(F32)
-        out[here : here + rows] = total.astype(BF)
-
-
-def grads_kernel(shard, place, *refs):
-    feats, (mine, other), outs, whole = refs[:4], refs[4:6], refs[6:-1], refs[-1]
+def turn_kernel(*refs):
+    feats, outs = refs[:4], refs[4:]
     rows, depth = feats[0].shape[0], outs[0].shape[0]
+    for j, out in enumerate(outs):
+        for g in range(4):
+            out[:, g * rows : (g + 1) * rows] = feats[g][:, j * depth : (j + 1) * depth].T
+
+
+def residual_kernel(*refs):
+    ours, theirs, out = refs[: len(refs) // 2], refs[len(refs) // 2 : -1], refs[-1]
+    half = out.shape[0] // 2
+    if len(ours) == 1:
+        ours = (ours[0].at[:half], ours[0].at[half:])
+        theirs = (theirs[0].at[:half], theirs[0].at[half:])
+    for i in range(2):
+        total = ours[i][...].astype(F32) + theirs[1 - i][...].astype(F32)
+        out[i * half : (i + 1) * half] = total.astype(BF)
+
+
+def grads_kernel(place, feats, mine, other, *refs):
+    outs, whole = refs[:-1], refs[-1]
+    rows = mine.shape[0] // 4
     core = place[0] % 2
     cols = mine.shape[1] // CHUNKS
     for k in range(CHUNKS):
@@ -137,20 +147,11 @@
             for g in range(4):
                 there = (g ^ flip) * rows
                 whole[g * rows : (g + 1) * rows, columns] = residual[there : there + rows, part]
-    at = slice(shard * depth, (shard + 1) * depth)
-    dims = (((0,), (0,)), ((), ()))
-    total = None
-    for g in range(4):
-        term = lax.dot_general(
-            feats[g][:, at],
-            whole[g * rows : (g + 1) * rows],
-            dims,
-            preferred_element_type=F32,
-        )
-        total = term if total is None else total + term
     cols = outs[0].shape[1]
     for k, out in enumerate(outs):
-        out[...] = total[:, k * cols : (k + 1) * cols].astype(out.dtype)
+        part = whole[:, k * cols : (k + 1) * cols]
+        grad = jnp.dot(feats[...], part, preferred_element_type=F32)
+        out[...] = grad.astype(out.dtype)
 
 
 def cast_kernel(drift, out):
@@ -181,11 +182,30 @@
     return one, two, updated
 
 
-def first_update_kernel(factor, kept, far, own, one, two, outer, new, new_one, new_two):
-    first, second, updated = adam(factor, kept[...], far[...], own[...], one[...], two[...])
-    new_one[...] = first
-    new_two[...] = second
-    new[...] = (mix_share * updated + (1.0 - mix_share) * outer[...]).astype(BF)
+def outer_update(mean_drift, global_weights, outer_moment):
+    mean_drift = mean_drift.astype(F32)
+    new_moment = outer_beta * outer_moment + mean_drift
+    return global_weights - outer_rate * (mean_drift + outer_beta * new_moment)
+
+
+def outer_kernel(pieces, global_weights, outer_moment, out):
+    share, rows = pieces.shape[0], pieces.shape[1]
+    for i in range(share):
+        at = slice(i * rows, (i + 1) * rows)
+        out[at] = outer_update(pieces[i], global_weights[at], outer_moment[at])
+
+
+def first_update_kernel(
+    factor, kept, far, own, one, two, pieces, global_weights, outer_moment, new, new_one, new_two
+):
+    share, rows = pieces.shape[0], pieces.shape[1]
+    for i in range(share):
+        at = slice(i * rows, (i + 1) * rows)
+        first, second, updated = adam(factor, kept[at], far[at], own[at], one[at], two[at])
+        outer = outer_update(pieces[i], global_weights[at], outer_moment[at])
+        new_one[at] = first
+        new_two[at] = second
+        new[at] = (mix_share * updated + (1.0 - mix_share) * outer).astype(BF)
 
 
 def update_kernel(factor, kept, far, own, one, two, *rest):
@@ -198,15 +218,6 @@
         out[0, :, len(done) * cols :] = updated.astype(BF)
     else:
         out[...] = updated.astype(BF)
-
-
-def outer_kernel(pieces, global_weights, outer_moment, out):
-    share, rows = pieces.shape[0], pieces.shape[1]
-    for i in range(share):
-        at = slice(i * rows, (i + 1) * rows)
-        mean_drift = pieces[i].astype(F32)
-        new_moment = outer_beta * outer_moment[at] + mean_drift
-        out[at] = global_weights[at] - outer_rate * (mean_drift + outer_beta * new_moment)
 
 
 def per_device(
@@ -240,49 +251,61 @@
         height = tok_rows if len(lead) > 1 else rows
         return pl.BlockSpec((None,) * len(lead) + (height, wide), lambda i: at)
 
-    def keys(step, feats, chunks, own, far, gates):
+    def keys(step, groups, feats, chunks, own, far, gates):
         views, specs = [], []
         for k in chunks:
             views += [targets, own, far]
             specs += [chunk((step, 0), k)] + ([chunk((0,), k)] if step == 0 else [FULL]) * 2
-        return call(
-            functools.partial(keys_kernel, scale),
-            [shaped((4 * tok_rows, len(chunks) * cols), F32)] * 2,
-            [place, *feats, *views],
-            gates,
-            [SCALAR] + [FULL] * 4 + specs,
+        count = len(groups)
+        return call(
+            functools.partial(keys_kernel, scale, count, groups[0] == 0),
+            [shaped((count * tok_rows, len(chunks) * cols), F32)] * 2,
+            [place, *[feats[g] for g in groups], *views],
+            gates,
+            [SCALAR] + [FULL] * count + specs,
             scratch=[pltpu.VMEM((tok_rows, wide), F32)],
         )
+
+    def turn(feats, gates):
+        return call(turn_kernel, [shaped((rows, 4 * tok_rows), BF)] * 2, feats, gates)
 
     def core_sum(pairs, gates):
         blocks = []
         for kept, sent in pairs:
             blocks += [kept, pair_swap(sent, 1)]
+        height = pairs[0][0].shape[0]
+        return call(
+            functools.partial(core_sum_kernel, tok_rows),
+            shaped((height, columns // 2), BF),
+            blocks,
+            gates,
+        )
+
+    def residuals(ours, theirs, gates):
         out = shaped((4 * tok_rows, columns // 2), BF)
-        return call(core_sum_kernel, out, blocks, gates)
-
-    def residuals(part, gates):
-        return call(residual_kernel, shaped(part.shape, BF), [part, pair_swap(part, 2)], gates)
-
-    def grads(shard, dtype, parts, feats, mine, other, gates):
-        return call(
-            functools.partial(grads_kernel, shard),
+        return call(residual_kernel, out, [*ours, *theirs], gates)
+
+    def grads(dtype, parts, feats, mine, other, gates):
+        return call(
+            grads_kernel,
             [shaped((rows, columns // parts), dtype)] * parts,
-            [place, *feats, mine, other],
-            gates,
-            [SCALAR] + [FULL] * 6,
+            [place, feats, mine, other],
+            gates,
+            [SCALAR] + [FULL] * 3,
             scratch=[pltpu.VMEM((4 * tok_rows, columns), BF)],
         )
 
     def first_update(k, kept, far, gates):
         state = chunk((0,), k)
+        outer = chunk((), k)
         block = shaped((rows, wide), F32)
+        pieces = pl.BlockSpec((share, rows_of, wide), lambda i: (0, 0, k))
         return call(
             functools.partial(first_update_kernel, factor),
             [shaped((rows, wide), BF), block, block],
-            [kept, far, weights, first_moment, second_moment, global_out],
-            gates,
-            [chunk((), k), FULL, state, state, state, chunk((), k)],
+            [kept, far, weights, first_moment, second_moment, means, global_weights, outer_moment],
+            gates,
+            [outer, FULL, state, state, state, pieces, outer, outer],
         )
 
     def update(k, kept, far, own, one, two, done, gates):
@@ -300,44 +323,52 @@
     rows_of = rows // share
     casted = call(cast_kernel, shaped((share, rows_of, columns), BF), [drift], [feats[1]])
     pieces = lax.all_to_all(casted, "rep", 0, 0, axis_index_groups=groups)
-    packs = prepare(1, (0, 1, 2, 3), [casted])
-    summed = call(sum_kernel, shaped((rows_of, columns), BF), [pieces], [packs[0]])
+    (keep,) = prepare(1, (0,), [casted])
+    summed = call(sum_kernel, shaped((rows_of, columns), BF), [pieces], [keep])
     summed_other = swap(summed, "rep", lambda i: i ^ 4)
 
-    both = keys(0, feats, (0, 1), weights, far, [summed])
-    part = core_sum([both], [])
+    near_keys = keys(0, (0, 1), feats, (0, 1), weights, far, [summed])
+    pair_keys = keys(0, (2, 3), feats, (0, 1), weights, far, [near_keys[0]])
+    near_part = core_sum([near_keys], [])
+    near_other = pair_swap(near_part, 2)
+    pair_part = core_sum([pair_keys], [near_part])
+    pair_other = pair_swap(pair_part, 2)
+    own_t, far_t = turn(feats, [pair_part, summed_other, near_other])
+    mine = residuals([near_part, pair_part], [near_other, pair_other], [far_t])
+    other = pair_swap(mine, 1)
+    across_a, across_b = grads(BF, CHUNKS, far_t, mine, other, [])
+    far_a, far_b = far_swap(across_a), far_swap(across_b)
+    (kept,) = grads(F32, 1, own_t, mine, other, [across_b])
     copies = call(
         functools.partial(mean_kernel, replicas),
         shaped((share, rows_of, columns), BF),
         [summed, summed_other],
-        [part],
+        [kept],
     )
     means = lax.all_to_all(copies, "rep", 0, 0, axis_index_groups=groups)
-    mine = residuals(part, [means])
+    packs = prepare(1, (1, 2, 3), [copies])
+    later = [keep] + [pair_swap(packs[g - 1], g) for g in (1, 2, 3)]
+    own_a, one_a, two_a = first_update(0, kept, far_a, [packs[0]])
+    gather_a = far_swap(own_a)
+    own_b, one_b, two_b = first_update(1, kept, far_b, [own_a, *later[1:3]])
+    gather_b = far_swap(own_b)
+
+    every = (0, 1, 2, 3)
+    keys_a = keys(1, every, later, (0,), own_a, gather_a, [own_b])
+    keys_b = keys(1, every, later, (1,), own_b, gather_b, [keys_a[0]])
+    part = core_sum([keys_a, keys_b], [])
+    own_t, far_t = turn(later, [part])
+    mine = residuals([part], [pair_swap(part, 2)], [far_t])
     other = pair_swap(mine, 1)
-    across_a, across_b = grads(1, BF, CHUNKS, feats, mine, other, [])
+    across_a, across_b = grads(BF, CHUNKS, far_t, mine, other, [])
     far_a, far_b = far_swap(across_a), far_swap(across_b)
-    later = [packs[0]] + [pair_swap(packs[g], g) for g in (1, 2, 3)]
-    (kept,) = grads(0, F32, 1, feats, mine, other, [across_b])
+    (kept,) = grads(F32, 1, own_t, mine, other, [across_b])
     global_out = call(
         outer_kernel,
         shaped((rows, columns), F32),
         [means, global_weights, outer_moment],
         [kept],
     )
-    own_a, one_a, two_a = first_update(0, kept, far_a, [])
-    gather_a = far_swap(own_a)
-    own_b, one_b, two_b = first_update(1, kept, far_b, [own_a, *later[1:3]])
-    gather_b = far_swap(own_b)
-
-    keys_a = keys(1, later, (0,), own_a, gather_a, [own_b])
-    keys_b = keys(1, later, (1,), own_b, gather_b, [keys_a[0]])
-    part = core_sum([keys_a, keys_b], [])
-    mine = residuals(part, [])
-    other = pair_swap(mine, 1)
-    across_a, across_b = grads(1, BF, CHUNKS, later, mine, other, [])
-    far_a, far_b = far_swap(across_a), far_swap(across_b)
-    (kept,) = grads(0, F32, 1, later, mine, other, [across_b])
     done_a = update(0, kept, far_a, own_a, one_a, two_a, [], [])
     weights_out = update(1, kept, far_b, own_b, one_b, two_b, [done_a], [])
     return (weights_out, global_out)

time: 178 us -> 169 us (0.949)
  blocking collectives: 16.1 us -> 0 us
  waiting for transfers between devices: 97.5 us -> 84.8 us
  starting transfers between devices: 26 us -> 37.5 us
  local copies, waits for them, and re-layouts: 3.82 us -> 8.26 us
  Pallas kernels: 32.4 us -> 36.8 us
    all_to_all x1 -> x0, blocking collectives: 16.1 us -> none  [per_device(): means = lax.all_to_all(copies, 'rep', 0, 0, axis_index_groups=groups)]
    ppermute x21 -> x23, waiting for transfers between devices: 89.9 us -> 74 us  [swap(): return lax.ppermute(value, axis, pairs)]
    all_to_all x0 -> x1, starting transfers between devices: none -> 7.48 us  [per_device(): means = lax.all_to_all(copies, 'rep', 0, 0, axis_index_groups=groups)]
    unnamed x38 -> x36, local copies, waits for them, and re-layouts: 3.82 us -> 8.26 us
    pallas_call x21 -> x26, Pallas kernels: 32.4 us -> 36.8 us  [call(): pl.pallas_call(kernel, name=getattr(body, 'func', body).__name__.removesu...]
    ppermute x21 -> x23, starting transfers between devices: 18.5 us -> 22.5 us  [swap(): return lax.ppermute(value, axis, pairs)]
    all_to_all x0 -> x1, waiting for transfers between devices: none -> 2.15 us  [per_device(): means = lax.all_to_all(copies, 'rep', 0, 0, axis_index_groups=groups)]
  transfers between devices with their start and end apart: 22 -> 25, of which waited for: 16 -> 16; matrix products, arithmetic and copies ran while one was open for 0% -> 0% of each run, Pallas kernels for 12% -> 17%
where the time goes in v3:
time: 169 us; the launch traced here: 168 us
  waiting for transfers between devices  84.8 us (50%)
  starting transfers between devices  37.5 us (22%)
  Pallas kernels  36.8 us (22%)
  local copies, waits for them, and re-layouts  8.26 us (5%)
    ppermute x23, waiting for transfers between devices, swap(): return lax.ppermute(value, axis, pairs)  74 us
    pallas_call x26, Pallas kernels, call(): pl.pallas_call(kernel, name=getattr(body, 'func', body).__name__.removesu...  36.8 us
    ppermute x23, starting transfers between devices, swap(): return lax.ppermute(value, axis, pairs)  22.5 us
    all_to_all x1, waiting for transfers between devices, per_device(): pieces = lax.all_to_all(casted, 'rep', 0, 0, axis_index_groups=groups)  8.6 us
    unnamed x36, local copies, waits for them, and re-layouts  8.26 us
    all_to_all x1, starting transfers between devices, per_device(): pieces = lax.all_to_all(casted, 'rep', 0, 0, axis_index_groups=groups)  7.48 us
    all_to_all x1, starting transfers between devices, per_device(): means = lax.all_to_all(copies, 'rep', 0, 0, axis_index_groups=groups)  7.48 us
  transfers between devices with their start and end apart: 25, of which 16 were waited for; matrix products, arithmetic and copies ran while one was open for 0% of the time, Pallas kernels for 17%

profile of v3, /device:TPU:34, one launch (start us, length us, event | category | flops | bytes accessed | tf_op | source)
XLA Modules:
  0.0 168.2 jit_solution(2844036223367064077)
XLA Ops:
  0.6 3.0 %prepare.3 = (bf16[256,1024]{1,0:T(8,128)(2,1)}, bf16[256,1024]{1,0:T(8,128)(2,1)}, bf16[256,1024]{1,0:T(8,128)(2,1)}, bf16[256,1024]{1,0:T(8,128)(2,1)}) custom-call(s32[1]{0:T(128)} %bitcast.refs_0_.refs_1_, bf16[2,1,256,4096]{3,2,1,0:T(8,128)(2,1)} %refs_2_.4), custom_call_target="tpu_custom_call" | custom-call | flops 99999997952 | bytes 4194308 | tf_op jit(solution)/shard_map/prepare/pallas_call | solution.py:56
  3.7 2.0 %collective-permute-start.1 = (bf16[1,512,512]{2,1,0:T(8,128)(2,1)}, bf16[1,512,512]{2,1,0:T(8,128)(2,1)}, u32[]{:S(2)}, u32[]{:S(2)}) collective-permute-start(bf16[1,512,512]{2,1,0:T(8,128)(2,1)} %refs_5_.7), channel_id=1, source_target_pairs={{0,6},{1,7},{2,4},{3,5},{4,2},{5,3},{6,0},{7,1},{8,14},{9,15},{10,... | collective-permute-start | bytes 1572872 | tf_op jit(solution)/shard_map/ppermute | solution.py:34
  5.7 2.8 %collective-permute-start.3 = (bf16[256,1024]{1,0:T(8,128)(2,1)}, bf16[256,1024]{1,0:T(8,128)(2,1)}, u32[]{:S(2)}, u32[]{:S(2)}) collective-permute-start(bf16[256,1024]{1,0:T(8,128)(2,1)} %get-tuple-element.35), channel_id=1, source_target_pairs={{0,2},{1,3},{2,0},{3,1},{4,6},{5,7},{6,4},{7,5},{8,10},{9,11},{10,... | collective-permute-start | bytes 1572872 | tf_op jit(solution)/shard_map/ppermute | solution.py:34
  8.6 0.8 cast.1.refs_0_
  9.4 0.8 copy-done.9
  10.2 7.5 %all-to-all-start = ((bf16[16,32,512]{2,1,0:T(8,128)(2,1)}), bf16[16,32,512]{2,1,0:T(8,128)(2,1)S(1)}, u32[]{:S(2)}, u32[]{:S(2)}) async-start(bf16[16,32,512]{2,1,0:T(8,128)(2,1)} %cast.1.refs_0_), calls=%async_computation | async-start | bytes 1048576 | tf_op jit(solution)/shard_map/all_to_all | solution.py:325
  17.7 1.8 %prepare.4.refs_0_.refs_2_.refs_1_ = bf16[256,1024]{1,0:T(8,128)(2,1)} custom-call(bf16[16,32,512]{2,1,0:T(8,128)(2,1)} %cast.1.refs_0_, s32[1]{0:T(128)} %bitcast.refs_0_.refs_1_, bf16[2,1,256,4096]{3,2,1,0:T(8,128)(2,1)} %refs_2_.4), custom_call_target="tpu_custom_call" | custom-call | flops 99999997952 | bytes 4194308 | tf_op jit(solution)/shard_map/prepare/pallas_call | solution.py:56
  19.6 8.6 %all-to-all-done.refs_1_ = bf16[16,32,512]{2,1,0:T(8,128)(2,1)S(1)} async-done(((bf16[16,32,512]{2,1,0:T(8,128)(2,1)}), bf16[16,32,512]{2,1,0:T(8,128)(2,1)S(1)}, u32[]{:S(2)}, u32[]{:S(2)}) %all-to-all-start) | async-done | bytes 524320 | tf_op jit(solution)/shard_map/all_to_all | solution.py:325
  28.2 1.0 copy-done.14
  29.2 0.7 sum.1.refs_0_.refs_1_
  29.9 4.6 %collective-permute-start.6 = (bf16[32,512]{1,0:T(8,128)(2,1)}, bf16[32,512]{1,0:T(8,128)(2,1)}, u32[]{:S(2)}, u32[]{:S(2)}) collective-permute-start(bf16[32,512]{1,0:T(8,128)(2,1)} %sum.1.refs_0_.refs_1_), channel_id=1, source_target_pairs={{0,32},{8,40},{16,48},{24,56},{32,0},{40,8},{48,16},{56,24},{64,96... | collective-permute-start | bytes 98312 | tf_op jit(solution)/shard_map/ppermute | solution.py:34
  34.5 2.1 %keys.4 = (f32[512,256]{1,0:T(8,128)S(1)}, f32[512,256]{1,0:T(8,128)S(1)}) custom-call(bf16[32,512]{1,0:T(8,128)(2,1)} %sum.1.refs_0_.refs_1_, s32[1]{0:T(128)} %bitcast.refs_0_.refs_1_, bf16[256,1024]{1,0:T(8,128)(2,1)S(1)} %copy-done.16, bf16[256,1024]{1,0:T(8,128)(2,1)S(1)} %copy-done.10, bf16[2,1,256,512]{3,2,1,0:T(8,128)(2,1)S(1)} %copy-done.7, ...), custom_call_target="tpu_custom_call" | custom-call | flops 99999997952 | bytes 4194308 | tf_op jit(solution)/shard_map/keys/pallas_call | solution.py:56
  36.7 6.4 %collective-permute-done.4.refs_3_.refs_6_ = bf16[256,1024]{1,0:T(8,128)(2,1)} collective-permute-done((bf16[256,1024]{1,0:T(8,128)(2,1)}, bf16[256,1024]{1,0:T(8,128)(2,1)}, u32[]{:S(2)}, u32[]{:S(2)}) %collective-permute-start.4) | collective-permute-done | bytes 524320 | tf_op jit(solution)/shard_map/ppermute | solution.py:34
  43.1 2.4 %keys.5 = (f32[512,256]{1,0:T(8,128)S(1)}, f32[512,256]{1,0:T(8,128)S(1)}) custom-call(f32[512,256]{1,0:T(8,128)S(1)} %get-tuple-element.33.refs_0_, s32[1]{0:T(128)} %bitcast.refs_0_.refs_1_, bf16[256,1024]{1,0:T(8,128)(2,1)} %collective-permute-done.3.refs_2_.refs_5_, bf16[256,1024]{1,0:T(8,128)(2,1)} %collective-permute-done.4.refs_3_.refs_6_, ...), custom_call_target="tpu_custom_call" | custom-call | flops 99999997952 | bytes 4194308 | tf_op jit(solution)/shard_map/keys/pallas_call | solution.py:56
  45.6 0.7 collective-permute-start.5
  46.4 0.5 collective-permute-start.7
  46.9 1.0 collective-permute-done.5.refs_2_
  47.9 0.7 collective-permute-start.8
  48.6 0.2 collective-permute-done.6.refs_1_.refs_2_
  48.8 6.8 %collective-permute-done.7.refs_2_.refs_3_ = bf16[512,256]{1,0:T(8,128)(2,1)S(1)} collective-permute-done((bf16[512,256]{1,0:T(8,128)(2,1)S(1)}, bf16[512,256]{1,0:T(8,128)(2,1)S(1)}, u32[]{:S(2)}, u32[]{:S(2)}) %collective-permute-start.7) | collective-permute-done | bytes 262176 | tf_op jit(solution)/shard_map/ppermute | solution.py:34
  55.6 1.8 %turn.2 = (bf16[512,1024]{1,0:T(8,128)(2,1)S(1)}, bf16[512,1024]{1,0:T(8,128)(2,1)S(1)}) custom-call(bf16[512,256]{1,0:T(8,128)(2,1)S(1)} %core_sum.4.refs_0_.refs_2_, bf16[32,512]{1,0:T(8,128)(2,1)} %collective-permute-done.6.refs_1_.refs_2_, bf16[512,256]{1,0:T(8,128)(2,1)S(1)} %collective-permute-done.7.refs_2_.refs_3_, bf16[256,1024]{1,0:T(8,128)(2,1)S(1)} %copy-done.17, ...), custom_call_target="tpu_custom_call" | custom-call | flops 99999997952 | bytes 2097152 | tf_op jit(solution)/shard_map/turn/pallas_call | solution.py:56
  57.5 2.8 %collective-permute-done.8.refs_4_ = bf16[512,256]{1,0:T(8,128)(2,1)S(1)} collective-permute-done((bf16[512,256]{1,0:T(8,128)(2,1)S(1)}, bf16[512,256]{1,0:T(8,128)(2,1)S(1)}, u32[]{:S(2)}, u32[]{:S(2)}) %collective-permute-start.8) | collective-permute-done | bytes 262176 | tf_op jit(solution)/shard_map/ppermute | solution.py:34
  60.3 0.1 residual.2.refs_2_.refs_3_
  60.5 1.9 %collective-permute-done.9.refs_3_.refs_4_ = bf16[1024,256]{1,0:T(8,128)(2,1)S(1)} collective-permute-done((bf16[1024,256]{1,0:T(8,128)(2,1)S(1)}, bf16[1024,256]{1,0:T(8,128)(2,1)S(1)}, u32[]{:S(2)}, u32[]{:S(2)}) %collective-permute-start.9) | collective-permute-done | bytes 524320 | tf_op jit(solution)/shard_map/ppermute | solution.py:34
  62.4 1.7 grads.4
  64.1 2.0 %collective-permute-start.13 = (bf16[512,256]{1,0:T(8,128)(2,1)}, bf16[512,256]{1,0:T(8,128)(2,1)}, u32[]{:S(2)}, u32[]{:S(2)}) collective-permute-start(bf16[512,256]{1,0:T(8,128)(2,1)} %get-tuple-element.40.refs_0_), channel_id=1, source_target_pairs={{0,6},{1,7},{2,4},{3,5},{4,2},{5,3},{6,0},{7,1},{8,14},{9,15},{10,... | collective-permute-start | bytes 786440 | tf_op jit(solution)/shard_map/ppermute | solution.py:34
  66.1 0.8 grads.5.refs_0_.refs_1_.refs_3_
  66.9 1.6 mean.1.refs_0_
  68.6 1.0 copy-done.12
  69.5 7.5 %all-to-all-start.1 = ((bf16[16,32,512]{2,1,0:T(8,128)(2,1)}), bf16[16,32,512]{2,1,0:T(8,128)(2,1)S(1)}, u32[]{:S(2)}, u32[]{:S(2)}) async-start(bf16[16,32,512]{2,1,0:T(8,128)(2,1)} %mean.1.refs_0_), calls=%async_computation.1 | async-start | bytes 1048576 | tf_op jit(solution)/shard_map/all_to_all | solution.py:348
  77.0 2.7 %prepare.5 = (bf16[256,1024]{1,0:T(8,128)(2,1)}, bf16[256,1024]{1,0:T(8,128)(2,1)}, bf16[256,1024]{1,0:T(8,128)(2,1)}) custom-call(bf16[16,32,512]{2,1,0:T(8,128)(2,1)} %mean.1.refs_0_, s32[1]{0:T(128)} %bitcast.refs_0_.refs_1_, bf16[2,1,256,4096]{3,2,1,0:T(8,128)(2,1)} %refs_2_.4), custom_call_target="tpu_custom_call" | custom-call | flops 99999997952 | bytes 4194308 | tf_op jit(solution)/shard_map/prepare/pallas_call | solution.py:56
  79.8 2.7 %collective-permute-start.12 = (bf16[256,1024]{1,0:T(8,128)(2,1)}, bf16[256,1024]{1,0:T(8,128)(2,1)S(1)}, u32[]{:S(2)}, u32[]{:S(2)}) collective-permute-start(bf16[256,1024]{1,0:T(8,128)(2,1)} %get-tuple-element.45), channel_id=1, source_target_pairs={{0,2},{1,3},{2,0},{3,1},{4,6},{5,7},{6,4},{7,5},{8,10},{9,11},{10,... | collective-permute-start | bytes 1572872 | tf_op jit(solution)/shard_map/ppermute | solution.py:34
  82.5 0.4 collective-permute-start.11
  82.8 1.9 %collective-permute-done.10.refs_2_ = bf16[512,256]{1,0:T(8,128)(2,1)} collective-permute-done((bf16[512,256]{1,0:T(8,128)(2,1)}, bf16[512,256]{1,0:T(8,128)(2,1)}, u32[]{:S(2)}, u32[]{:S(2)}) %collective-permute-start.10) | collective-permute-done | bytes 262176 | tf_op jit(solution)/shard_map/ppermute | solution.py:34
  84.8 2.1 %all-to-all-done.1.refs_6_.refs_8_.refs_1_ = bf16[16,32,512]{2,1,0:T(8,128)(2,1)S(1)} async-done(((bf16[16,32,512]{2,1,0:T(8,128)(2,1)}), bf16[16,32,512]{2,1,0:T(8,128)(2,1)S(1)}, u32[]{:S(2)}, u32[]{:S(2)}) %all-to-all-start.1) | async-done | bytes 524320 | tf_op jit(solution)/shard_map/all_to_all | solution.py:348
  86.9 1.2 copy-done.3
  88.2 1.2 copy-done.5
  89.4 1.0 copy-done.11
  90.4 1.2 copy-done.13
  91.7 1.7 first_update.2
  93.3 0.4 collective-permute-start.15
  93.8 1.8 %collective-permute-done.12.refs_2_.refs_4_.refs_3_ = bf16[256,1024]{1,0:T(8,128)(2,1)S(1)} collective-permute-done((bf16[256,1024]{1,0:T(8,128)(2,1)}, bf16[256,1024]{1,0:T(8,128)(2,1)S(1)}, u32[]{:S(2)}, u32[]{:S(2)}) %collective-permute-start.12) | collective-permute-done | bytes 524320 | tf_op jit(solution)/shard_map/ppermute | solution.py:34
  95.5 1.7 first_update.3
  97.2 0.3 collective-permute-start.17
  97.5 18.1 %collective-permute-done.14.refs_5_.refs_4_ = bf16[256,1024]{1,0:T(8,128)(2,1)} collective-permute-done((bf16[256,1024]{1,0:T(8,128)(2,1)}, bf16[256,1024]{1,0:T(8,128)(2,1)}, u32[]{:S(2)}, u32[]{:S(2)}) %collective-permute-start.14) | collective-permute-done | bytes 524320 | tf_op jit(solution)/shard_map/ppermute | solution.py:34
  115.7 2.1 %keys.6 = (f32[1024,128]{1,0:T(8,128)S(1)}, f32[1024,128]{1,0:T(8,128)S(1)}) custom-call(bf16[512,256]{1,0:T(8,128)(2,1)S(1)} %get-tuple-element.46.refs_0_.refs_7_.refs_2_, s32[1]{0:T(128)} %bitcast.refs_0_.refs_1_, bf16[256,1024]{1,0:T(8,128)(2,1)S(1)} %copy-done.15, bf16[256,1024]{1,0:T(8,128)(2,1)} %collective-permute-done.11.refs_1_.refs_3_.refs_2_, ...), custom_call_target="tpu_custom_call" | custom-call | flops 99999997952 | bytes 3145732 | tf_op jit(solution)/shard_map/keys/pallas_call | solution.py:56
  117.9 2.1 %keys.7 = (f32[1024,128]{1,0:T(8,128)S(1)}, f32[1024,128]{1,0:T(8,128)S(1)}) custom-call(f32[1024,128]{1,0:T(8,128)S(1)} %get-tuple-element.48.refs_0_, s32[1]{0:T(128)} %bitcast.refs_0_.refs_1_, bf16[256,1024]{1,0:T(8,128)(2,1)S(1)} %copy-done.15, bf16[256,1024]{1,0:T(8,128)(2,1)} %collective-permute-done.11.refs_1_.refs_3_.refs_2_, ...), custom_call_target="tpu_custom_call" | custom-call | flops 99999997952 | bytes 3145732 | tf_op jit(solution)/shard_map/keys/pallas_call | solution.py:56
  120.0 0.6 collective-permute-start.18
  120.6 1.5 collective-permute-done.18.refs_3_
  122.2 2.2 %collective-permute-start.19 = (bf16[1024,256]{1,0:T(8,128)(2,1)S(1)}, bf16[1024,256]{1,0:T(8,128)(2,1)S(1)}, u32[]{:S(2)}, u32[]{:S(2)}) collective-permute-start(bf16[1024,256]{1,0:T(8,128)(2,1)S(1)} %core_sum.5.refs_0_.refs_1_), channel_id=1, source_target_pairs={{0,2},{1,3},{2,0},{3,1},{4,6},{5,7},{6,4},{7,5},{8,10},{9,11},{10,... | collective-permute-start | bytes 1572872 | tf_op jit(solution)/shard_map/ppermute | solution.py:34
  124.5 1.8 %turn.3 = (bf16[512,1024]{1,0:T(8,128)(2,1)S(1)}, bf16[512,1024]{1,0:T(8,128)(2,1)S(1)}) custom-call(bf16[1024,256]{1,0:T(8,128)(2,1)S(1)} %core_sum.5.refs_0_.refs_1_, bf16[256,1024]{1,0:T(8,128)(2,1)S(1)} %copy-done.15, bf16[256,1024]{1,0:T(8,128)(2,1)} %collective-permute-done.11.refs_1_.refs_3_.refs_2_, ...), custom_call_target="tpu_custom_call" | custom-call | flops 99999997952 | bytes 2097152 | tf_op jit(solution)/shard_map/turn/pallas_call | solution.py:56
  126.3 10.4 %collective-permute-done.19.refs_2_ = bf16[1024,256]{1,0:T(8,128)(2,1)S(1)} collective-permute-done((bf16[1024,256]{1,0:T(8,128)(2,1)S(1)}, bf16[1024,256]{1,0:T(8,128)(2,1)S(1)}, u32[]{:S(2)}, u32[]{:S(2)}) %collective-permute-start.19) | collective-permute-done | bytes 524320 | tf_op jit(solution)/shard_map/ppermute | solution.py:34
  136.7 0.1 residual.3.refs_2_.refs_3_
  136.9 1.9 %collective-permute-done.20.refs_3_.refs_4_ = bf16[1024,256]{1,0:T(8,128)(2,1)S(1)} collective-permute-done((bf16[1024,256]{1,0:T(8,128)(2,1)S(1)}, bf16[1024,256]{1,0:T(8,128)(2,1)S(1)}, u32[]{:S(2)}, u32[]{:S(2)}) %collective-permute-start.20) | collective-permute-done | bytes 524320 | tf_op jit(solution)/shard_map/ppermute | solution.py:34
  138.8 1.6 grads.6
  140.4 2.0 %collective-permute-start.21 = (bf16[512,256]{1,0:T(8,128)(2,1)}, bf16[512,256]{1,0:T(8,128)(2,1)}, u32[]{:S(2)}, u32[]{:S(2)}) collective-permute-start(bf16[512,256]{1,0:T(8,128)(2,1)} %get-tuple-element.53.refs_0_), channel_id=1, source_target_pairs={{0,6},{1,7},{2,4},{3,5},{4,2},{5,3},{6,0},{7,1},{8,14},{9,15},{10,... | collective-permute-start | bytes 786440 | tf_op jit(solution)/shard_map/ppermute | solution.py:34
  142.5 0.8 grads.7.refs_0_
  143.3 0.4 copy-done.4
  143.7 0.3 copy-done.6
  144.0 1.2 outer.1
  145.2 15.9 %collective-permute-done.22.refs_1_ = bf16[512,256]{1,0:T(8,128)(2,1)} collective-permute-done((bf16[512,256]{1,0:T(8,128)(2,1)}, bf16[512,256]{1,0:T(8,128)(2,1)}, u32[]{:S(2)}, u32[]{:S(2)}) %collective-permute-start.22) | collective-permute-done | bytes 262176 | tf_op jit(solution)/shard_map/ppermute | solution.py:34
  161.1 1.4 update.2.refs_5_
  162.6 3.4 %collective-permute-done.21.refs_1_ = bf16[512,256]{1,0:T(8,128)(2,1)} collective-permute-done((bf16[512,256]{1,0:T(8,128)(2,1)}, bf16[512,256]{1,0:T(8,128)(2,1)}, u32[]{:S(2)}, u32[]{:S(2)}) %collective-permute-start.21) | collective-permute-done | bytes 262176 | tf_op jit(solution)/shard_map/ppermute | solution.py:34
  166.0 2.2 %update.3 = bf16[1,512,512]{2,1,0:T(8,128)(2,1)} custom-call(f32[512,512]{1,0:T(8,128)S(1)} %grads.7.refs_0_, bf16[512,256]{1,0:T(8,128)(2,1)} %collective-permute-done.21.refs_1_, bf16[512,256]{1,0:T(8,128)(2,1)S(1)} %get-tuple-element.46.refs_0_.refs_7_.refs_2_, f32[512,256]{1,0:T(8,128)S(1)} %get-tuple-element.55.refs_3_, ...), custom_call_target="tpu_custom_call" | custom-call | flops 99999997952 | bytes 2883584 | tf_op jit(solution)/shard_map/update/pallas_call | solution.py:56
  (48 shorter events, 0.8 us)
Async XLA Ops:
  0.6 7.9 %copy-start = (f32[1,512,512]{2,1,0:T(8,128)S(1)}, f32[1,512,512]{2,1,0:T(8,128)}, u32[]{:S(2)}) copy-start(f32[1,512,512]{2,1,0:T(8,128)} %refs_1_.3) | copy-start | bytes 3145732
  3.6 4.9 %collective-permute-start = (bf16[256,1024]{1,0:T(8,128)(2,1)}, bf16[256,1024]{1,0:T(8,128)(2,1)S(1)}, u32[]{:S(2)}, u32[]{:S(2)}) collective-permute-start(bf16[256,1024]{1,0:T(8,128)(2,1)} %get-tuple-element.31), channel_id=1, source_target_pairs={{0,1},{1,0},{2,3},{3,2},{4,5},{5,4},{6,7},{7,6},{8,9},{9,8},{10,11... | collective-permute-start | bytes 1572872 | tf_op jit(solution)/shard_map/ppermute | solution.py:34
  3.7 30.7 %collective-permute-start.1 = (bf16[1,512,512]{2,1,0:T(8,128)(2,1)}, bf16[1,512,512]{2,1,0:T(8,128)(2,1)}, u32[]{:S(2)}, u32[]{:S(2)}) collective-permute-start(bf16[1,512,512]{2,1,0:T(8,128)(2,1)} %refs_5_.7), channel_id=1, source_target_pairs={{0,6},{1,7},{2,4},{3,5},{4,2},{5,3},{6,0},{7,1},{8,14},{9,15},{10,... | collective-permute-start | bytes 1572872 | tf_op jit(solution)/shard_map/ppermute | solution.py:34
  5.7 31.0 %collective-permute-start.3 = (bf16[256,1024]{1,0:T(8,128)(2,1)}, bf16[256,1024]{1,0:T(8,128)(2,1)}, u32[]{:S(2)}, u32[]{:S(2)}) collective-permute-start(bf16[256,1024]{1,0:T(8,128)(2,1)} %get-tuple-element.35), channel_id=1, source_target_pairs={{0,2},{1,3},{2,0},{3,1},{4,6},{5,7},{6,4},{7,5},{8,10},{9,11},{10,... | collective-permute-start | bytes 1572872 | tf_op jit(solution)/shard_map/ppermute | solution.py:34
  8.6 34.6 %collective-permute-start.4 = (bf16[256,1024]{1,0:T(8,128)(2,1)}, bf16[256,1024]{1,0:T(8,128)(2,1)}, u32[]{:S(2)}, u32[]{:S(2)}) collective-permute-start(bf16[256,1024]{1,0:T(8,128)(2,1)} %get-tuple-element.36), channel_id=1, source_target_pairs={{0,3},{1,2},{2,1},{3,0},{4,7},{5,6},{6,5},{7,4},{8,11},{9,10},{10,... | collective-permute-start | bytes 1572872 | tf_op jit(solution)/shard_map/ppermute | solution.py:34
  9.4 0.8 copy-start.9
  10.2 18.0 %all-to-all-start = ((bf16[16,32,512]{2,1,0:T(8,128)(2,1)}), bf16[16,32,512]{2,1,0:T(8,128)(2,1)S(1)}, u32[]{:S(2)}, u32[]{:S(2)}) async-start(bf16[16,32,512]{2,1,0:T(8,128)(2,1)} %cast.1.refs_0_), calls=%async_computation | async-start | bytes 1048576 | tf_op jit(solution)/shard_map/all_to_all | solution.py:325
  19.5 14.9 %copy-start.7 = (bf16[2,1,256,512]{3,2,1,0:T(8,128)(2,1)S(1)}, bf16[2,1,256,512]{3,2,1,0:T(8,128)(2,1)}, u32[]{:S(2)}) copy-start(bf16[2,1,256,512]{3,2,1,0:T(8,128)(2,1)} %refs_6_.5) | copy-start | bytes 1572868
  19.5 14.9 %copy-start.10 = (bf16[256,1024]{1,0:T(8,128)(2,1)S(1)}, bf16[256,1024]{1,0:T(8,128)(2,1)}, u32[]{:S(2)}) copy-start(bf16[256,1024]{1,0:T(8,128)(2,1)} %copy-done.9) | copy-start | bytes 1572868
  28.2 1.0 copy-start.14
  29.2 5.3 %copy-start.16 = (bf16[256,1024]{1,0:T(8,128)(2,1)S(1)}, bf16[256,1024]{1,0:T(8,128)(2,1)}, u32[]{:S(2)}) copy-start(bf16[256,1024]{1,0:T(8,128)(2,1)} %get-tuple-element.32.refs_2_.refs_3_) | copy-start | bytes 1572868
  29.9 18.9 %collective-permute-start.6 = (bf16[32,512]{1,0:T(8,128)(2,1)}, bf16[32,512]{1,0:T(8,128)(2,1)}, u32[]{:S(2)}, u32[]{:S(2)}) collective-permute-start(bf16[32,512]{1,0:T(8,128)(2,1)} %sum.1.refs_0_.refs_1_), channel_id=1, source_target_pairs={{0,32},{8,40},{16,48},{24,56},{32,0},{40,8},{48,16},{56,24},{64,96... | collective-permute-start | bytes 98312 | tf_op jit(solution)/shard_map/ppermute | solution.py:34
  36.6 9.7 %collective-permute-start.2 = (f32[512,256]{1,0:T(8,128)S(1)}, f32[512,256]{1,0:T(8,128)S(1)}, u32[]{:S(2)}, u32[]{:S(2)}) collective-permute-start(f32[512,256]{1,0:T(8,128)S(1)} %get-tuple-element.34), channel_id=1, source_target_pairs={{0,1},{1,0},{2,3},{3,2},{4,5},{5,4},{6,7},{7,6},{8,9},{9,8},{10,11... | collective-permute-start | bytes 1572872 | tf_op jit(solution)/shard_map/ppermute | solution.py:34
  45.6 2.3 %collective-permute-start.5 = (f32[512,256]{1,0:T(8,128)S(1)}, f32[512,256]{1,0:T(8,128)S(1)}, u32[]{:S(2)}, u32[]{:S(2)}) collective-permute-start(f32[512,256]{1,0:T(8,128)S(1)} %get-tuple-element.38), channel_id=1, source_target_pairs={{0,1},{1,0},{2,3},{3,2},{4,5},{5,4},{6,7},{7,6},{8,9},{9,8},{10,11... | collective-permute-start | bytes 1572872 | tf_op jit(solution)/shard_map/ppermute | solution.py:34
  46.4 9.3 %collective-permute-start.7 = (bf16[512,256]{1,0:T(8,128)(2,1)S(1)}, bf16[512,256]{1,0:T(8,128)(2,1)S(1)}, u32[]{:S(2)}, u32[]{:S(2)}) collective-permute-start(bf16[512,256]{1,0:T(8,128)(2,1)S(1)} %core_sum.3.refs_0_.refs_1_), channel_id=1, source_target_pairs={{0,2},{1,3},{2,0},{3,1},{4,6},{5,7},{6,4},{7,5},{8,10},{9,11},{10,... | collective-permute-start | bytes 786440 | tf_op jit(solution)/shard_map/ppermute | solution.py:34
  47.8 7.8 %copy-start.17 = (bf16[256,1024]{1,0:T(8,128)(2,1)S(1)}, bf16[256,1024]{1,0:T(8,128)(2,1)}, u32[]{:S(2)}) copy-start(bf16[256,1024]{1,0:T(8,128)(2,1)} %get-tuple-element.32.refs_2_.refs_3_) | copy-start | bytes 1572868
  47.9 12.4 %collective-permute-start.8 = (bf16[512,256]{1,0:T(8,128)(2,1)S(1)}, bf16[512,256]{1,0:T(8,128)(2,1)S(1)}, u32[]{:S(2)}, u32[]{:S(2)}) collective-permute-start(bf16[512,256]{1,0:T(8,128)(2,1)S(1)} %core_sum.4.refs_0_.refs_2_), channel_id=1, source_target_pairs={{0,2},{1,3},{2,0},{3,1},{4,6},{5,7},{6,4},{7,5},{8,10},{9,11},{10,... | collective-permute-start | bytes 786440 | tf_op jit(solution)/shard_map/ppermute | solution.py:34
  60.4 2.0 %collective-permute-start.9 = (bf16[1024,256]{1,0:T(8,128)(2,1)S(1)}, bf16[1024,256]{1,0:T(8,128)(2,1)S(1)}, u32[]{:S(2)}, u32[]{:S(2)}) collective-permute-start(bf16[1024,256]{1,0:T(8,128)(2,1)S(1)} %residual.2.refs_2_.refs_3_), channel_id=1, source_target_pairs={{0,1},{1,0},{2,3},{3,2},{4,5},{5,4},{6,7},{7,6},{8,9},{9,8},{10,11... | collective-permute-start | bytes 1572872 | tf_op jit(solution)/shard_map/ppermute | solution.py:34
  64.1 20.7 %collective-permute-start.10 = (bf16[512,256]{1,0:T(8,128)(2,1)}, bf16[512,256]{1,0:T(8,128)(2,1)}, u32[]{:S(2)}, u32[]{:S(2)}) collective-permute-start(bf16[512,256]{1,0:T(8,128)(2,1)} %get-tuple-element.43), channel_id=1, source_target_pairs={{0,6},{1,7},{2,4},{3,5},{4,2},{5,3},{6,0},{7,1},{8,14},{9,15},{10,... | collective-permute-start | bytes 786440 | tf_op jit(solution)/shard_map/ppermute | solution.py:34
  64.1 29.7 %collective-permute-start.13 = (bf16[512,256]{1,0:T(8,128)(2,1)}, bf16[512,256]{1,0:T(8,128)(2,1)}, u32[]{:S(2)}, u32[]{:S(2)}) collective-permute-start(bf16[512,256]{1,0:T(8,128)(2,1)} %get-tuple-element.40.refs_0_), channel_id=1, source_target_pairs={{0,6},{1,7},{2,4},{3,5},{4,2},{5,3},{6,0},{7,1},{8,14},{9,15},{10,... | collective-permute-start | bytes 786440 | tf_op jit(solution)/shard_map/ppermute | solution.py:34
  68.6 1.0 copy-start.12
  69.5 17.4 %all-to-all-start.1 = ((bf16[16,32,512]{2,1,0:T(8,128)(2,1)}), bf16[16,32,512]{2,1,0:T(8,128)(2,1)S(1)}, u32[]{:S(2)}, u32[]{:S(2)}) async-start(bf16[16,32,512]{2,1,0:T(8,128)(2,1)} %mean.1.refs_0_), calls=%async_computation.1 | async-start | bytes 1048576 | tf_op jit(solution)/shard_map/all_to_all | solution.py:348
  77.0 9.9 %copy-start.1 = (f32[1,512,512]{2,1,0:T(8,128)S(1)}, f32[1,512,512]{2,1,0:T(8,128)}, u32[]{:S(2)}) copy-start(f32[1,512,512]{2,1,0:T(8,128)} %refs_6_.3) | copy-start | bytes 3145732
  77.0 9.9 %copy-start.2 = (f32[1,512,512]{2,1,0:T(8,128)S(1)}, f32[1,512,512]{2,1,0:T(8,128)}, u32[]{:S(2)}) copy-start(f32[1,512,512]{2,1,0:T(8,128)} %refs_7_.7) | copy-start | bytes 3145732
  79.8 15.7 %collective-permute-start.12 = (bf16[256,1024]{1,0:T(8,128)(2,1)}, bf16[256,1024]{1,0:T(8,128)(2,1)S(1)}, u32[]{:S(2)}, u32[]{:S(2)}) collective-permute-start(bf16[256,1024]{1,0:T(8,128)(2,1)} %get-tuple-element.45), channel_id=1, source_target_pairs={{0,2},{1,3},{2,0},{3,1},{4,6},{5,7},{6,4},{7,5},{8,10},{9,11},{10,... | collective-permute-start | bytes 1572872 | tf_op jit(solution)/shard_map/ppermute | solution.py:34
  82.5 33.2 %collective-permute-start.14 = (bf16[256,1024]{1,0:T(8,128)(2,1)}, bf16[256,1024]{1,0:T(8,128)(2,1)}, u32[]{:S(2)}, u32[]{:S(2)}) collective-permute-start(bf16[256,1024]{1,0:T(8,128)(2,1)} %get-tuple-element.47), channel_id=1, source_target_pairs={{0,3},{1,2},{2,1},{3,0},{4,7},{5,6},{6,5},{7,4},{8,11},{9,10},{10,... | collective-permute-start | bytes 1572872 | tf_op jit(solution)/shard_map/ppermute | solution.py:34
  82.5 13.1 %collective-permute-start.11 = (bf16[256,1024]{1,0:T(8,128)(2,1)}, bf16[256,1024]{1,0:T(8,128)(2,1)}, u32[]{:S(2)}, u32[]{:S(2)}) collective-permute-start(bf16[256,1024]{1,0:T(8,128)(2,1)} %get-tuple-element.42.refs_0_), channel_id=1, source_target_pairs={{0,1},{1,0},{2,3},{3,2},{4,5},{5,4},{6,7},{7,6},{8,9},{9,8},{10,11... | collective-permute-start | bytes 1572872 | tf_op jit(solution)/shard_map/ppermute | solution.py:34
  86.9 1.2 copy-start.3
  88.2 1.2 copy-start.5
  89.4 1.0 copy-start.11
  90.4 1.2 copy-start.13
  93.3 22.3 %copy-start.8 = (bf16[2,1,256,512]{3,2,1,0:T(8,128)(2,1)S(1)}, bf16[2,1,256,512]{3,2,1,0:T(8,128)(2,1)}, u32[]{:S(2)}) copy-start(bf16[2,1,256,512]{3,2,1,0:T(8,128)(2,1)} %refs_6_.5) | copy-start | bytes 1572868
  93.3 22.3 %copy-start.15 = (bf16[256,1024]{1,0:T(8,128)(2,1)S(1)}, bf16[256,1024]{1,0:T(8,128)(2,1)}, u32[]{:S(2)}) copy-start(bf16[256,1024]{1,0:T(8,128)(2,1)} %prepare.4.refs_0_.refs_2_.refs_1_) | copy-start | bytes 1572868
  93.3 22.3 %collective-permute-start.15 = (bf16[512,256]{1,0:T(8,128)(2,1)S(1)}, bf16[512,256]{1,0:T(8,128)(2,1)S(1)}, u32[]{:S(2)}, u32[]{:S(2)}) collective-permute-start(bf16[512,256]{1,0:T(8,128)(2,1)S(1)} %get-tuple-element.44.refs_0_.refs_7_.refs_2_), channel_id=1, source_target_pairs={{0,6},{1,7},{2,4},{3,5},{4,2},{5,3},{6,0},{7,1},{8,14},{9,15},{10,... | collective-permute-start | bytes 786440 | tf_op jit(solution)/shard_map/ppermute | solution.py:34
  97.2 20.7 %collective-permute-start.17 = (bf16[512,256]{1,0:T(8,128)(2,1)S(1)}, bf16[512,256]{1,0:T(8,128)(2,1)S(1)}, u32[]{:S(2)}, u32[]{:S(2)}) collective-permute-start(bf16[512,256]{1,0:T(8,128)(2,1)S(1)} %get-tuple-element.46.refs_0_.refs_7_.refs_2_), channel_id=1, source_target_pairs={{0,6},{1,7},{2,4},{3,5},{4,2},{5,3},{6,0},{7,1},{8,14},{9,15},{10,... | collective-permute-start | bytes 786440 | tf_op jit(solution)/shard_map/ppermute | solution.py:34
  117.8 2.8 %collective-permute-start.16 = (f32[1024,128]{1,0:T(8,128)S(1)}, f32[1024,128]{1,0:T(8,128)S(1)}, u32[]{:S(2)}, u32[]{:S(2)}) collective-permute-start(f32[1024,128]{1,0:T(8,128)S(1)} %get-tuple-element.49), channel_id=1, source_target_pairs={{0,1},{1,0},{2,3},{3,2},{4,5},{5,4},{6,7},{7,6},{8,9},{9,8},{10,11... | collective-permute-start | bytes 1572872 | tf_op jit(solution)/shard_map/ppermute | solution.py:34
  120.0 2.1 %collective-permute-start.18 = (f32[1024,128]{1,0:T(8,128)S(1)}, f32[1024,128]{1,0:T(8,128)S(1)}, u32[]{:S(2)}, u32[]{:S(2)}) collective-permute-start(f32[1024,128]{1,0:T(8,128)S(1)} %get-tuple-element.51), channel_id=1, source_target_pairs={{0,1},{1,0},{2,3},{3,2},{4,5},{5,4},{6,7},{7,6},{8,9},{9,8},{10,11... | collective-permute-start | bytes 1572872 | tf_op jit(solution)/shard_map/ppermute | solution.py:34
  122.2 14.4 %collective-permute-start.19 = (bf16[1024,256]{1,0:T(8,128)(2,1)S(1)}, bf16[1024,256]{1,0:T(8,128)(2,1)S(1)}, u32[]{:S(2)}, u32[]{:S(2)}) collective-permute-start(bf16[1024,256]{1,0:T(8,128)(2,1)S(1)} %core_sum.5.refs_0_.refs_1_), channel_id=1, source_target_pairs={{0,2},{1,3},{2,0},{3,1},{4,6},{5,7},{6,4},{7,5},{8,10},{9,11},{10,... | collective-permute-start | bytes 1572872 | tf_op jit(solution)/shard_map/ppermute | solution.py:34
  136.8 2.0 %collective-permute-start.20 = (bf16[1024,256]{1,0:T(8,128)(2,1)S(1)}, bf16[1024,256]{1,0:T(8,128)(2,1)S(1)}, u32[]{:S(2)}, u32[]{:S(2)}) collective-permute-start(bf16[1024,256]{1,0:T(8,128)(2,1)S(1)} %residual.3.refs_2_.refs_3_), channel_id=1, source_target_pairs={{0,1},{1,0},{2,3},{3,2},{4,5},{5,4},{6,7},{7,6},{8,9},{9,8},{10,11... | collective-permute-start | bytes 1572872 | tf_op jit(solution)/shard_map/ppermute | solution.py:34
  140.4 20.7 %collective-permute-start.22 = (bf16[512,256]{1,0:T(8,128)(2,1)}, bf16[512,256]{1,0:T(8,128)(2,1)}, u32[]{:S(2)}, u32[]{:S(2)}) collective-permute-start(bf16[512,256]{1,0:T(8,128)(2,1)} %get-tuple-element.57), channel_id=1, source_target_pairs={{0,6},{1,7},{2,4},{3,5},{4,2},{5,3},{6,0},{7,1},{8,14},{9,15},{10,... | collective-permute-start | bytes 786440 | tf_op jit(solution)/shard_map/ppermute | solution.py:34
  140.4 25.5 %collective-permute-start.21 = (bf16[512,256]{1,0:T(8,128)(2,1)}, bf16[512,256]{1,0:T(8,128)(2,1)}, u32[]{:S(2)}, u32[]{:S(2)}) collective-permute-start(bf16[512,256]{1,0:T(8,128)(2,1)} %get-tuple-element.53.refs_0_), channel_id=1, source_target_pairs={{0,6},{1,7},{2,4},{3,5},{4,2},{5,3},{6,0},{7,1},{8,14},{9,15},{10,... | collective-permute-start | bytes 786440 | tf_op jit(solution)/shard_map/ppermute | solution.py:34
  142.5 1.2 copy-start.4
  142.5 1.5 copy-start.6

commit v4 on v3

--- a/solution.py
+++ b/solution.py
@@ -46,7 +46,7 @@
     return jax.ShapeDtypeStruct(shape, dtype)
 
 
-def call(body, outs, operands, gates=(), specs=None, limit=VMEM_LIMIT, scratch=()):
+def call(body, outs, operands, gates=(), specs=None, limit=VMEM_LIMIT, scratch=(), out_specs=None, aliases={}):
     n = len(gates)
     size = sum(v.size * v.dtype.itemsize for v in operands)
 
@@ -59,7 +59,8 @@
         grid=(1,),
         out_shape=outs,
         in_specs=[ANY] * n + (specs or [FULL] * len(operands)),
-        out_specs=jax.tree.map(lambda _: FULL, outs),
+        out_specs=out_specs or jax.tree.map(lambda _: FULL, outs),
+        input_output_aliases=aliases,
         scratch_shapes=scratch,
         compiler_params=pltpu.CompilerParams(vmem_limit_bytes=limit),
         cost_estimate=pl.CostEstimate(flops=FLOPS, bytes_accessed=size, transcendentals=0),
@@ -102,7 +103,9 @@
             whole[...] = part
             for half, out in ((1 - core, sent), (core, kept)):
                 columns = pl.ds(pl.multiple_of(half * cols, cols), cols)
-                out[g * rows : (g + 1) * rows, k * cols : (k + 1) * cols] = whole[:, columns]
+                out[g * rows : (g + 1) * rows, k * cols : (k + 1) * cols] = whole[
+                    :, columns
+                ].astype(out.dtype)
 
 
 def core_sum_kernel(rows, *refs):
@@ -112,7 +115,7 @@
         kept, other = pairs[2 * k : 2 * k + 2]
         for g in range(out.shape[0] // rows):
             here, there = g * rows, (g ^ 1) * rows
-            total = kept[here : here + rows] + other[there : there + rows]
+            total = kept[here : here + rows] + other[there : there + rows].astype(F32)
             out[here : here + rows, k * cols : (k + 1) * cols] = total.astype(BF)
 
 
@@ -209,15 +212,8 @@
 
 
 def update_kernel(factor, kept, far, own, one, two, *rest):
-    done, out = rest[:-1], rest[-1]
     _, _, updated = adam(factor, kept[...], far[...], own[...], one[...], two[...])
-    cols = updated.shape[1]
-    if done:
-        for k, block in enumerate(done):
-            out[0, :, k * cols : (k + 1) * cols] = block[...]
-        out[0, :, len(done) * cols :] = updated.astype(BF)
-    else:
-        out[...] = updated.astype(BF)
+    rest[-1][...] = updated.astype(BF)
 
 
 def per_device(
@@ -259,7 +255,7 @@
         count = len(groups)
         return call(
             functools.partial(keys_kernel, scale, count, groups[0] == 0),
-            [shaped((count * tok_rows, len(chunks) * cols), F32)] * 2,
+            [shaped((count * tok_rows, len(chunks) * cols), kind) for kind in (F32, BF)],
             [place, *[feats[g] for g in groups], *views],
             gates,
             [SCALAR] + [FULL] * count + specs,
@@ -311,10 +307,12 @@
     def update(k, kept, far, own, one, two, done, gates):
         return call(
             functools.partial(update_kernel, factor),
-            shaped((1, rows, columns) if done else (rows, wide), BF),
+            shaped((1, rows, columns), BF),
             [kept, far, own, one, two, *done],
             gates,
-            [chunk((), k)] + [FULL] * (4 + len(done)),
+            [chunk((), k)] + [FULL] * 4 + [ANY] * len(done),
+            out_specs=chunk((0,), k),
+            aliases={len(gates) + 5: 0} if done else {},
         )
 
     far = far_swap(weights)

time: 169 us -> 169 us (level)
    unnamed x36 -> x40, local copies, waits for them, and re-layouts: 8.26 us -> 8.27 us
where the time goes in v4:
time: 169 us; the launch traced here: 168 us
  waiting for transfers between devices  83.2 us (49%)
  starting transfers between devices  37.8 us (22%)
  Pallas kernels  37.6 us (22%)
  local copies, waits for them, and re-layouts  8.27 us (5%)
    ppermute x23, waiting for transfers between devices, swap(): return lax.ppermute(value, axis, pairs)  72.5 us
    pallas_call x26, Pallas kernels, call(): pl.pallas_call(kernel, name=getattr(body, 'func', body).__name__.removesu...  37.6 us
    ppermute x23, starting transfers between devices, swap(): return lax.ppermute(value, axis, pairs)  22.9 us
    all_to_all x1, waiting for transfers between devices, per_device(): pieces = lax.all_to_all(casted, 'rep', 0, 0, axis_index_groups=groups)  8.6 us
    unnamed x40, local copies, waits for them, and re-layouts  8.27 us
    all_to_all x1, starting transfers between devices, per_device(): pieces = lax.all_to_all(casted, 'rep', 0, 0, axis_index_groups=groups)  7.48 us
    all_to_all x1, starting transfers between devices, per_device(): means = lax.all_to_all(copies, 'rep', 0, 0, axis_index_groups=groups)  7.48 us
  transfers between devices with their start and end apart: 25, of which 16 were waited for; matrix products, arithmetic and copies ran while one was open for 0% of the time, Pallas kernels for 17%

profile of v4, /device:TPU:34, one launch (start us, length us, event | category | flops | bytes accessed | tf_op | source)
XLA Modules:
  0.0 167.9 jit_solution(18163299760077990251)
XLA Ops:
  0.6 3.0 %prepare.3 = (bf16[256,1024]{1,0:T(8,128)(2,1)}, bf16[256,1024]{1,0:T(8,128)(2,1)}, bf16[256,1024]{1,0:T(8,128)(2,1)}, bf16[256,1024]{1,0:T(8,128)(2,1)}) custom-call(s32[1]{0:T(128)} %bitcast.refs_0_.refs_1_, bf16[2,1,256,4096]{3,2,1,0:T(8,128)(2,1)} %refs_2_.4), custom_call_target="tpu_custom_call" | custom-call | flops 99999997952 | bytes 4194308 | tf_op jit(solution)/shard_map/prepare/pallas_call | solution.py:56
  3.7 2.0 %collective-permute-start.1 = (bf16[1,512,512]{2,1,0:T(8,128)(2,1)}, bf16[1,512,512]{2,1,0:T(8,128)(2,1)}, u32[]{:S(2)}, u32[]{:S(2)}) collective-permute-start(bf16[1,512,512]{2,1,0:T(8,128)(2,1)} %refs_5_.7), channel_id=1, source_target_pairs={{0,6},{1,7},{2,4},{3,5},{4,2},{5,3},{6,0},{7,1},{8,14},{9,15},{10,... | collective-permute-start | bytes 1572872 | tf_op jit(solution)/shard_map/ppermute | solution.py:34
  5.7 2.8 %collective-permute-start.3 = (bf16[256,1024]{1,0:T(8,128)(2,1)}, bf16[256,1024]{1,0:T(8,128)(2,1)}, u32[]{:S(2)}, u32[]{:S(2)}) collective-permute-start(bf16[256,1024]{1,0:T(8,128)(2,1)} %get-tuple-element.35), channel_id=1, source_target_pairs={{0,2},{1,3},{2,0},{3,1},{4,6},{5,7},{6,4},{7,5},{8,10},{9,11},{10,... | collective-permute-start | bytes 1572872 | tf_op jit(solution)/shard_map/ppermute | solution.py:34
  8.6 0.8 cast.1.refs_0_
  9.4 0.8 copy-done.9
  10.2 7.5 %all-to-all-start = ((bf16[16,32,512]{2,1,0:T(8,128)(2,1)}), bf16[16,32,512]{2,1,0:T(8,128)(2,1)S(1)}, u32[]{:S(2)}, u32[]{:S(2)}) async-start(bf16[16,32,512]{2,1,0:T(8,128)(2,1)} %cast.1.refs_0_), calls=%async_computation | async-start | bytes 1048576 | tf_op jit(solution)/shard_map/all_to_all | solution.py:323
  17.7 1.9 %prepare.4.refs_0_.refs_2_.refs_1_ = bf16[256,1024]{1,0:T(8,128)(2,1)} custom-call(bf16[16,32,512]{2,1,0:T(8,128)(2,1)} %cast.1.refs_0_, s32[1]{0:T(128)} %bitcast.refs_0_.refs_1_, bf16[2,1,256,4096]{3,2,1,0:T(8,128)(2,1)} %refs_2_.4), custom_call_target="tpu_custom_call" | custom-call | flops 99999997952 | bytes 4194308 | tf_op jit(solution)/shard_map/prepare/pallas_call | solution.py:56
  19.6 8.6 %all-to-all-done.refs_1_ = bf16[16,32,512]{2,1,0:T(8,128)(2,1)S(1)} async-done(((bf16[16,32,512]{2,1,0:T(8,128)(2,1)}), bf16[16,32,512]{2,1,0:T(8,128)(2,1)S(1)}, u32[]{:S(2)}, u32[]{:S(2)}) %all-to-all-start) | async-done | bytes 524320 | tf_op jit(solution)/shard_map/all_to_all | solution.py:323
  28.2 1.0 copy-done.16
  29.2 0.7 sum.1.refs_0_.refs_1_
  29.9 4.6 %collective-permute-start.6 = (bf16[32,512]{1,0:T(8,128)(2,1)}, bf16[32,512]{1,0:T(8,128)(2,1)}, u32[]{:S(2)}, u32[]{:S(2)}) collective-permute-start(bf16[32,512]{1,0:T(8,128)(2,1)} %sum.1.refs_0_.refs_1_), channel_id=1, source_target_pairs={{0,32},{8,40},{16,48},{24,56},{32,0},{40,8},{48,16},{56,24},{64,96... | collective-permute-start | bytes 98312 | tf_op jit(solution)/shard_map/ppermute | solution.py:34
  34.5 2.2 %keys.4 = (f32[512,256]{1,0:T(8,128)S(1)}, bf16[512,256]{1,0:T(8,128)(2,1)S(1)}) custom-call(bf16[32,512]{1,0:T(8,128)(2,1)} %sum.1.refs_0_.refs_1_, s32[1]{0:T(128)} %bitcast.refs_0_.refs_1_, bf16[256,1024]{1,0:T(8,128)(2,1)S(1)} %copy-done.18, bf16[256,1024]{1,0:T(8,128)(2,1)S(1)} %copy-done.10, bf16[2,1,256,512]{3,2,1,0:T(8,128)(2,1)S(1)} %copy-done.7, ...), custom_call_target="tpu_custom_call" | custom-call | flops 99999997952 | bytes 4194308 | tf_op jit(solution)/shard_map/keys/pallas_call | solution.py:56
  36.8 6.3 %collective-permute-done.4.refs_3_.refs_6_ = bf16[256,1024]{1,0:T(8,128)(2,1)} collective-permute-done((bf16[256,1024]{1,0:T(8,128)(2,1)}, bf16[256,1024]{1,0:T(8,128)(2,1)}, u32[]{:S(2)}, u32[]{:S(2)}) %collective-permute-start.4) | collective-permute-done | bytes 524320 | tf_op jit(solution)/shard_map/ppermute | solution.py:34
  43.2 2.5 %keys.5 = (f32[512,256]{1,0:T(8,128)S(1)}, bf16[512,256]{1,0:T(8,128)(2,1)S(1)}) custom-call(f32[512,256]{1,0:T(8,128)S(1)} %get-tuple-element.33.refs_0_, s32[1]{0:T(128)} %bitcast.refs_0_.refs_1_, bf16[256,1024]{1,0:T(8,128)(2,1)} %collective-permute-done.3.refs_2_.refs_5_, bf16[256,1024]{1,0:T(8,128)(2,1)} %collective-permute-done.4.refs_3_.refs_6_, ...), custom_call_target="tpu_custom_call" | custom-call | flops 99999997952 | bytes 4194308 | tf_op jit(solution)/shard_map/keys/pallas_call | solution.py:56
  45.6 0.7 collective-permute-start.5
  46.5 0.5 collective-permute-start.7
  46.9 0.6 collective-permute-done.5.refs_2_
  47.6 1.1 collective-permute-start.8
  48.7 0.1 collective-permute-done.6.refs_1_.refs_2_
  48.8 6.9 %collective-permute-done.7.refs_2_.refs_3_ = bf16[512,256]{1,0:T(8,128)(2,1)S(1)} collective-permute-done((bf16[512,256]{1,0:T(8,128)(2,1)S(1)}, bf16[512,256]{1,0:T(8,128)(2,1)S(1)}, u32[]{:S(2)}, u32[]{:S(2)}) %collective-permute-start.7) | collective-permute-done | bytes 262176 | tf_op jit(solution)/shard_map/ppermute | solution.py:34
  55.7 1.8 %turn.2 = (bf16[512,1024]{1,0:T(8,128)(2,1)S(1)}, bf16[512,1024]{1,0:T(8,128)(2,1)S(1)}) custom-call(bf16[512,256]{1,0:T(8,128)(2,1)S(1)} %core_sum.4.refs_0_.refs_2_, bf16[32,512]{1,0:T(8,128)(2,1)} %collective-permute-done.6.refs_1_.refs_2_, bf16[512,256]{1,0:T(8,128)(2,1)S(1)} %collective-permute-done.7.refs_2_.refs_3_, bf16[256,1024]{1,0:T(8,128)(2,1)S(1)} %copy-done.19, ...), custom_call_target="tpu_custom_call" | custom-call | flops 99999997952 | bytes 2097152 | tf_op jit(solution)/shard_map/turn/pallas_call | solution.py:56
  57.5 2.8 %collective-permute-done.8.refs_4_ = bf16[512,256]{1,0:T(8,128)(2,1)S(1)} collective-permute-done((bf16[512,256]{1,0:T(8,128)(2,1)S(1)}, bf16[512,256]{1,0:T(8,128)(2,1)S(1)}, u32[]{:S(2)}, u32[]{:S(2)}) %collective-permute-start.8) | collective-permute-done | bytes 262176 | tf_op jit(solution)/shard_map/ppermute | solution.py:34
  60.4 0.1 residual.2.refs_2_.refs_3_
  60.6 1.9 %collective-permute-done.9.refs_3_.refs_4_ = bf16[1024,256]{1,0:T(8,128)(2,1)S(1)} collective-permute-done((bf16[1024,256]{1,0:T(8,128)(2,1)S(1)}, bf16[1024,256]{1,0:T(8,128)(2,1)S(1)}, u32[]{:S(2)}, u32[]{:S(2)}) %collective-permute-start.9) | collective-permute-done | bytes 524320 | tf_op jit(solution)/shard_map/ppermute | solution.py:34
  62.5 1.7 grads.4
  64.2 2.0 %collective-permute-start.13 = (bf16[512,256]{1,0:T(8,128)(2,1)}, bf16[512,256]{1,0:T(8,128)(2,1)}, u32[]{:S(2)}, u32[]{:S(2)}) collective-permute-start(bf16[512,256]{1,0:T(8,128)(2,1)} %get-tuple-element.40.refs_0_), channel_id=1, source_target_pairs={{0,6},{1,7},{2,4},{3,5},{4,2},{5,3},{6,0},{7,1},{8,14},{9,15},{10,... | collective-permute-start | bytes 786440 | tf_op jit(solution)/shard_map/ppermute | solution.py:34
  66.2 0.8 grads.5.refs_0_.refs_1_.refs_3_
  67.0 1.6 mean.1.refs_0_
  68.7 1.0 copy-done.14
  69.6 7.5 %all-to-all-start.1 = ((bf16[16,32,512]{2,1,0:T(8,128)(2,1)}), bf16[16,32,512]{2,1,0:T(8,128)(2,1)S(1)}, u32[]{:S(2)}, u32[]{:S(2)}) async-start(bf16[16,32,512]{2,1,0:T(8,128)(2,1)} %mean.1.refs_0_), calls=%async_computation.1 | async-start | bytes 1048576 | tf_op jit(solution)/shard_map/all_to_all | solution.py:346
  77.1 2.7 %prepare.5 = (bf16[256,1024]{1,0:T(8,128)(2,1)}, bf16[256,1024]{1,0:T(8,128)(2,1)}, bf16[256,1024]{1,0:T(8,128)(2,1)}) custom-call(bf16[16,32,512]{2,1,0:T(8,128)(2,1)} %mean.1.refs_0_, s32[1]{0:T(128)} %bitcast.refs_0_.refs_1_, bf16[2,1,256,4096]{3,2,1,0:T(8,128)(2,1)} %refs_2_.4), custom_call_target="tpu_custom_call" | custom-call | flops 99999997952 | bytes 4194308 | tf_op jit(solution)/shard_map/prepare/pallas_call | solution.py:56
  79.9 2.7 %collective-permute-start.12 = (bf16[256,1024]{1,0:T(8,128)(2,1)}, bf16[256,1024]{1,0:T(8,128)(2,1)S(1)}, u32[]{:S(2)}, u32[]{:S(2)}) collective-permute-start(bf16[256,1024]{1,0:T(8,128)(2,1)} %get-tuple-element.45), channel_id=1, source_target_pairs={{0,2},{1,3},{2,0},{3,1},{4,6},{5,7},{6,4},{7,5},{8,10},{9,11},{10,... | collective-permute-start | bytes 1572872 | tf_op jit(solution)/shard_map/ppermute | solution.py:34
  82.6 0.4 collective-permute-start.11
  82.9 1.9 %collective-permute-done.10.refs_2_ = bf16[512,256]{1,0:T(8,128)(2,1)} collective-permute-done((bf16[512,256]{1,0:T(8,128)(2,1)}, bf16[512,256]{1,0:T(8,128)(2,1)}, u32[]{:S(2)}, u32[]{:S(2)}) %collective-permute-start.10) | collective-permute-done | bytes 262176 | tf_op jit(solution)/shard_map/ppermute | solution.py:34
  84.9 2.2 %all-to-all-done.1.refs_6_.refs_8_.refs_1_ = bf16[16,32,512]{2,1,0:T(8,128)(2,1)S(1)} async-done(((bf16[16,32,512]{2,1,0:T(8,128)(2,1)}), bf16[16,32,512]{2,1,0:T(8,128)(2,1)S(1)}, u32[]{:S(2)}, u32[]{:S(2)}) %all-to-all-start.1) | async-done | bytes 524320 | tf_op jit(solution)/shard_map/all_to_all | solution.py:346
  87.0 1.2 copy-done.3
  88.3 1.2 copy-done.5
  89.5 1.0 copy-done.11
  90.5 1.2 copy-done.15
  91.8 1.7 first_update.2
  93.4 0.4 collective-permute-start.15
  93.8 1.8 %collective-permute-done.12.refs_2_.refs_4_.refs_3_ = bf16[256,1024]{1,0:T(8,128)(2,1)S(1)} collective-permute-done((bf16[256,1024]{1,0:T(8,128)(2,1)}, bf16[256,1024]{1,0:T(8,128)(2,1)S(1)}, u32[]{:S(2)}, u32[]{:S(2)}) %collective-permute-start.12) | collective-permute-done | bytes 524320 | tf_op jit(solution)/shard_map/ppermute | solution.py:34
  95.6 1.7 first_update.3
  97.3 0.3 collective-permute-start.17
  97.6 18.1 %collective-permute-done.14.refs_5_.refs_4_ = bf16[256,1024]{1,0:T(8,128)(2,1)} collective-permute-done((bf16[256,1024]{1,0:T(8,128)(2,1)}, bf16[256,1024]{1,0:T(8,128)(2,1)}, u32[]{:S(2)}, u32[]{:S(2)}) %collective-permute-start.14) | collective-permute-done | bytes 524320 | tf_op jit(solution)/shard_map/ppermute | solution.py:34
  115.8 2.1 %keys.6 = (f32[1024,128]{1,0:T(8,128)S(1)}, bf16[1024,128]{1,0:T(8,128)(2,1)S(1)}) custom-call(bf16[512,256]{1,0:T(8,128)(2,1)S(1)} %get-tuple-element.46.refs_0_.refs_7_.refs_2_, s32[1]{0:T(128)} %bitcast.refs_0_.refs_1_, bf16[256,1024]{1,0:T(8,128)(2,1)S(1)} %copy-done.17, bf16[256,1024]{1,0:T(8,128)(2,1)} %collective-permute-done.11.refs_1_.refs_3_.refs_2_, ...), custom_call_target="tpu_custom_call" | custom-call | flops 99999997952 | bytes 3145732 | tf_op jit(solution)/shard_map/keys/pallas_call | solution.py:56
  118.0 2.1 %keys.7 = (f32[1024,128]{1,0:T(8,128)S(1)}, bf16[1024,128]{1,0:T(8,128)(2,1)S(1)}) custom-call(f32[1024,128]{1,0:T(8,128)S(1)} %get-tuple-element.48.refs_0_, s32[1]{0:T(128)} %bitcast.refs_0_.refs_1_, bf16[256,1024]{1,0:T(8,128)(2,1)S(1)} %copy-done.17, bf16[256,1024]{1,0:T(8,128)(2,1)} %collective-permute-done.11.refs_1_.refs_3_.refs_2_, ...), custom_call_target="tpu_custom_call" | custom-call | flops 99999997952 | bytes 3145732 | tf_op jit(solution)/shard_map/keys/pallas_call | solution.py:56
  120.1 0.6 collective-permute-start.18
  120.7 1.2 collective-permute-done.18.refs_3_
  122.0 2.2 %collective-permute-start.19 = (bf16[1024,256]{1,0:T(8,128)(2,1)S(1)}, bf16[1024,256]{1,0:T(8,128)(2,1)S(1)}, u32[]{:S(2)}, u32[]{:S(2)}) collective-permute-start(bf16[1024,256]{1,0:T(8,128)(2,1)S(1)} %core_sum.5.refs_0_.refs_1_), channel_id=1, source_target_pairs={{0,2},{1,3},{2,0},{3,1},{4,6},{5,7},{6,4},{7,5},{8,10},{9,11},{10,... | collective-permute-start | bytes 1572872 | tf_op jit(solution)/shard_map/ppermute | solution.py:34
  124.2 1.8 %turn.3 = (bf16[512,1024]{1,0:T(8,128)(2,1)S(1)}, bf16[512,1024]{1,0:T(8,128)(2,1)S(1)}) custom-call(bf16[1024,256]{1,0:T(8,128)(2,1)S(1)} %core_sum.5.refs_0_.refs_1_, bf16[256,1024]{1,0:T(8,128)(2,1)S(1)} %copy-done.17, bf16[256,1024]{1,0:T(8,128)(2,1)} %collective-permute-done.11.refs_1_.refs_3_.refs_2_, ...), custom_call_target="tpu_custom_call" | custom-call | flops 99999997952 | bytes 2097152 | tf_op jit(solution)/shard_map/turn/pallas_call | solution.py:56
  126.1 10.4 %collective-permute-done.19.refs_2_ = bf16[1024,256]{1,0:T(8,128)(2,1)S(1)} collective-permute-done((bf16[1024,256]{1,0:T(8,128)(2,1)S(1)}, bf16[1024,256]{1,0:T(8,128)(2,1)S(1)}, u32[]{:S(2)}, u32[]{:S(2)}) %collective-permute-start.19) | collective-permute-done | bytes 524320 | tf_op jit(solution)/shard_map/ppermute | solution.py:34
  136.5 0.1 residual.3.refs_2_.refs_3_
  136.7 1.9 %collective-permute-done.20.refs_3_.refs_4_ = bf16[1024,256]{1,0:T(8,128)(2,1)S(1)} collective-permute-done((bf16[1024,256]{1,0:T(8,128)(2,1)S(1)}, bf16[1024,256]{1,0:T(8,128)(2,1)S(1)}, u32[]{:S(2)}, u32[]{:S(2)}) %collective-permute-start.20) | collective-permute-done | bytes 524320 | tf_op jit(solution)/shard_map/ppermute | solution.py:34
  138.6 1.6 grads.6
  140.2 2.0 %collective-permute-start.21 = (bf16[512,256]{1,0:T(8,128)(2,1)}, bf16[512,256]{1,0:T(8,128)(2,1)}, u32[]{:S(2)}, u32[]{:S(2)}) collective-permute-start(bf16[512,256]{1,0:T(8,128)(2,1)} %get-tuple-element.53.refs_0_), channel_id=1, source_target_pairs={{0,6},{1,7},{2,4},{3,5},{4,2},{5,3},{6,0},{7,1},{8,14},{9,15},{10,... | collective-permute-start | bytes 786440 | tf_op jit(solution)/shard_map/ppermute | solution.py:34
  142.2 0.8 grads.7.refs_0_
  143.1 0.4 copy-done.4
  143.5 0.3 copy-done.6
  143.8 1.2 outer.1
  145.0 15.9 %collective-permute-done.22.refs_1_ = bf16[512,256]{1,0:T(8,128)(2,1)} collective-permute-done((bf16[512,256]{1,0:T(8,128)(2,1)}, bf16[512,256]{1,0:T(8,128)(2,1)}, u32[]{:S(2)}, u32[]{:S(2)}) %collective-permute-start.22) | collective-permute-done | bytes 262176 | tf_op jit(solution)/shard_map/ppermute | solution.py:34
  160.9 2.2 %update.2.refs_5_ = bf16[1,512,512]{2,1,0:T(8,128)(2,1)} custom-call(f32[512,512]{1,0:T(8,128)S(1)} %grads.7.refs_0_, bf16[512,256]{1,0:T(8,128)(2,1)} %collective-permute-done.22.refs_1_, bf16[512,256]{1,0:T(8,128)(2,1)S(1)} %get-tuple-element.44.refs_0_.refs_7_.refs_2_, f32[512,256]{1,0:T(8,128)S(1)} %get-tuple-element.58.refs_3_, ...), custom_call_target="tpu_custom_call" | custom-call | flops 99999997952 | bytes 2621440 | tf_op jit(solution)/shard_map/update/pallas_call | solution.py:56
  163.1 2.6 %collective-permute-done.21.refs_1_ = bf16[512,256]{1,0:T(8,128)(2,1)} collective-permute-done((bf16[512,256]{1,0:T(8,128)(2,1)}, bf16[512,256]{1,0:T(8,128)(2,1)}, u32[]{:S(2)}, u32[]{:S(2)}) %collective-permute-start.21) | collective-permute-done | bytes 262176 | tf_op jit(solution)/shard_map/ppermute | solution.py:34
  165.7 2.1 %update.3 = bf16[1,512,512]{2,1,0:T(8,128)(2,1)} custom-call(f32[512,512]{1,0:T(8,128)S(1)} %grads.7.refs_0_, bf16[512,256]{1,0:T(8,128)(2,1)} %collective-permute-done.21.refs_1_, bf16[512,256]{1,0:T(8,128)(2,1)S(1)} %copy-done.13, f32[512,256]{1,0:T(8,128)S(1)} %get-tuple-element.55.refs_3_, ...), custom_call_target="tpu_custom_call", output_to_operand_aliasing={{}: (5, {})} | custom-call | flops 99999997952 | bytes 3145728 | tf_op jit(solution)/shard_map/update/pallas_call | solution.py:56
  (52 shorter events, 0.8 us)
Async XLA Ops:
  0.6 7.9 %copy-start = (f32[1,512,512]{2,1,0:T(8,128)S(1)}, f32[1,512,512]{2,1,0:T(8,128)}, u32[]{:S(2)}) copy-start(f32[1,512,512]{2,1,0:T(8,128)} %refs_1_.3) | copy-start | bytes 3145732
  3.6 4.9 %collective-permute-start = (bf16[256,1024]{1,0:T(8,128)(2,1)}, bf16[256,1024]{1,0:T(8,128)(2,1)S(1)}, u32[]{:S(2)}, u32[]{:S(2)}) collective-permute-start(bf16[256,1024]{1,0:T(8,128)(2,1)} %get-tuple-element.31), channel_id=1, source_target_pairs={{0,1},{1,0},{2,3},{3,2},{4,5},{5,4},{6,7},{7,6},{8,9},{9,8},{10,11... | collective-permute-start | bytes 1572872 | tf_op jit(solution)/shard_map/ppermute | solution.py:34
  3.7 30.7 %collective-permute-start.1 = (bf16[1,512,512]{2,1,0:T(8,128)(2,1)}, bf16[1,512,512]{2,1,0:T(8,128)(2,1)}, u32[]{:S(2)}, u32[]{:S(2)}) collective-permute-start(bf16[1,512,512]{2,1,0:T(8,128)(2,1)} %refs_5_.7), channel_id=1, source_target_pairs={{0,6},{1,7},{2,4},{3,5},{4,2},{5,3},{6,0},{7,1},{8,14},{9,15},{10,... | collective-permute-start | bytes 1572872 | tf_op jit(solution)/shard_map/ppermute | solution.py:34
  5.7 31.1 %collective-permute-start.3 = (bf16[256,1024]{1,0:T(8,128)(2,1)}, bf16[256,1024]{1,0:T(8,128)(2,1)}, u32[]{:S(2)}, u32[]{:S(2)}) collective-permute-start(bf16[256,1024]{1,0:T(8,128)(2,1)} %get-tuple-element.35), channel_id=1, source_target_pairs={{0,2},{1,3},{2,0},{3,1},{4,6},{5,7},{6,4},{7,5},{8,10},{9,11},{10,... | collective-permute-start | bytes 1572872 | tf_op jit(solution)/shard_map/ppermute | solution.py:34
  8.6 34.6 %collective-permute-start.4 = (bf16[256,1024]{1,0:T(8,128)(2,1)}, bf16[256,1024]{1,0:T(8,128)(2,1)}, u32[]{:S(2)}, u32[]{:S(2)}) collective-permute-start(bf16[256,1024]{1,0:T(8,128)(2,1)} %get-tuple-element.36), channel_id=1, source_target_pairs={{0,3},{1,2},{2,1},{3,0},{4,7},{5,6},{6,5},{7,4},{8,11},{9,10},{10,... | collective-permute-start | bytes 1572872 | tf_op jit(solution)/shard_map/ppermute | solution.py:34
  9.4 0.8 copy-start.9
  10.2 18.0 %all-to-all-start = ((bf16[16,32,512]{2,1,0:T(8,128)(2,1)}), bf16[16,32,512]{2,1,0:T(8,128)(2,1)S(1)}, u32[]{:S(2)}, u32[]{:S(2)}) async-start(bf16[16,32,512]{2,1,0:T(8,128)(2,1)} %cast.1.refs_0_), calls=%async_computation | async-start | bytes 1048576 | tf_op jit(solution)/shard_map/all_to_all | solution.py:323
  19.6 14.9 %copy-start.7 = (bf16[2,1,256,512]{3,2,1,0:T(8,128)(2,1)S(1)}, bf16[2,1,256,512]{3,2,1,0:T(8,128)(2,1)}, u32[]{:S(2)}) copy-start(bf16[2,1,256,512]{3,2,1,0:T(8,128)(2,1)} %refs_6_.5) | copy-start | bytes 1572868
  19.6 14.9 %copy-start.10 = (bf16[256,1024]{1,0:T(8,128)(2,1)S(1)}, bf16[256,1024]{1,0:T(8,128)(2,1)}, u32[]{:S(2)}) copy-start(bf16[256,1024]{1,0:T(8,128)(2,1)} %copy-done.9) | copy-start | bytes 1572868
  28.2 1.0 copy-start.16
  29.2 5.3 %copy-start.18 = (bf16[256,1024]{1,0:T(8,128)(2,1)S(1)}, bf16[256,1024]{1,0:T(8,128)(2,1)}, u32[]{:S(2)}) copy-start(bf16[256,1024]{1,0:T(8,128)(2,1)} %get-tuple-element.32.refs_2_.refs_3_) | copy-start | bytes 1572868
  29.9 18.9 %collective-permute-start.6 = (bf16[32,512]{1,0:T(8,128)(2,1)}, bf16[32,512]{1,0:T(8,128)(2,1)}, u32[]{:S(2)}, u32[]{:S(2)}) collective-permute-start(bf16[32,512]{1,0:T(8,128)(2,1)} %sum.1.refs_0_.refs_1_), channel_id=1, source_target_pairs={{0,32},{8,40},{16,48},{24,56},{32,0},{40,8},{48,16},{56,24},{64,96... | collective-permute-start | bytes 98312 | tf_op jit(solution)/shard_map/ppermute | solution.py:34
  36.7 9.7 %collective-permute-start.2 = (bf16[512,256]{1,0:T(8,128)(2,1)S(1)}, bf16[512,256]{1,0:T(8,128)(2,1)S(1)}, u32[]{:S(2)}, u32[]{:S(2)}) collective-permute-start(bf16[512,256]{1,0:T(8,128)(2,1)S(1)} %get-tuple-element.34), channel_id=1, source_target_pairs={{0,1},{1,0},{2,3},{3,2},{4,5},{5,4},{6,7},{7,6},{8,9},{9,8},{10,11... | collective-permute-start | bytes 786440 | tf_op jit(solution)/shard_map/ppermute | solution.py:34
  45.6 1.9 %collective-permute-start.5 = (bf16[512,256]{1,0:T(8,128)(2,1)S(1)}, bf16[512,256]{1,0:T(8,128)(2,1)S(1)}, u32[]{:S(2)}, u32[]{:S(2)}) collective-permute-start(bf16[512,256]{1,0:T(8,128)(2,1)S(1)} %get-tuple-element.38), channel_id=1, source_target_pairs={{0,1},{1,0},{2,3},{3,2},{4,5},{5,4},{6,7},{7,6},{8,9},{9,8},{10,11... | collective-permute-start | bytes 786440 | tf_op jit(solution)/shard_map/ppermute | solution.py:34
  46.5 9.3 %collective-permute-start.7 = (bf16[512,256]{1,0:T(8,128)(2,1)S(1)}, bf16[512,256]{1,0:T(8,128)(2,1)S(1)}, u32[]{:S(2)}, u32[]{:S(2)}) collective-permute-start(bf16[512,256]{1,0:T(8,128)(2,1)S(1)} %core_sum.3.refs_0_.refs_1_), channel_id=1, source_target_pairs={{0,2},{1,3},{2,0},{3,1},{4,6},{5,7},{6,4},{7,5},{8,10},{9,11},{10,... | collective-permute-start | bytes 786440 | tf_op jit(solution)/shard_map/ppermute | solution.py:34
  47.5 8.2 %copy-start.19 = (bf16[256,1024]{1,0:T(8,128)(2,1)S(1)}, bf16[256,1024]{1,0:T(8,128)(2,1)}, u32[]{:S(2)}) copy-start(bf16[256,1024]{1,0:T(8,128)(2,1)} %get-tuple-element.32.refs_2_.refs_3_) | copy-start | bytes 1572868
  47.6 12.8 %collective-permute-start.8 = (bf16[512,256]{1,0:T(8,128)(2,1)S(1)}, bf16[512,256]{1,0:T(8,128)(2,1)S(1)}, u32[]{:S(2)}, u32[]{:S(2)}) collective-permute-start(bf16[512,256]{1,0:T(8,128)(2,1)S(1)} %core_sum.4.refs_0_.refs_2_), channel_id=1, source_target_pairs={{0,2},{1,3},{2,0},{3,1},{4,6},{5,7},{6,4},{7,5},{8,10},{9,11},{10,... | collective-permute-start | bytes 786440 | tf_op jit(solution)/shard_map/ppermute | solution.py:34
  60.5 2.0 %collective-permute-start.9 = (bf16[1024,256]{1,0:T(8,128)(2,1)S(1)}, bf16[1024,256]{1,0:T(8,128)(2,1)S(1)}, u32[]{:S(2)}, u32[]{:S(2)}) collective-permute-start(bf16[1024,256]{1,0:T(8,128)(2,1)S(1)} %residual.2.refs_2_.refs_3_), channel_id=1, source_target_pairs={{0,1},{1,0},{2,3},{3,2},{4,5},{5,4},{6,7},{7,6},{8,9},{9,8},{10,11... | collective-permute-start | bytes 1572872 | tf_op jit(solution)/shard_map/ppermute | solution.py:34
  64.2 20.7 %collective-permute-start.10 = (bf16[512,256]{1,0:T(8,128)(2,1)}, bf16[512,256]{1,0:T(8,128)(2,1)}, u32[]{:S(2)}, u32[]{:S(2)}) collective-permute-start(bf16[512,256]{1,0:T(8,128)(2,1)} %get-tuple-element.43), channel_id=1, source_target_pairs={{0,6},{1,7},{2,4},{3,5},{4,2},{5,3},{6,0},{7,1},{8,14},{9,15},{10,... | collective-permute-start | bytes 786440 | tf_op jit(solution)/shard_map/ppermute | solution.py:34
  64.2 29.7 %collective-permute-start.13 = (bf16[512,256]{1,0:T(8,128)(2,1)}, bf16[512,256]{1,0:T(8,128)(2,1)}, u32[]{:S(2)}, u32[]{:S(2)}) collective-permute-start(bf16[512,256]{1,0:T(8,128)(2,1)} %get-tuple-element.40.refs_0_), channel_id=1, source_target_pairs={{0,6},{1,7},{2,4},{3,5},{4,2},{5,3},{6,0},{7,1},{8,14},{9,15},{10,... | collective-permute-start | bytes 786440 | tf_op jit(solution)/shard_map/ppermute | solution.py:34
  68.7 1.0 copy-start.14
  69.6 17.4 %all-to-all-start.1 = ((bf16[16,32,512]{2,1,0:T(8,128)(2,1)}), bf16[16,32,512]{2,1,0:T(8,128)(2,1)S(1)}, u32[]{:S(2)}, u32[]{:S(2)}) async-start(bf16[16,32,512]{2,1,0:T(8,128)(2,1)} %mean.1.refs_0_), calls=%async_computation.1 | async-start | bytes 1048576 | tf_op jit(solution)/shard_map/all_to_all | solution.py:346
  77.1 9.9 %copy-start.1 = (f32[1,512,512]{2,1,0:T(8,128)S(1)}, f32[1,512,512]{2,1,0:T(8,128)}, u32[]{:S(2)}) copy-start(f32[1,512,512]{2,1,0:T(8,128)} %refs_6_.3) | copy-start | bytes 3145732
  77.1 9.9 %copy-start.2 = (f32[1,512,512]{2,1,0:T(8,128)S(1)}, f32[1,512,512]{2,1,0:T(8,128)}, u32[]{:S(2)}) copy-start(f32[1,512,512]{2,1,0:T(8,128)} %refs_7_.7) | copy-start | bytes 3145732
  79.9 15.7 %collective-permute-start.12 = (bf16[256,1024]{1,0:T(8,128)(2,1)}, bf16[256,1024]{1,0:T(8,128)(2,1)S(1)}, u32[]{:S(2)}, u32[]{:S(2)}) collective-permute-start(bf16[256,1024]{1,0:T(8,128)(2,1)} %get-tuple-element.45), channel_id=1, source_target_pairs={{0,2},{1,3},{2,0},{3,1},{4,6},{5,7},{6,4},{7,5},{8,10},{9,11},{10,... | collective-permute-start | bytes 1572872 | tf_op jit(solution)/shard_map/ppermute | solution.py:34
  82.6 33.2 %collective-permute-start.14 = (bf16[256,1024]{1,0:T(8,128)(2,1)}, bf16[256,1024]{1,0:T(8,128)(2,1)}, u32[]{:S(2)}, u32[]{:S(2)}) collective-permute-start(bf16[256,1024]{1,0:T(8,128)(2,1)} %get-tuple-element.47), channel_id=1, source_target_pairs={{0,3},{1,2},{2,1},{3,0},{4,7},{5,6},{6,5},{7,4},{8,11},{9,10},{10,... | collective-permute-start | bytes 1572872 | tf_op jit(solution)/shard_map/ppermute | solution.py:34
  82.6 13.1 %collective-permute-start.11 = (bf16[256,1024]{1,0:T(8,128)(2,1)}, bf16[256,1024]{1,0:T(8,128)(2,1)}, u32[]{:S(2)}, u32[]{:S(2)}) collective-permute-start(bf16[256,1024]{1,0:T(8,128)(2,1)} %get-tuple-element.42.refs_0_), channel_id=1, source_target_pairs={{0,1},{1,0},{2,3},{3,2},{4,5},{5,4},{6,7},{7,6},{8,9},{9,8},{10,11... | collective-permute-start | bytes 1572872 | tf_op jit(solution)/shard_map/ppermute | solution.py:34
  87.0 1.2 copy-start.3
  88.3 1.2 copy-start.5
  89.5 1.0 copy-start.11
  90.5 1.2 copy-start.15
  93.4 22.3 %copy-start.8 = (bf16[2,1,256,512]{3,2,1,0:T(8,128)(2,1)S(1)}, bf16[2,1,256,512]{3,2,1,0:T(8,128)(2,1)}, u32[]{:S(2)}) copy-start(bf16[2,1,256,512]{3,2,1,0:T(8,128)(2,1)} %refs_6_.5) | copy-start | bytes 1572868
  93.4 22.3 %copy-start.17 = (bf16[256,1024]{1,0:T(8,128)(2,1)S(1)}, bf16[256,1024]{1,0:T(8,128)(2,1)}, u32[]{:S(2)}) copy-start(bf16[256,1024]{1,0:T(8,128)(2,1)} %prepare.4.refs_0_.refs_2_.refs_1_) | copy-start | bytes 1572868
  93.4 22.3 %collective-permute-start.15 = (bf16[512,256]{1,0:T(8,128)(2,1)S(1)}, bf16[512,256]{1,0:T(8,128)(2,1)S(1)}, u32[]{:S(2)}, u32[]{:S(2)}) collective-permute-start(bf16[512,256]{1,0:T(8,128)(2,1)S(1)} %get-tuple-element.44.refs_0_.refs_7_.refs_2_), channel_id=1, source_target_pairs={{0,6},{1,7},{2,4},{3,5},{4,2},{5,3},{6,0},{7,1},{8,14},{9,15},{10,... | collective-permute-start | bytes 786440 | tf_op jit(solution)/shard_map/ppermute | solution.py:34
  97.3 20.7 %copy-start.12 = (bf16[512,256]{1,0:T(8,128)(2,1)}, bf16[512,256]{1,0:T(8,128)(2,1)S(1)}, u32[]{:S(2)}) copy-start(bf16[512,256]{1,0:T(8,128)(2,1)S(1)} %get-tuple-element.46.refs_0_.refs_7_.refs_2_) | copy-start | bytes 786436
  97.3 20.7 %collective-permute-start.17 = (bf16[512,256]{1,0:T(8,128)(2,1)S(1)}, bf16[512,256]{1,0:T(8,128)(2,1)S(1)}, u32[]{:S(2)}, u32[]{:S(2)}) collective-permute-start(bf16[512,256]{1,0:T(8,128)(2,1)S(1)} %get-tuple-element.46.refs_0_.refs_7_.refs_2_), channel_id=1, source_target_pairs={{0,6},{1,7},{2,4},{3,5},{4,2},{5,3},{6,0},{7,1},{8,14},{9,15},{10,... | collective-permute-start | bytes 786440 | tf_op jit(solution)/shard_map/ppermute | solution.py:34
  117.9 2.8 %collective-permute-start.16 = (bf16[1024,128]{1,0:T(8,128)(2,1)S(1)}, bf16[1024,128]{1,0:T(8,128)(2,1)S(1)}, u32[]{:S(2)}, u32[]{:S(2)}) collective-permute-start(bf16[1024,128]{1,0:T(8,128)(2,1)S(1)} %get-tuple-element.49), channel_id=1, source_target_pairs={{0,1},{1,0},{2,3},{3,2},{4,5},{5,4},{6,7},{7,6},{8,9},{9,8},{10,11... | collective-permute-start | bytes 786440 | tf_op jit(solution)/shard_map/ppermute | solution.py:34
  120.1 1.7 %collective-permute-start.18 = (bf16[1024,128]{1,0:T(8,128)(2,1)S(1)}, bf16[1024,128]{1,0:T(8,128)(2,1)S(1)}, u32[]{:S(2)}, u32[]{:S(2)}) collective-permute-start(bf16[1024,128]{1,0:T(8,128)(2,1)S(1)} %get-tuple-element.51), channel_id=1, source_target_pairs={{0,1},{1,0},{2,3},{3,2},{4,5},{5,4},{6,7},{7,6},{8,9},{9,8},{10,11... | collective-permute-start | bytes 786440 | tf_op jit(solution)/shard_map/ppermute | solution.py:34
  122.0 14.5 %collective-permute-start.19 = (bf16[1024,256]{1,0:T(8,128)(2,1)S(1)}, bf16[1024,256]{1,0:T(8,128)(2,1)S(1)}, u32[]{:S(2)}, u32[]{:S(2)}) collective-permute-start(bf16[1024,256]{1,0:T(8,128)(2,1)S(1)} %core_sum.5.refs_0_.refs_1_), channel_id=1, source_target_pairs={{0,2},{1,3},{2,0},{3,1},{4,6},{5,7},{6,4},{7,5},{8,10},{9,11},{10,... | collective-permute-start | bytes 1572872 | tf_op jit(solution)/shard_map/ppermute | solution.py:34
  136.6 2.0 %collective-permute-start.20 = (bf16[1024,256]{1,0:T(8,128)(2,1)S(1)}, bf16[1024,256]{1,0:T(8,128)(2,1)S(1)}, u32[]{:S(2)}, u32[]{:S(2)}) collective-permute-start(bf16[1024,256]{1,0:T(8,128)(2,1)S(1)} %residual.3.refs_2_.refs_3_), channel_id=1, source_target_pairs={{0,1},{1,0},{2,3},{3,2},{4,5},{5,4},{6,7},{7,6},{8,9},{9,8},{10,11... | collective-permute-start | bytes 1572872 | tf_op jit(solution)/shard_map/ppermute | solution.py:34
  140.2 20.7 %collective-permute-start.22 = (bf16[512,256]{1,0:T(8,128)(2,1)}, bf16[512,256]{1,0:T(8,128)(2,1)}, u32[]{:S(2)}, u32[]{:S(2)}) collective-permute-start(bf16[512,256]{1,0:T(8,128)(2,1)} %get-tuple-element.57), channel_id=1, source_target_pairs={{0,6},{1,7},{2,4},{3,5},{4,2},{5,3},{6,0},{7,1},{8,14},{9,15},{10,... | collective-permute-start | bytes 786440 | tf_op jit(solution)/shard_map/ppermute | solution.py:34
  140.2 25.5 %collective-permute-start.21 = (bf16[512,256]{1,0:T(8,128)(2,1)}, bf16[512,256]{1,0:T(8,128)(2,1)}, u32[]{:S(2)}, u32[]{:S(2)}) collective-permute-start(bf16[512,256]{1,0:T(8,128)(2,1)} %get-tuple-element.53.refs_0_), channel_id=1, source_target_pairs={{0,6},{1,7},{2,4},{3,5},{4,2},{5,3},{6,0},{7,1},{8,14},{9,15},{10,... | collective-permute-start | bytes 786440 | tf_op jit(solution)/shard_map/ppermute | solution.py:34
  142.2 1.2 copy-start.4
  142.2 1.5 copy-start.6
  160.9 4.8 %copy-start.13 = (bf16[512,256]{1,0:T(8,128)(2,1)S(1)}, bf16[512,256]{1,0:T(8,128)(2,1)}, u32[]{:S(2)}) copy-start(bf16[512,256]{1,0:T(8,128)(2,1)} %copy-done.12) | copy-start | bytes 786436
